TPU v7x, 32 devices: a whole 2x2x4 slice. The times are simulated.
32 devices in a mesh: edp: 2 (over core), ep: 16 (over z, y, x).
Axes of the slice: x: 2, y: 2, z: 4, core: 2. Of those that a mesh axis runs over, the one named last changes fastest.
Arguments:
- tokens: bfloat16 [4096, 3584], P(('edp', 'ep')), may hold values from -6 to 6
- cotangent: bfloat16 [4096, 3584], P(('edp', 'ep')), may hold values from -6 to 6
- expert_ids: int32 [4096, 8], P(('edp', 'ep')), may hold values from 0 to 383, as said below
- route_weight: float32 [4096, 8], P(('edp', 'ep')), may hold values from 0.1 to 0.7
- gate_weight: bfloat16 [16, 3584, 1024], P('ep', None, 'edp'), may hold values from -0.09375 to 0.09375
- up_weight: bfloat16 [16, 3584, 1024], P('ep', None, 'edp'), may hold values from -0.09375 to 0.09375
- down_weight: bfloat16 [16, 1024, 3584], P('ep', 'edp'), may hold values from -0.1875 to 0.1875
Outputs:
- routed_out: bfloat16 [4096, 3584], P(('edp', 'ep'))
- token_grad: bfloat16 [4096, 3584], P(('edp', 'ep'))
- grad_gate: bfloat16 [16, 3584, 1024], P('ep', None, 'edp')
- grad_up: bfloat16 [16, 3584, 1024], P('ep', None, 'edp')
- grad_down: bfloat16 [16, 1024, 3584], P('ep', 'edp')
Inputs may be any that keep to these rules, and one draw needn't show every extreme that they name: `expert_ids`: each token names 8 different experts. Among the 128 tokens of one device (rows of one aligned block of 128) every expert is named by 2 to 4 tokens, and in every draw some expert below 16 is named by exactly 4 tokens of every device.
All inputs are finite; a program needn't handle non-finite values.
Results may differ from a plain program's by a relative error of at most 0.019.
Values may be sent and summed in bfloat16 or wider, within the bound.
No kernel may reach another device: no remote copies, remote signals or barrier semaphores. Data moves between devices by JAX's collectives and lax.ppermute only.
A program may use at most 128 MiB of HBM per device.

v0:
```python
import jax
import jax.numpy as jnp
from jax import lax
from jax.sharding import PartitionSpec as P


def rounded(values):
    return lax.optimization_barrier(values.astype(jnp.bfloat16)).astype(jnp.float32)


def activations(expert_rows, w_gate, w_up):
    gate_act = jnp.dot(expert_rows, w_gate, preferred_element_type=jnp.float32)
    up_act = jnp.dot(expert_rows, w_up, preferred_element_type=jnp.float32)
    sigma_gate = jax.nn.sigmoid(gate_act)
    hidden = (gate_act * sigma_gate * up_act).astype(jnp.bfloat16)
    return (gate_act, up_act, sigma_gate, hidden)


def per_device(tokens, cotangent, expert_ids, route_weight, gate_weight, up_weight, down_weight):
    experts_here = lax.axis_size("ep")
    groups = lax.axis_size("edp")
    tok_rows, top_count = expert_ids.shape
    capacity = tok_rows // 32
    slot_count = experts_here * capacity
    contract_rows = (((0,), (0,)), ((), ()))
    contract_last = (((1,), (1,)), ((), ()))
    flat_ids = expert_ids.reshape(-1)
    member = (flat_ids[:, None] == jnp.arange(experts_here, dtype=jnp.int32)[None, :]).astype(
        jnp.int32
    )
    earlier = jnp.sum((jnp.cumsum(member, axis=0) - 1) * member, axis=1)
    slot_of = jnp.where(flat_ids < experts_here, flat_ids * capacity + earlier, -1).reshape(
        tok_rows, top_count
    )
    matches = (
        slot_of[:, :, None] == jnp.arange(slot_count, dtype=jnp.int32)[None, None, :]
    ).astype(jnp.float32)
    selector = jnp.sum(matches, axis=1).astype(jnp.bfloat16)
    slot_weight = jnp.sum(matches * route_weight[:, :, None], axis=(0, 1))
    send_tokens = lax.dot_general(
        selector, tokens, contract_rows, preferred_element_type=jnp.float32
    ).astype(jnp.bfloat16)
    picked_cotan = lax.dot_general(
        selector, cotangent, contract_rows, preferred_element_type=jnp.float32
    )
    send_cotan = (slot_weight[:, None] * picked_cotan).astype(jnp.bfloat16)
    arrived_tokens, arrived_cotan = (
        lax.all_to_all(send_tokens, "ep", split_axis=0, concat_axis=0, tiled=True),
        lax.all_to_all(send_cotan, "ep", split_axis=0, concat_axis=0, tiled=True),
    )
    w_gate = gate_weight[0]
    w_up = up_weight[0]
    w_down = down_weight[0]
    block_width = w_gate.shape[1]
    expert_rows, expert_cotan = (
        lax.all_gather(arrived_tokens, "edp", axis=0, tiled=True),
        lax.all_gather(arrived_cotan, "edp", axis=0, tiled=True),
    )
    gate_act, up_act, sigma_gate, hidden = activations(expert_rows, w_gate, w_up)
    expert_out = lax.psum_scatter(
        rounded(jnp.dot(hidden, w_down, preferred_element_type=jnp.float32)).astype(jnp.bfloat16),
        "edp",
        scatter_dimension=0,
        tiled=True,
    )
    hidden_cot = lax.dot_general(
        expert_cotan, w_down, contract_last, preferred_element_type=jnp.float32
    )
    group_terms = jnp.einsum(
        "grf,grd->gfd",
        hidden.reshape(groups, slot_count, block_width),
        expert_cotan.reshape(groups, slot_count, -1),
        preferred_element_type=jnp.float32,
    )
    grad_down = jnp.sum(rounded(group_terms), axis=0).astype(jnp.bfloat16)
    gate_cot = (hidden_cot * up_act * sigma_gate * (1.0 + gate_act * (1.0 - sigma_gate))).astype(
        jnp.bfloat16
    )
    up_cot = (hidden_cot * gate_act * sigma_gate).astype(jnp.bfloat16)
    grad_gate = lax.dot_general(
        expert_rows, gate_cot, contract_rows, preferred_element_type=jnp.float32
    ).astype(jnp.bfloat16)
    grad_up = lax.dot_general(
        expert_rows, up_cot, contract_rows, preferred_element_type=jnp.float32
    ).astype(jnp.bfloat16)
    block_sum = lax.dot_general(gate_cot, w_gate, contract_last, preferred_element_type=jnp.float32)
    block_sum = block_sum + lax.dot_general(
        up_cot, w_up, contract_last, preferred_element_type=jnp.float32
    )
    row_grad = lax.psum_scatter(
        rounded(block_sum).astype(jnp.bfloat16), "edp", scatter_dimension=0, tiled=True
    )
    out_back = lax.all_to_all(expert_out, "ep", split_axis=0, concat_axis=0, tiled=True)
    grad_back = lax.all_to_all(row_grad, "ep", split_axis=0, concat_axis=0, tiled=True)
    valid_pair = slot_of >= 0
    safe_slot = jnp.where(valid_pair, slot_of, 0)
    pair_weight = jnp.where(valid_pair, route_weight, 0.0)
    out_total = jnp.zeros((tok_rows, out_back.shape[1]), jnp.float32)
    for choice_index in range(top_count):
        chosen_rows = out_back[safe_slot[:, choice_index]].astype(jnp.float32)
        out_total = out_total + pair_weight[:, choice_index][:, None] * chosen_rows
    routed_out = out_total.astype(jnp.bfloat16)
    token_grad = jnp.dot(selector, grad_back, preferred_element_type=jnp.float32).astype(
        jnp.bfloat16
    )
    return (routed_out, token_grad, grad_gate[None], grad_up[None], grad_down[None])


def solution(mesh):
    in_specs = (
        P(("edp", "ep"), None),
        P(("edp", "ep"), None),
        P(("edp", "ep"), None),
        P(("edp", "ep"), None),
        P("ep", None, "edp"),
        P("ep", None, "edp"),
        P("ep", "edp", None),
    )
    out_specs = (
        P(("edp", "ep"), None),
        P(("edp", "ep"), None),
        P("ep", None, "edp"),
        P("ep", None, "edp"),
        P("ep", "edp", None),
    )
    return jax.shard_map(
        per_device, mesh=mesh, in_specs=in_specs, out_specs=out_specs, check_vma=False
    )
```

profile of v0, /device:TPU:0, one launch (start us, length us, event | category | flops | bytes accessed | tf_op | source)
XLA Modules:
  0.0 148.0 jit_solution(2712260783521376352)
XLA Ops:
  7.2 0.0 copy-start
  7.2 0.9 copy.46
  8.0 0.1 eq.42
  8.1 0.1 eq.38
  8.2 4.5 %reduce-window.6 = s32[16,8,128]{2,1,0:T(8,128)S(1)} reduce-window(s32[16,8,128]{2,1,0:T(8,128)S(1)} %fusion.16, s32[]{:T(128)} %constant.10.clone.1), window={size=1x1x128 pad=0_0x0_0x127_0}, to_apply=%region_0.0 | reduce-window | flops 2080768 | bytes 131076 | tf_op jit(solution)/shard_map/reduce-window
  12.8 0.1 slice.88
  12.8 0.1 copy.48
  13.0 0.1 copy.49
  13.1 0.1 add_add_fusion
  13.2 0.1 reduce_sum.42
  13.4 0.7 compare_select_fusion.1
  14.1 0.8 select_reduce_fusion
  14.9 0.3 fusion.3
  15.2 0.9 all_to_all.38
  16.1 8.3 %all-to-all-start.2 = ((bf16[16,4,3584]{2,1,0:T(4,128)(2,1)}), bf16[16,4,3584]{2,1,0:T(4,128)(2,1)S(1)}, u32[]{:S(2)}, u32[]{:S(2)}) async-start(bf16[16,4,3584]{2,1,0:T(4,128)(2,1)} %all_to_all.38), calls=%async_computation.3 | async-start | bytes 917504 | tf_op jit(solution)/shard_map/all_to_all | solution.py:49
  24.4 0.3 convolution_convert_fusion.5
  24.7 0.9 all_to_all.32
  25.6 12.7 %all-to-all-done.2 = bf16[16,4,3584]{2,1,0:T(4,128)(2,1)S(1)} async-done(((bf16[16,4,3584]{2,1,0:T(4,128)(2,1)}), bf16[16,4,3584]{2,1,0:T(4,128)(2,1)S(1)}, u32[]{:S(2)}, u32[]{:S(2)}) %all-to-all-start.2) | async-done | bytes 458784 | tf_op jit(solution)/shard_map/all_to_all | solution.py:49
  38.3 3.8 %all-to-all-start = ((bf16[16,4,3584]{2,1,0:T(4,128)(2,1)}), bf16[16,4,3584]{2,1,0:T(4,128)(2,1)S(1)}, u32[]{:S(2)}, u32[]{:S(2)}) async-start(bf16[16,4,3584]{2,1,0:T(4,128)(2,1)} %all_to_all.32), calls=%async_computation | async-start | bytes 917504 | tf_op jit(solution)/shard_map/all_to_all | solution.py:48
  42.0 0.0 reduce-scatter.3.cloned.1.call-start
  42.1 0.1 all_to_all.40
  42.2 2.5 %all_gather.7 = bf16[128,3584]{1,0:T(8,128)(2,1)S(1)} all-gather(bf16[64,3584]{1,0:T(8,128)(2,1)S(1)} %all_to_all.40), channel_id=1, replica_groups=mesh['edp'=2,'ep'=16] {'edp'}, dimensions={0}, use_global_device_ids=true | all-gather | bytes 1376256 | tf_op jit(solution)/shard_map/all_gather | solution.py:57
  44.7 10.6 %all-to-all-done = bf16[16,4,3584]{2,1,0:T(4,128)(2,1)S(1)} async-done(((bf16[16,4,3584]{2,1,0:T(4,128)(2,1)}), bf16[16,4,3584]{2,1,0:T(4,128)(2,1)S(1)}, u32[]{:S(2)}, u32[]{:S(2)}) %all-to-all-start) | async-done | bytes 458784 | tf_op jit(solution)/shard_map/all_to_all | solution.py:48
  55.3 0.1 all_to_all.34
  55.4 2.5 %all_gather.6 = bf16[128,3584]{1,0:T(8,128)(2,1)S(1)} all-gather(bf16[64,3584]{1,0:T(8,128)(2,1)S(1)} %all_to_all.34), channel_id=1, replica_groups=mesh['edp'=2,'ep'=16] {'edp'}, dimensions={0}, use_global_device_ids=true | all-gather | bytes 1376256 | tf_op jit(solution)/shard_map/all_gather | solution.py:56
  57.8 2.8 %fusion.12 = f32[128,512]{1,0:T(8,128)S(1)} fusion(bf16[128,3584]{1,0:T(8,128)(2,1)S(1)} %all_gather.6, bf16[1,3584,512]{2,1,0:T(8,128)(2,1)} %param.11), kind=kOutput, calls=%fused_computation.28 | convolution fusion | flops 469762048 | bytes 4849664 | tf_op jit(solution)/shard_map/dot_general | solution.py:12
  60.7 0.3 copy-done.1
  61.0 0.6 fusion.8
  61.6 1.4 copy-done.4
  63.0 1.3 multiply_convert_fusion
  64.4 0.0 copy-start.8
  64.4 1.6 %convolution_convert_fusion.4 = bf16[128,3584]{1,0:T(8,128)(2,1)} fusion(bf16[128,512]{1,0:T(8,128)(2,1)S(1)} %get-tuple-element.11, bf16[1,512,3584]{2,1,0:T(8,128)(2,1)S(1)} %copy-done.4), kind=kOutput, calls=%fused_computation.16 | convolution fusion | flops 470220800 | bytes 4718592 | tf_op jit(solution)/shard_map/dot_general | solution.py:61
  66.0 0.0 reduce-scatter.3.cloned.1.call-update
  66.0 0.0 reduce-scatter.5.cloned.1.call-start
  66.1 0.0 copy-start.2
  66.1 3.5 %fusion.10 = f32[128,3584]{1,0:T(8,128)S(1)} fusion(bf16[128,512]{1,0:T(8,128)(2,1)S(1)} %get-tuple-element.10, bf16[1,3584,512]{2,1,0:T(8,128)(2,1)} %param.11), kind=kOutput, calls=%fused_computation.26 | convolution fusion | flops 469762048 | bytes 5636096 | tf_op jit(solution)/shard_map/dot_general | solution.py:86
  69.6 2.3 %fusion.2 = bf16[128,3584]{1,0:T(8,128)(2,1)} fusion(f32[128,3584]{1,0:T(8,128)S(1)} %fusion.10, bf16[128,512]{1,0:T(8,128)(2,1)S(1)} %get-tuple-element.9, bf16[1,3584,512]{2,1,0:T(8,128)(2,1)S(1)} %copy-done.2), kind=kOutput, calls=%fused_computation.14 | convolution fusion | flops 470679552 | bytes 6553600 | tf_op jit(solution)/shard_map/dot_general | solution.py:87
  71.9 0.0 reduce-scatter.5.cloned.1.call-update
  71.9 0.8 reduce-scatter.3.cloned.1.call-done
  72.7 1.9 %all_to_all.35 = bf16[16,4,3584]{2,1,0:T(4,128)(2,1)} reshape(bf16[64,3584]{1,0:T(8,128)(2,1)} %reduce-scatter.3.cloned.1.call-done) | data formatting | bytes 917504 | tf_op jit(solution)/shard_map/all_to_all | solution.py:93
  74.6 6.7 %all-to-all-start.1 = ((bf16[16,4,3584]{2,1,0:T(4,128)(2,1)}), bf16[16,4,3584]{2,1,0:T(4,128)(2,1)S(1)}, u32[]{:S(2)}, u32[]{:S(2)}) async-start(bf16[16,4,3584]{2,1,0:T(4,128)(2,1)} %all_to_all.35), calls=%async_computation.2 | async-start | bytes 917504 | tf_op jit(solution)/shard_map/all_to_all | solution.py:93
  81.4 0.5 fusion.17
  81.9 3.3 %reduce-scatter.5.cloned.1.call-done = bf16[64,3584]{1,0:T(8,128)(2,1)} async-done(((bf16[128,3584]{1,0:T(8,128)(2,1)}), bf16[64,3584]{1,0:T(8,128)(2,1)}) %reduce-scatter.5.cloned.1.call-update) | async-done | bytes 458768 | tf_op jit(solution)/shard_map/reduce_scatter | solution.py:90
  85.2 1.9 %all_to_all.41 = bf16[16,4,3584]{2,1,0:T(4,128)(2,1)} reshape(bf16[64,3584]{1,0:T(8,128)(2,1)} %reduce-scatter.5.cloned.1.call-done) | data formatting | bytes 917504 | tf_op jit(solution)/shard_map/all_to_all | solution.py:94
  87.1 8.6 %all-to-all-done.1 = bf16[16,4,3584]{2,1,0:T(4,128)(2,1)S(1)} async-done(((bf16[16,4,3584]{2,1,0:T(4,128)(2,1)}), bf16[16,4,3584]{2,1,0:T(4,128)(2,1)S(1)}, u32[]{:S(2)}, u32[]{:S(2)}) %all-to-all-start.1) | async-done | bytes 458784 | tf_op jit(solution)/shard_map/all_to_all | solution.py:93
  95.7 4.4 %all-to-all-start.3 = ((bf16[16,4,3584]{2,1,0:T(4,128)(2,1)}), bf16[16,4,3584]{2,1,0:T(4,128)(2,1)}, u32[]{:S(2)}, u32[]{:S(2)}) async-start(bf16[16,4,3584]{2,1,0:T(4,128)(2,1)} %all_to_all.41), calls=%async_computation.5 | async-start | bytes 917504 | tf_op jit(solution)/shard_map/all_to_all | solution.py:94
  100.1 0.7 pad_clamp_fusion
  100.8 5.0 %convolution_convert_fusion = bf16[2,512,3584]{2,1,0:T(8,128)(2,1)} fusion(bf16[2,64,512]{2,1,0:T(8,128)(2,1)S(1)} %bitcast.90, bf16[2,64,3584]{2,1,0:T(8,128)(2,1)S(1)} %bitcast.89), kind=kOutput, calls=%fused_computation.8 | convolution fusion | flops 473432064 | bytes 8388608 | tf_op jit(solution)/shard_map/grf,grd->gfd/dot_general | solution.py:69
  105.8 7.3 %reduce_sum.45 = bf16[512,3584]{1,0:T(8,128)(2,1)} reduce(bf16[2,512,3584]{2,1,0:T(8,128)(2,1)} %convolution_convert_fusion, bf16[]{:T(256)} %constant.24.clone.1), dimensions={0}, to_apply=%region_7.8 | reduce | flops 1835008 | bytes 11010050 | tf_op jit(solution)/shard_map/reduce_sum | solution.py:75
  113.1 3.0 %fusion = bf16[1,3584,512]{2,1,0:T(8,128)(2,1)} fusion(bf16[128,3584]{1,0:T(8,128)(2,1)S(1)} %all_gather.6, bf16[128,512]{1,0:T(8,128)(2,1)S(1)} %copy-done.9), kind=kOutput, calls=%fused_computation.11 | convolution fusion | flops 471597056 | bytes 4718592 | tf_op jit(solution)/shard_map/dot_general | solution.py:80
  116.1 3.0 %fusion.1 = bf16[1,3584,512]{2,1,0:T(8,128)(2,1)} fusion(bf16[128,3584]{1,0:T(8,128)(2,1)S(1)} %all_gather.6, bf16[128,512]{1,0:T(8,128)(2,1)S(1)} %get-tuple-element.9), kind=kOutput, calls=%fused_computation.12 | convolution fusion | flops 471597056 | bytes 4718592 | tf_op jit(solution)/shard_map/dot_general | solution.py:83
  119.1 0.1 all_to_all.37
  119.2 1.1 gather_fusion
  120.3 1.1 gather_fusion.1
  121.4 2.0 %gather_fusion.2 = bf16[128,3584]{1,0:T(8,128)(2,1)} fusion(bf16[64,3584]{1,0:T(8,128)(2,1)S(1)} %all_to_all.37, s32[1024]{0:T(1024)S(1)} %get-tuple-element.33), kind=kCustom, calls=%fused_computation.2 | custom fusion | bytes 1835520 | tf_op jit(solution)/shard_map/gather | solution.py:100
  123.5 2.0 %gather_fusion.3 = bf16[128,3584]{1,0:T(8,128)(2,1)} fusion(bf16[64,3584]{1,0:T(8,128)(2,1)S(1)} %all_to_all.37, s32[1024]{0:T(1024)S(1)} %get-tuple-element.32), kind=kCustom, calls=%fused_computation.3 | custom fusion | bytes 1835520 | tf_op jit(solution)/shard_map/gather | solution.py:100
  125.5 2.1 %gather_fusion.4 = bf16[128,3584]{1,0:T(8,128)(2,1)} fusion(bf16[64,3584]{1,0:T(8,128)(2,1)S(1)} %all_to_all.37, s32[1024]{0:T(1024)S(1)} %get-tuple-element.31), kind=kCustom, calls=%fused_computation.4 | custom fusion | bytes 1835520 | tf_op jit(solution)/shard_map/gather | solution.py:100
  127.6 2.1 %gather_fusion.5 = bf16[128,3584]{1,0:T(8,128)(2,1)} fusion(bf16[64,3584]{1,0:T(8,128)(2,1)S(1)} %all_to_all.37, s32[1024]{0:T(1024)S(1)} %get-tuple-element.30), kind=kCustom, calls=%fused_computation.5 | custom fusion | bytes 1835520 | tf_op jit(solution)/shard_map/gather | solution.py:100
  129.7 2.1 %gather_fusion.6 = bf16[128,3584]{1,0:T(8,128)(2,1)} fusion(bf16[64,3584]{1,0:T(8,128)(2,1)S(1)} %all_to_all.37, s32[1024]{0:T(1024)S(1)} %get-tuple-element.29), kind=kCustom, calls=%fused_computation.6 | custom fusion | bytes 1835520 | tf_op jit(solution)/shard_map/gather | solution.py:100
  131.7 2.0 %gather_fusion.7 = bf16[128,3584]{1,0:T(8,128)(2,1)} fusion(bf16[64,3584]{1,0:T(8,128)(2,1)S(1)} %all_to_all.37, s32[1024]{0:T(1024)S(1)} %get-tuple-element.28), kind=kCustom, calls=%fused_computation.7 | custom fusion | bytes 1835520 | tf_op jit(solution)/shard_map/gather | solution.py:100
  133.8 0.0 all-to-all-done.3
  133.8 1.1 all_to_all.43
  134.9 1.3 convolution_convert_fusion.3
  136.3 4.9 %add_convert_fusion = bf16[128,3584]{1,0:T(8,128)(2,1)} fusion(bf16[128,3584]{1,0:T(8,128)(2,1)} %gather_fusion.7, bf16[128,3584]{1,0:T(8,128)(2,1)} %gather_fusion.6, bf16[128,3584]{1,0:T(8,128)(2,1)} %gather_fusion.5, bf16[128,3584]{1,0:T(8,128)(2,1)} %gather_fusion.4, bf16[128,3584]{1,0:T(8,128)(2,1)} %gather_fusion.3, ...), kind=kLoop, calls=%fused_computation.30 | loop fusion | flops 11010048 | bytes 8261632 | tf_op jit(solution)/shard_map/convert_element_type | solution.py:102
  (25 shorter events, 0.2 us)
Async XLA Ops:
  7.2 7.8 %copy-start = (bf16[128,3584]{1,0:T(8,128)(2,1)S(1)}, bf16[128,3584]{1,0:T(8,128)(2,1)}, u32[]{:S(2)}) copy-start(bf16[128,3584]{1,0:T(8,128)(2,1)} %param.8) | copy-start | bytes 2752516
  13.0 11.4 %copy-start.7 = (bf16[128,3584]{1,0:T(8,128)(2,1)S(1)}, bf16[128,3584]{1,0:T(8,128)(2,1)}, u32[]{:S(2)}) copy-start(bf16[128,3584]{1,0:T(8,128)(2,1)} %param.7) | copy-start | bytes 2752516
  16.1 22.2 %all-to-all-start.2 = ((bf16[16,4,3584]{2,1,0:T(4,128)(2,1)}), bf16[16,4,3584]{2,1,0:T(4,128)(2,1)S(1)}, u32[]{:S(2)}, u32[]{:S(2)}) async-start(bf16[16,4,3584]{2,1,0:T(4,128)(2,1)} %all_to_all.38), calls=%async_computation.3 | async-start | bytes 917504 | tf_op jit(solution)/shard_map/all_to_all | solution.py:49
  38.3 17.0 %all-to-all-start = ((bf16[16,4,3584]{2,1,0:T(4,128)(2,1)}), bf16[16,4,3584]{2,1,0:T(4,128)(2,1)S(1)}, u32[]{:S(2)}, u32[]{:S(2)}) async-start(bf16[16,4,3584]{2,1,0:T(4,128)(2,1)} %all_to_all.32), calls=%async_computation | async-start | bytes 917504 | tf_op jit(solution)/shard_map/all_to_all | solution.py:48
  42.0 30.7 %reduce-scatter.3.cloned.1.call-start = ((), (), s32[]{:S(2)}) async-start(), calls=%async_computation.6 | async-start | bytes 1376256 | tf_op jit(solution)/shard_map/reduce_scatter | solution.py:60
  57.8 3.1 %copy-start.1 = (bf16[1,3584,512]{2,1,0:T(8,128)(2,1)S(1)}, bf16[1,3584,512]{2,1,0:T(8,128)(2,1)}, u32[]{:S(2)}) copy-start(bf16[1,3584,512]{2,1,0:T(8,128)(2,1)} %param.12) | copy-start | bytes 11010052
  61.0 2.0 %copy-start.4 = (bf16[1,512,3584]{2,1,0:T(8,128)(2,1)S(1)}, bf16[1,512,3584]{2,1,0:T(8,128)(2,1)}, u32[]{:S(2)}) copy-start(bf16[1,512,3584]{2,1,0:T(8,128)(2,1)} %param.13) | copy-start | bytes 11010052
  64.4 1.7 %copy-start.8 = (bf16[128,512]{1,0:T(8,128)(2,1)}, bf16[128,512]{1,0:T(8,128)(2,1)S(1)}, u32[]{:S(2)}) copy-start(bf16[128,512]{1,0:T(8,128)(2,1)S(1)} %get-tuple-element.10) | copy-start | bytes 393220
  66.0 19.2 %reduce-scatter.5.cloned.1.call-start = ((), (), s32[]{:S(2)}) async-start(), calls=%async_computation.7 | async-start | bytes 1376256 | tf_op jit(solution)/shard_map/reduce_scatter | solution.py:90
  66.1 3.5 %copy-start.2 = (bf16[1,3584,512]{2,1,0:T(8,128)(2,1)S(1)}, bf16[1,3584,512]{2,1,0:T(8,128)(2,1)}, u32[]{:S(2)}) copy-start(bf16[1,3584,512]{2,1,0:T(8,128)(2,1)} %param.12) | copy-start | bytes 11010052
  74.6 21.1 %all-to-all-start.1 = ((bf16[16,4,3584]{2,1,0:T(4,128)(2,1)}), bf16[16,4,3584]{2,1,0:T(4,128)(2,1)S(1)}, u32[]{:S(2)}, u32[]{:S(2)}) async-start(bf16[16,4,3584]{2,1,0:T(4,128)(2,1)} %all_to_all.35), calls=%async_computation.2 | async-start | bytes 917504 | tf_op jit(solution)/shard_map/all_to_all | solution.py:93
  95.7 10.1 %copy-start.5 = (bf16[16,4,3584]{2,1,0:T(4,128)(2,1)}, bf16[16,4,3584]{2,1,0:T(4,128)(2,1)S(1)}, u32[]{:S(2)}) copy-start(bf16[16,4,3584]{2,1,0:T(4,128)(2,1)S(1)} %all-to-all-done.1) | copy-start | bytes 1376260
  95.7 38.1 %all-to-all-start.3 = ((bf16[16,4,3584]{2,1,0:T(4,128)(2,1)}), bf16[16,4,3584]{2,1,0:T(4,128)(2,1)}, u32[]{:S(2)}, u32[]{:S(2)}) async-start(bf16[16,4,3584]{2,1,0:T(4,128)(2,1)} %all_to_all.41), calls=%async_computation.5 | async-start | bytes 917504 | tf_op jit(solution)/shard_map/all_to_all | solution.py:94
  105.8 7.3 %copy-start.9 = (bf16[128,512]{1,0:T(8,128)(2,1)S(1)}, bf16[128,512]{1,0:T(8,128)(2,1)}, u32[]{:S(2)}) copy-start(bf16[128,512]{1,0:T(8,128)(2,1)} %copy-done.8) | copy-start | bytes 393220
  116.1 3.0 %copy-start.6 = (bf16[16,4,3584]{2,1,0:T(4,128)(2,1)S(1)}, bf16[16,4,3584]{2,1,0:T(4,128)(2,1)}, u32[]{:S(2)}) copy-start(bf16[16,4,3584]{2,1,0:T(4,128)(2,1)} %copy-done.5) | copy-start | bytes 1376260
  134.9 1.4 copy-start.3
Sparse Core Ops, SparseCore 0:
  66.1 6.5 reduce-scatter.2
  75.6 9.5 reduce-scatter.4
where the time goes:
time: 149 us; the launch traced here: 148 us
  waiting for transfers between devices  36 us (24%)
  matrix products  25.1 us (17%)
  local copies, waits for them, and re-layouts  24.8 us (17%)
  starting transfers between devices  23.3 us (16%)
  other arithmetic  19.7 us (13%)
  between operations  14.3 us (10%)
  blocking collectives  4.93 us (3%)
    gather x8, local copies, waits for them, and re-layouts, per_device(): chosen_rows = out_back[safe_slot[:, choice_index]].astype(jnp.float32)  14.6 us
    all_to_all x1, waiting for transfers between devices, per_device(): lax.all_to_all(send_cotan, 'ep', split_axis=0, concat_axis=0, tiled=True)  12.7 us
    all_to_all x1, waiting for transfers between devices, per_device(): lax.all_to_all(send_tokens, 'ep', split_axis=0, concat_axis=0, tiled=True)  10.6 us
    all_to_all x1, waiting for transfers between devices, per_device(): lax.all_to_all(expert_out, 'ep', split_axis=0, concat_axis=0, tiled=True)  8.61 us
    all_to_all x1, starting transfers between devices, per_device(): lax.all_to_all(send_cotan, 'ep', split_axis=0, concat_axis=0, tiled=True)  8.31 us
    reduce_sum x1, other arithmetic, per_device(): grad_down = jnp.sum(rounded(group_terms), axis=0).astype(jnp.bfloat16)  7.27 us
    all_to_all x1, starting transfers between devices, per_device(): lax.all_to_all(expert_out, 'ep', split_axis=0, concat_axis=0, tiled=True)  6.72 us
    dot_general x1, matrix products, per_device(): jnp.einsum('grf,grd->gfd', hidden.reshape(groups, slot_count, block_width...  5.05 us
  transfers between devices with their start and end apart: 6, of which 5 were waited for; matrix products, arithmetic and copies ran while one was open for 27% of the time, Pallas kernels for 0%

commit v1 on v0

v1 whole, which is shorter than its diff:
```python
import jax
import jax.numpy as jnp
from jax import lax
from jax.experimental import pallas as pl
from jax.experimental.pallas import tpu as pltpu
from jax.sharding import PartitionSpec as P

F32 = jnp.float32
BF16 = jnp.bfloat16
VMEM_LIMIT = 60 * 1024 * 1024
ROWS_FIRST = (((0,), (0,)), ((), ()))
ROWS_LAST = (((1,), (1,)), ((), ()))
COLS = 512


def matmul(a, b, dims=(((1,), (0,)), ((), ()))):
    return lax.dot_general(a, b, dims, preferred_element_type=F32)


def route_kernel(cap, ids_ref, weight_ref, tok_ref, cot_ref, send_ref, hi_ref, lo_ref, pick_ref, scale_ref):
    tokens, width = hi_ref.shape
    block = 2 * cap

    @pl.when(pl.program_id(0) == 0)
    def _():
        lane = lax.broadcasted_iota(jnp.int32, (tokens, width), 1)
        expert = lane // block
        place = lane % block
        member = jnp.zeros((tokens, width), F32)
        weight = jnp.zeros((tokens, width), F32)
        for k in range(ids_ref.shape[1]):
            hit = ids_ref[:, k : k + 1] == expert
            member = member + jnp.where(hit, 1.0, 0.0)
            weight = weight + jnp.where(hit, weight_ref[:, k : k + 1], 0.0)
        above = lax.broadcasted_iota(jnp.int32, (tokens, tokens), 0) > lax.broadcasted_iota(
            jnp.int32, (tokens, tokens), 1
        )
        rank = matmul(jnp.where(above, 1.0, 0.0).astype(BF16), member.astype(BF16))
        chosen = jnp.where(rank == (place % cap).astype(F32), member, 0.0)
        forward = jnp.where(place < cap, chosen, 0.0)
        backward = chosen - forward
        weighted = forward * weight
        high = weighted.astype(BF16)
        hi_ref[...] = high
        lo_ref[...] = (weighted - high.astype(F32)).astype(BF16)
        pick_ref[...] = backward.astype(BF16)
        scale = jnp.transpose(forward + backward * weight)
        scale_ref[...] = jnp.broadcast_to(jnp.sum(scale, axis=1, keepdims=True), scale_ref.shape)

    first = jnp.where(hi_ref[...] != 0, 1.0, 0.0).astype(BF16)
    rows = matmul(first, tok_ref[...], ROWS_FIRST) + matmul(pick_ref[...], cot_ref[...], ROWS_FIRST)
    send_ref[...] = (rows * scale_ref[:, :1]).astype(BF16)


def route(ids, weight, tokens, cotangent, experts, cap):
    rows, depth = tokens.shape
    width = experts * 2 * cap
    fixed = lambda shape: pl.BlockSpec(shape, lambda j: (0, 0))
    moving = lambda shape: pl.BlockSpec(shape, lambda j: (0, j))
    return pl.pallas_call(
        lambda *refs: route_kernel(cap, *refs),
        grid=(depth // COLS,),
        in_specs=[fixed(ids.shape), fixed(weight.shape), moving((rows, COLS)), moving((rows, COLS))],
        out_specs=[moving((width, COLS)), fixed((rows, width)), fixed((rows, width)), fixed((rows, width))],
        out_shape=[
            jax.ShapeDtypeStruct((width, depth), BF16),
            jax.ShapeDtypeStruct((rows, width), BF16),
            jax.ShapeDtypeStruct((rows, width), BF16),
            jax.ShapeDtypeStruct((rows, width), BF16),
        ],
        scratch_shapes=[pltpu.VMEM((width, 128), F32)],
        compiler_params=pltpu.CompilerParams(vmem_limit_bytes=VMEM_LIMIT),
        name="route",
    )(ids, weight, tokens, cotangent)


def expert_kernel(cap, mine_ref, theirs_ref, gate_ref, up_ref, down_ref, own_ref, other_ref, hid_ref, gate_cot_ref, up_cot_ref):
    half = mine_ref.shape[0]
    total = 2 * half
    depth, hidden_width = gate_ref.shape
    rows = jnp.concatenate([mine_ref[...], theirs_ref[...]], axis=0)
    gate_act = matmul(rows, gate_ref[...])
    up_act = matmul(rows, up_ref[...])
    hidden_cot = matmul(rows, down_ref[...], ROWS_LAST)
    hidden_cot = pltpu.roll(hidden_cot, total - cap, 0)
    place = lax.broadcasted_iota(jnp.int32, (total, hidden_width), 0) % (2 * cap)
    is_token = place < cap
    sigma = jax.nn.sigmoid(gate_act)
    silu = gate_act * sigma
    hidden = jnp.where(is_token, silu * up_act, 0.0)
    gate_cot = jnp.where(is_token, hidden_cot * up_act * sigma * (1.0 + gate_act * (1.0 - sigma)), 0.0)
    up_cot = jnp.where(is_token, hidden_cot * silu, 0.0)
    gate_cot_ref[...] = gate_cot.astype(BF16)
    up_cot_ref[...] = up_cot.astype(BF16)
    hid_ref[...] = pltpu.roll(hidden, cap, 0).astype(BF16)
    hidden = hidden.astype(BF16)
    gate_cot = pltpu.roll(gate_cot, cap, 0).astype(BF16)
    up_cot = pltpu.roll(up_cot, cap, 0).astype(BF16)
    for j in range(depth // COLS):
        cols = pl.ds(j * COLS, COLS)
        back = matmul(hidden, down_ref[:, cols])
        back = back + matmul(gate_cot, gate_ref[cols, :], ROWS_LAST)
        back = back + matmul(up_cot, up_ref[cols, :], ROWS_LAST)
        own_ref[:, cols] = back[:half].astype(BF16)
        other_ref[:, cols] = back[half:].astype(BF16)


def expert(mine, theirs, gate, up, down, cap):
    half, depth = mine.shape
    hidden_width = gate.shape[1]
    whole = pl.BlockSpec(memory_space=pltpu.VMEM)
    return pl.pallas_call(
        lambda *refs: expert_kernel(cap, *refs),
        in_specs=[whole] * 5,
        out_specs=[whole] * 5,
        out_shape=[jax.ShapeDtypeStruct((half, depth), BF16)] * 2
        + [jax.ShapeDtypeStruct((2 * half, hidden_width), BF16)] * 3,
        compiler_params=pltpu.CompilerParams(vmem_limit_bytes=VMEM_LIMIT),
        name="expert",
    )(mine, theirs, gate, up, down)


def grads_kernel(mine_ref, theirs_ref, hid_ref, gate_cot_ref, up_cot_ref, gate_ref, up_ref, down_ref):
    rows = jnp.concatenate([mine_ref[...], theirs_ref[...]], axis=0)
    width = gate_ref.shape[1]
    pair = jnp.concatenate([gate_cot_ref[...], up_cot_ref[...]], axis=1)
    both = matmul(rows, pair, ROWS_FIRST)
    gate_ref[...] = both[:, :width].astype(BF16)
    up_ref[...] = both[:, width:].astype(BF16)
    down_ref[...] = matmul(hid_ref[...], rows, ROWS_FIRST).astype(BF16)


def grads(mine, theirs, hidden, gate_cot, up_cot):
    half, depth = mine.shape
    width = hidden.shape[1]
    fixed = pl.BlockSpec(hidden.shape, lambda j: (0, 0))
    moving = pl.BlockSpec((half, COLS), lambda j: (0, j))
    return pl.pallas_call(
        grads_kernel,
        grid=(depth // COLS,),
        in_specs=[moving, moving, fixed, fixed, fixed],
        out_specs=[
            pl.BlockSpec((COLS, width), lambda j: (j, 0)),
            pl.BlockSpec((COLS, width), lambda j: (j, 0)),
            pl.BlockSpec((width, COLS), lambda j: (0, j)),
        ],
        out_shape=[
            jax.ShapeDtypeStruct((depth, width), BF16),
            jax.ShapeDtypeStruct((depth, width), BF16),
            jax.ShapeDtypeStruct((width, depth), BF16),
        ],
        compiler_params=pltpu.CompilerParams(vmem_limit_bytes=VMEM_LIMIT),
        name="weight_grads",
    )(mine, theirs, hidden, gate_cot, up_cot)


def combine_kernel(back_ref, hi_ref, lo_ref, pick_ref, out_ref, grad_ref):
    back = back_ref[...]
    out_ref[...] = (matmul(hi_ref[...], back) + matmul(lo_ref[...], back)).astype(BF16)
    grad_ref[...] = matmul(pick_ref[...], back).astype(BF16)


def combine(back, high, low, pick):
    width, depth = back.shape
    rows = high.shape[0]
    fixed = pl.BlockSpec((rows, width), lambda j: (0, 0))
    moving = pl.BlockSpec((rows, COLS), lambda j: (0, j))
    return pl.pallas_call(
        combine_kernel,
        grid=(depth // COLS,),
        in_specs=[pl.BlockSpec((width, COLS), lambda j: (0, j)), fixed, fixed, fixed],
        out_specs=[moving, moving],
        out_shape=[jax.ShapeDtypeStruct((rows, depth), BF16)] * 2,
        compiler_params=pltpu.CompilerParams(vmem_limit_bytes=VMEM_LIMIT),
        name="combine",
    )(back, high, low, pick)


def per_device(tokens, cotangent, expert_ids, route_weight, gate_weight, up_weight, down_weight):
    experts = lax.axis_size("ep")
    cap = tokens.shape[0] // 32
    depth = tokens.shape[1]
    swap = [(0, 1), (1, 0)]
    send, high, low, pick = route(expert_ids, route_weight, tokens, cotangent, experts, cap)

    def exchange(rows):
        blocks = rows.reshape(experts, 2 * cap, depth)
        return lax.all_to_all(blocks, "ep", split_axis=0, concat_axis=0, tiled=True).reshape(rows.shape)

    mine = exchange(send)
    theirs = lax.ppermute(mine, "edp", swap)
    own, other, hidden, gate_cot, up_cot = expert(
        mine, theirs, gate_weight[0], up_weight[0], down_weight[0], cap
    )
    arrived = lax.ppermute(other, "edp", swap)
    total = (own.astype(F32) + arrived.astype(F32)).astype(BF16)
    back = exchange(total)
    grad_gate, grad_up, grad_down = grads(mine, theirs, hidden, gate_cot, up_cot)
    routed_out, token_grad = combine(back, high, low, pick)
    return (routed_out, token_grad, grad_gate[None], grad_up[None], grad_down[None])


def solution(mesh):
    in_specs = (
        P(("edp", "ep"), None),
        P(("edp", "ep"), None),
        P(("edp", "ep"), None),
        P(("edp", "ep"), None),
        P("ep", None, "edp"),
        P("ep", None, "edp"),
        P("ep", "edp", None),
    )
    out_specs = (
        P(("edp", "ep"), None),
        P(("edp", "ep"), None),
        P("ep", None, "edp"),
        P("ep", None, "edp"),
        P("ep", "edp", None),
    )
    return jax.shard_map(
        per_device, mesh=mesh, in_specs=in_specs, out_specs=out_specs, check_vma=False
    )
```

time: 149 us -> 96.1 us (0.64)
  Pallas kernels: 0 us -> 32.8 us
  blocking collectives: 4.93 us -> 32.1 us
  matrix products: 25.1 us -> 0 us
  local copies, waits for them, and re-layouts: 24.8 us -> 4.68 us
  starting transfers between devices: 23.3 us -> 3.77 us
  other arithmetic: 19.7 us -> 2.32 us
  waiting for transfers between devices: 36 us -> 18.9 us
  between operations: 14.3 us -> 0.65 us
    pallas_call x0 -> x4, Pallas kernels: none -> 32.8 us  [the longest x1 12.3 us: expert(): pl.pallas_call(lambda *refs: expert_kernel(cap, *refs), in_specs=[whole]...]
    all_to_all x0 -> x1, blocking collectives: none -> 32.1 us  [exchange(): lax.all_to_all(blocks, 'ep', split_axis=0, concat_axis=0, tiled=True)]
    dot_general x12 -> x0, matrix products: 25.1 us -> none  [the longest x1 5.05 us: per_device(): jnp.einsum('grf,grd->gfd', hidden.reshape(groups, slot_count, block_width...]
    all_to_all x4 -> x1, starting transfers between devices: 23.2 us -> 3.64 us  [exchange(): lax.all_to_all(blocks, 'ep', split_axis=0, concat_axis=0, tiled=True)]
    all_to_all x4 -> x1, waiting for transfers between devices: 31.9 us -> 13.9 us  [exchange(): lax.all_to_all(blocks, 'ep', split_axis=0, concat_axis=0, tiled=True)]
    gather x8 -> x0, local copies, waits for them, and re-layouts: 14.6 us -> none  [per_device(): chosen_rows = out_back[safe_slot[:, choice_index]].astype(jnp.float32)]
    reduce_sum x3 -> x0, other arithmetic: 8.14 us -> none  [the longest x1 7.27 us: per_device(): grad_down = jnp.sum(rounded(group_terms), axis=0).astype(jnp.bfloat16)]
    all_to_all x8 -> x0, local copies, waits for them, and re-layouts: 6.97 us -> none  [the longest x2 3 us: per_device(): lax.all_to_all(row_grad, 'ep', split_axis=0, concat_axis=0, tiled=True)]
  transfers between devices with their start and end apart: 6 -> 3, of which waited for: 5 -> 3; matrix products, arithmetic and copies ran while one was open for 27% -> 0% of each run, Pallas kernels for 0% -> 9%
where the time goes in v1:
time: 96.1 us; the launch traced here: 95.3 us
  Pallas kernels  32.8 us (34%)
  blocking collectives  32.1 us (33%)
  waiting for transfers between devices  18.9 us (20%)
  local copies, waits for them, and re-layouts  4.68 us (5%)
  starting transfers between devices  3.77 us (4%)
  other arithmetic  2.32 us (2%)
    all_to_all x1, blocking collectives, exchange(): lax.all_to_all(blocks, 'ep', split_axis=0, concat_axis=0, tiled=True)  32.1 us
    all_to_all x1, waiting for transfers between devices, exchange(): lax.all_to_all(blocks, 'ep', split_axis=0, concat_axis=0, tiled=True)  13.9 us
    pallas_call x1, Pallas kernels, expert(): pl.pallas_call(lambda *refs: expert_kernel(cap, *refs), in_specs=[whole]...  12.3 us
    pallas_call x1, Pallas kernels, grads(): pl.pallas_call(grads_kernel, grid=(depth // COLS,), in_specs=[moving, mov...  8.47 us
    pallas_call x1, Pallas kernels, route(): pl.pallas_call(lambda *refs: route_kernel(cap, *refs), grid=(depth // COL...  6.46 us
    pallas_call x1, Pallas kernels, combine(): pl.pallas_call(combine_kernel, grid=(depth // COLS,), in_specs=[pl.BlockS...  5.55 us
    unnamed x8, local copies, waits for them, and re-layouts  4.68 us
    all_to_all x1, starting transfers between devices, exchange(): lax.all_to_all(blocks, 'ep', split_axis=0, concat_axis=0, tiled=True)  3.64 us
  transfers between devices with their start and end apart: 3, of which 3 were waited for; matrix products, arithmetic and copies ran while one was open for 0% of the time, Pallas kernels for 9%

profile of v1, /device:TPU:0, one launch (start us, length us, event | category | flops | bytes accessed | tf_op | source)
XLA Modules:
  0.0 95.3 jit_solution(2068402400918258897)
XLA Ops:
  0.6 1.4 %copy.12.refs_0_ = s32[128,8]{1,0:T(8,128)} copy(s32[128,8]{0,1:T(8,128)} %param.9) | data formatting | bytes 8192 | tf_op args[2]
  2.0 1.4 %copy.13.refs_1_ = f32[128,8]{1,0:T(8,128)} copy(f32[128,8]{0,1:T(8,128)} %param.10) | data formatting | bytes 8192 | tf_op args[3]
  3.5 6.5 %route.1 = (bf16[128,3584]{1,0:T(8,128)(2,1)}, bf16[128,128]{1,0:T(8,128)(2,1)}, bf16[128,128]{1,0:T(8,128)(2,1)}, bf16[128,128]{1,0:T(8,128)(2,1)}) custom-call(s32[128,8]{1,0:T(8,128)} %copy.12.refs_0_, f32[128,8]{1,0:T(8,128)} %copy.13.refs_1_, bf16[128,3584]{1,0:T(8,128)(2,1)} %refs_2_.1, bf16[128,3584]{1,0:T(8,128)(2,1)} %refs_3_.1), custom_call_target="tpu_custom_call" | custom-call | tf_op jit(solution)/shard_map/route/pallas_call | solution.py:60
  9.9 32.1 %all_to_all.10 = bf16[16,8,3584]{2,1,0:T(8,128)(2,1)S(1)} all-to-all(bf16[16,8,3584]{2,1,0:T(8,128)(2,1)} %bitcast.18), channel_id=1, replica_groups=mesh['edp'=2,'ep'=16] {'ep'}, dimensions={0} | all-to-all | bytes 1835008 | tf_op jit(solution)/shard_map/all_to_all | solution.py:188
  42.1 0.0 copy-start
  42.1 0.0 collective-permute-start
  42.1 2.5 %collective-permute-done.refs_1_.theirs_ref = bf16[128,3584]{1,0:T(8,128)(2,1)S(1)} collective-permute-done((bf16[128,3584]{1,0:T(8,128)(2,1)S(1)}, bf16[128,3584]{1,0:T(8,128)(2,1)S(1)}, u32[]{:S(2)}, u32[]{:S(2)}) %collective-permute-start) | collective-permute-done | bytes 917536 | tf_op jit(solution)/shard_map/ppermute | solution.py:191
  44.5 0.0 copy-start.1
  44.5 0.0 copy-done
  44.5 0.9 copy-done.1
  45.5 12.3 %expert.1 = (bf16[128,3584]{1,0:T(8,128)(2,1)}, bf16[128,3584]{1,0:T(8,128)(2,1)}, bf16[256,512]{1,0:T(8,128)(2,1)}, bf16[256,512]{1,0:T(8,128)(2,1)}, bf16[256,512]{1,0:T(8,128)(2,1)}) custom-call(bf16[128,3584]{1,0:T(8,128)(2,1)} %bitcast.12, bf16[128,3584]{1,0:T(8,128)(2,1)} %copy-done.1, bf16[3584,512]{1,0:T(8,128)(2,1)} %bitcast.15, ...), custom_call_target="tpu_custom_call" | custom-call | tf_op jit(solution)/shard_map/expert/pallas_call | solution.py:112
  57.8 0.1 collective-permute-start.1
  57.9 2.6 %collective-permute-done.1 = bf16[128,3584]{1,0:T(8,128)(2,1)S(1)} collective-permute-done((bf16[128,3584]{1,0:T(8,128)(2,1)}, bf16[128,3584]{1,0:T(8,128)(2,1)S(1)}, u32[]{:S(2)}, u32[]{:S(2)}) %collective-permute-start.1) | collective-permute-done | bytes 917536 | tf_op jit(solution)/shard_map/ppermute | solution.py:195
  60.5 2.3 %fusion = bf16[16,8,3584]{2,1,0:T(8,128)(2,1)} fusion(bf16[128,3584]{1,0:T(8,128)(2,1)S(1)} %collective-permute-done.1, bf16[128,3584]{1,0:T(8,128)(2,1)} %get-tuple-element.20), kind=kLoop, calls=%fused_computation.1 | loop fusion | flops 1835008 | bytes 2752512 | tf_op jit(solution)/shard_map/reshape | solution.py:187
  62.8 3.6 %all-to-all-start.1 = ((bf16[16,8,3584]{2,1,0:T(8,128)(2,1)}), bf16[16,8,3584]{2,1,0:T(8,128)(2,1)S(1)}, u32[]{:S(2)}, u32[]{:S(2)}) async-start(bf16[16,8,3584]{2,1,0:T(8,128)(2,1)} %fusion), calls=%async_computation.1 | async-start | bytes 1835008 | tf_op jit(solution)/shard_map/all_to_all | solution.py:188
  66.5 8.5 %weight_grads.1 = (bf16[3584,512]{1,0:T(8,128)(2,1)}, bf16[3584,512]{1,0:T(8,128)(2,1)}, bf16[512,3584]{1,0:T(8,128)(2,1)}) custom-call(bf16[128,3584]{1,0:T(8,128)(2,1)} %bitcast.13, bf16[128,3584]{1,0:T(8,128)(2,1)} %copy-done.1, bf16[256,512]{1,0:T(8,128)(2,1)} %get-tuple-element.27.hid_ref, bf16[256,512]{1,0:T(8,128)(2,1)} %get-tuple-element.28.gate_cot_ref, ...), custom_call_target="tpu_custom_call" | custom-call | tf_op jit(solution)/shard_map/weight_grads/pallas_call | solution.py:138
  74.9 13.9 %all-to-all-done.1 = bf16[16,8,3584]{2,1,0:T(8,128)(2,1)S(1)} async-done(((bf16[16,8,3584]{2,1,0:T(8,128)(2,1)}), bf16[16,8,3584]{2,1,0:T(8,128)(2,1)S(1)}, u32[]{:S(2)}, u32[]{:S(2)}) %all-to-all-start.1) | async-done | bytes 917536 | tf_op jit(solution)/shard_map/all_to_all | solution.py:188
  88.8 0.0 copy-start.2
  88.8 0.9 copy-done.2
  89.7 5.5 %combine.1 = (bf16[128,3584]{1,0:T(8,128)(2,1)}, bf16[128,3584]{1,0:T(8,128)(2,1)}) custom-call(bf16[128,3584]{1,0:T(8,128)(2,1)} %bitcast.14, bf16[128,128]{1,0:T(8,128)(2,1)} %get-tuple-element.22.hi_ref, bf16[128,128]{1,0:T(8,128)(2,1)} %get-tuple-element.23.lo_ref, bf16[128,128]{1,0:T(8,128)(2,1)} %get-tuple-element.24.pick_ref), custom_call_target="tpu_custom_call" | custom-call | tf_op jit(solution)/shard_map/combine/pallas_call | solution.py:168
Async XLA Ops:
  42.1 2.5 %copy-start = (bf16[16,8,3584]{2,1,0:T(8,128)(2,1)}, bf16[16,8,3584]{2,1,0:T(8,128)(2,1)S(1)}, u32[]{:S(2)}) copy-start(bf16[16,8,3584]{2,1,0:T(8,128)(2,1)S(1)} %all_to_all.10) | copy-start | bytes 2752516
  42.1 2.5 %collective-permute-start = (bf16[128,3584]{1,0:T(8,128)(2,1)S(1)}, bf16[128,3584]{1,0:T(8,128)(2,1)S(1)}, u32[]{:S(2)}, u32[]{:S(2)}) collective-permute-start(bf16[128,3584]{1,0:T(8,128)(2,1)S(1)} %bitcast.11), channel_id=1, source_target_pairs={{0,16},{16,0},{1,17},{17,1},{2,18},{18,2},{3,19},{19,3},{4,20},{20... | collective-permute-start | bytes 2752520 | tf_op jit(solution)/shard_map/ppermute | solution.py:191
  44.5 0.9 copy-start.1
  57.8 2.7 %collective-permute-start.1 = (bf16[128,3584]{1,0:T(8,128)(2,1)}, bf16[128,3584]{1,0:T(8,128)(2,1)S(1)}, u32[]{:S(2)}, u32[]{:S(2)}) collective-permute-start(bf16[128,3584]{1,0:T(8,128)(2,1)} %get-tuple-element.21), channel_id=1, source_target_pairs={{0,16},{16,0},{1,17},{17,1},{2,18},{18,2},{3,19},{19,3},{4,20},{20... | collective-permute-start | bytes 2752520 | tf_op jit(solution)/shard_map/ppermute | solution.py:195
  62.8 26.0 %all-to-all-start.1 = ((bf16[16,8,3584]{2,1,0:T(8,128)(2,1)}), bf16[16,8,3584]{2,1,0:T(8,128)(2,1)S(1)}, u32[]{:S(2)}, u32[]{:S(2)}) async-start(bf16[16,8,3584]{2,1,0:T(8,128)(2,1)} %fusion), calls=%async_computation.1 | async-start | bytes 1835008 | tf_op jit(solution)/shard_map/all_to_all | solution.py:188
  88.8 0.9 copy-start.2

commit v2 on v1

v2 whole, which is shorter than its diff:
```python
import jax
import jax.numpy as jnp
from jax import lax
from jax.experimental import pallas as pl
from jax.experimental.pallas import tpu as pltpu
from jax.sharding import PartitionSpec as P

F32 = jnp.float32
BF16 = jnp.bfloat16
MIB = 1024 * 1024
SCOPED = 16 * MIB
ROWS_FIRST = (((0,), (0,)), ((), ()))
ROWS_LAST = (((1,), (1,)), ((), ()))
COLS = 512


def matmul(a, b, dims=(((1,), (0,)), ((), ()))):
    return lax.dot_general(a, b, dims, preferred_element_type=F32)


WHOLE = pl.BlockSpec(memory_space=pltpu.VMEM)
REMOTE = pl.BlockSpec(memory_space=pl.ANY)


def spread(depth):
    return [pl.ds(j * COLS, COLS) for j in range(depth // COLS)]


def in_hbm(*arrays):
    return [pltpu.with_memory_space_constraint(a, pltpu.HBM) for a in arrays]


def in_vmem(*arrays):
    return [pltpu.with_memory_space_constraint(a, pltpu.VMEM) for a in arrays]


def route_kernel(
    cap, ids_hbm, weight_hbm, tok_hbm, cot_hbm, send_ref, select_hbm,
    ids_ref, weight_ref, tok_ref, cot_ref, select_ref, small_sems, sems,
):
    width, tokens = send_ref.shape[0], tok_ref.shape[0]
    block = 2 * cap
    parts = spread(tok_hbm.shape[1])
    small = [
        pltpu.make_async_copy(ids_hbm, ids_ref, small_sems.at[0]),
        pltpu.make_async_copy(weight_hbm, weight_ref, small_sems.at[1]),
    ]
    copies = [
        (
            pltpu.make_async_copy(tok_hbm.at[:, cols], tok_ref.at[:, cols], sems.at[0, j]),
            pltpu.make_async_copy(cot_hbm.at[:, cols], cot_ref.at[:, cols], sems.at[1, j]),
        )
        for j, cols in enumerate(parts)
    ]
    for copy in small:
        copy.start()
    for pair in copies:
        for copy in pair:
            copy.start()
    slot = lax.broadcasted_iota(jnp.int32, (width, tokens), 0)
    expert = slot // block
    place = slot % block
    before = lax.broadcasted_iota(jnp.int32, (tokens, tokens), 0) < lax.broadcasted_iota(
        jnp.int32, (tokens, tokens), 1
    )
    before = jnp.where(before, 1.0, 0.0).astype(BF16)
    for copy in small:
        copy.wait()
    member = jnp.zeros((width, tokens), F32)
    weight = jnp.zeros((width, tokens), F32)
    for k in range(ids_ref.shape[0]):
        hit = ids_ref[k : k + 1, :] == expert
        member = member + jnp.where(hit, 1.0, 0.0)
        weight = weight + jnp.where(hit, weight_ref[k : k + 1, :], 0.0)
    rank = matmul(member.astype(BF16), before)
    chosen = jnp.where(rank == (place % cap).astype(F32), member, 0.0)
    forward = jnp.where(place < cap, chosen, 0.0)
    backward = chosen - forward
    scale = jnp.sum(forward + backward * weight, axis=1, keepdims=True)
    first = forward.astype(BF16)
    second = backward.astype(BF16)
    for pair, cols in zip(copies, parts):
        for copy in pair:
            copy.wait()
        rows = matmul(first, tok_ref[:, cols]) + matmul(second, cot_ref[:, cols])
        send_ref[:, cols] = (rows * scale).astype(BF16)
    weighted = jnp.transpose(forward * weight)
    high = weighted.astype(BF16)
    select_ref[0] = high
    select_ref[1] = (weighted - high.astype(F32)).astype(BF16)
    select_ref[2] = jnp.transpose(backward).astype(BF16)
    copy = pltpu.make_async_copy(select_ref, select_hbm, small_sems.at[2])
    copy.start()
    copy.wait()


def route(ids, weight, tokens, cotangent, experts, cap):
    rows, depth = tokens.shape
    width = experts * 2 * cap
    return pl.pallas_call(
        lambda *refs: route_kernel(cap, *refs),
        in_specs=[REMOTE] * 4,
        out_specs=[WHOLE, REMOTE],
        out_shape=[pltpu.VMEM((width, depth), BF16), pltpu.HBM((3, rows, width), BF16)],
        scratch_shapes=[
            pltpu.VMEM(ids.shape, jnp.int32),
            pltpu.VMEM(weight.shape, F32),
            pltpu.VMEM((rows, depth), BF16),
            pltpu.VMEM((rows, depth), BF16),
            pltpu.VMEM((3, rows, width), BF16),
            pltpu.SemaphoreType.DMA((3,)),
            pltpu.SemaphoreType.DMA((2, depth // COLS)),
        ],
        compiler_params=pltpu.CompilerParams(vmem_limit_bytes=8 * MIB),
        name="route",
    )(*in_hbm(ids, weight, tokens, cotangent))


def load_kernel(after_ref, *refs):
    sems = refs[-1]
    count = (len(refs) - 1) // 2
    copies = [pltpu.make_async_copy(refs[i], refs[count + i], sems.at[i]) for i in range(count)]
    for copy in copies:
        copy.start()
    for copy in copies:
        copy.wait()


def load(after, arrays):
    return pl.pallas_call(
        load_kernel,
        in_specs=[REMOTE] * (1 + len(arrays)),
        out_specs=[WHOLE] * len(arrays),
        out_shape=[pltpu.VMEM(a.shape, a.dtype) for a in arrays],
        scratch_shapes=[pltpu.SemaphoreType.DMA((len(arrays),))],
        compiler_params=pltpu.CompilerParams(vmem_limit_bytes=2 * MIB),
        name="load_weights",
    )(after, *in_hbm(*arrays))


def back_rows(hidden, gate_cot, up_cot, gate_ref, up_ref, down_ref, own_ref, other_ref, first, count):
    half = own_ref.shape[0]
    for j in range(count):
        cols = pl.ds((first + j) * COLS, COLS)
        back = matmul(hidden, down_ref[:, cols])
        back = back + matmul(gate_cot, gate_ref[cols, :], ROWS_LAST)
        back = back + matmul(up_cot, up_ref[cols, :], ROWS_LAST)
        here = pl.ds(j * COLS, COLS)
        own_ref[:, here] = back[:half].astype(BF16)
        other_ref[:, here] = back[half:].astype(BF16)


def expert_kernel(
    cap, mine_ref, theirs_ref, gate_ref, up_hbm, down_hbm,
    own_ref, other_ref, hid_ref, gate_cot_ref, up_cot_ref, stack_ref, up_ref, down_ref, sems,
):
    half = mine_ref.shape[0]
    total = 2 * half
    depth, hidden_width = gate_ref.shape
    load_up = pltpu.make_async_copy(up_hbm, up_ref, sems.at[0])
    load_down = pltpu.make_async_copy(down_hbm, down_ref, sems.at[1])
    load_up.start()
    load_down.start()
    rows = jnp.concatenate([mine_ref[...], theirs_ref[...]], axis=0)
    gate_act = matmul(rows, gate_ref[...])
    load_up.wait()
    up_act = matmul(rows, up_ref[...])
    load_down.wait()
    hidden_cot = matmul(rows, down_ref[...], ROWS_LAST)
    hidden_cot = pltpu.roll(hidden_cot, total - cap, 0)
    place = lax.broadcasted_iota(jnp.int32, (total, hidden_width), 0) % (2 * cap)
    is_token = place < cap
    sigma = jax.nn.sigmoid(gate_act)
    silu = gate_act * sigma
    hidden = jnp.where(is_token, silu * up_act, 0.0)
    gate_cot = jnp.where(is_token, hidden_cot * up_act * sigma * (1.0 + gate_act * (1.0 - sigma)), 0.0)
    up_cot = jnp.where(is_token, hidden_cot * silu, 0.0)
    gate_cot_ref[...] = gate_cot.astype(BF16)
    up_cot_ref[...] = up_cot.astype(BF16)
    hid_ref[...] = pltpu.roll(hidden, cap, 0).astype(BF16)
    stack_ref[0] = hidden.astype(BF16)
    stack_ref[1] = pltpu.roll(gate_cot, cap, 0).astype(BF16)
    stack_ref[2] = pltpu.roll(up_cot, cap, 0).astype(BF16)
    back_rows(
        stack_ref[0], stack_ref[1], stack_ref[2], gate_ref, up_ref, down_ref, own_ref, other_ref,
        0, own_ref.shape[1] // COLS,
    )


def expert(mine, theirs, gate, up, down, cap):
    half, depth = mine.shape
    hidden_width = gate.shape[1]
    early = early_cols(depth)
    return pl.pallas_call(
        lambda *refs: expert_kernel(cap, *refs),
        in_specs=[WHOLE] * 3 + [REMOTE] * 2,
        out_specs=[WHOLE] * 8,
        out_shape=[pltpu.VMEM((half, early), BF16)] * 2
        + [pltpu.VMEM((2 * half, hidden_width), BF16)] * 3
        + [pltpu.VMEM((3, 2 * half, hidden_width), BF16), pltpu.VMEM(up.shape, BF16), pltpu.VMEM(down.shape, BF16)],
        scratch_shapes=[pltpu.SemaphoreType.DMA((2,))],
        compiler_params=pltpu.CompilerParams(vmem_limit_bytes=SCOPED),
        name="expert",
    )(*in_vmem(mine, theirs, gate), *in_hbm(up, down))


def early_cols(depth):
    return depth // COLS // 2 * COLS


def late_kernel(stack_ref, gate_ref, up_ref, down_ref, own_ref, other_ref):
    count = own_ref.shape[1] // COLS
    first = gate_ref.shape[0] // COLS - count
    back_rows(
        stack_ref[0], stack_ref[1], stack_ref[2], gate_ref, up_ref, down_ref, own_ref, other_ref, first, count
    )


def late_rows(stack, gate, up, down):
    half = stack.shape[1] // 2
    depth = gate.shape[0]
    late = depth - early_cols(depth)
    return pl.pallas_call(
        late_kernel,
        in_specs=[WHOLE] * 4,
        out_specs=[WHOLE] * 2,
        out_shape=[pltpu.VMEM((half, late), BF16)] * 2,
        compiler_params=pltpu.CompilerParams(vmem_limit_bytes=8 * MIB),
        name="late_rows",
    )(*in_vmem(stack, gate, up, down))


def add_kernel(own_early, other_early, own_late, other_late, out_hbm, out_ref, sems):
    early = own_early.shape[1]
    copies = []
    for j, cols in enumerate(spread(out_ref.shape[1])):
        if j * COLS < early:
            a, b, here = own_early, other_early, pl.ds(j * COLS, COLS)
        else:
            a, b, here = own_late, other_late, pl.ds(j * COLS - early, COLS)
        out_ref[:, cols] = (a[:, here].astype(F32) + b[:, here].astype(F32)).astype(BF16)
        copy = pltpu.make_async_copy(out_ref.at[:, cols], out_hbm.at[:, cols], sems.at[j])
        copy.start()
        copies.append(copy)
    for copy in copies:
        copy.wait()


def add_rows(own_early, other_early, own_late, other_late):
    rows = own_early.shape[0]
    depth = own_early.shape[1] + own_late.shape[1]
    return pl.pallas_call(
        add_kernel,
        in_specs=[WHOLE] * 4,
        out_specs=REMOTE,
        out_shape=pltpu.HBM((rows, depth), BF16),
        scratch_shapes=[pltpu.VMEM((rows, depth), BF16), pltpu.SemaphoreType.DMA((depth // COLS,))],
        compiler_params=pltpu.CompilerParams(vmem_limit_bytes=8 * MIB),
        name="add_rows",
    )(*in_vmem(own_early, other_early, own_late, other_late))


def grads_kernel(mine_ref, theirs_ref, hid_ref, gate_cot_ref, up_cot_ref, gate_ref, up_ref, down_ref):
    cols = pl.ds(pl.multiple_of(pl.program_id(0) * COLS, COLS), COLS)
    rows = jnp.concatenate([mine_ref[:, cols], theirs_ref[:, cols]], axis=0)
    width = gate_ref.shape[1]
    pair = jnp.concatenate([gate_cot_ref[...], up_cot_ref[...]], axis=1)
    both = matmul(rows, pair, ROWS_FIRST)
    gate_ref[...] = both[:, :width].astype(BF16)
    up_ref[...] = both[:, width:].astype(BF16)
    down_ref[...] = matmul(hid_ref[...], rows, ROWS_FIRST).astype(BF16)


def grads(mine, theirs, hidden, gate_cot, up_cot):
    half, depth = mine.shape
    width = hidden.shape[1]
    return pl.pallas_call(
        grads_kernel,
        grid=(depth // COLS,),
        in_specs=[WHOLE] * 5,
        out_specs=[
            pl.BlockSpec((COLS, width), lambda j: (j, 0)),
            pl.BlockSpec((COLS, width), lambda j: (j, 0)),
            pl.BlockSpec((width, COLS), lambda j: (0, j)),
        ],
        out_shape=[
            jax.ShapeDtypeStruct((depth, width), BF16),
            jax.ShapeDtypeStruct((depth, width), BF16),
            jax.ShapeDtypeStruct((width, depth), BF16),
        ],
        compiler_params=pltpu.CompilerParams(vmem_limit_bytes=SCOPED),
        name="weight_grads",
    )(*in_vmem(mine, theirs, hidden, gate_cot, up_cot))


def combine_kernel(back_ref, select_hbm, out_hbm, grad_hbm, select_ref, out_ref, grad_ref, select_sem, sems):
    load_select = pltpu.make_async_copy(select_hbm, select_ref, select_sem)
    load_select.start()
    load_select.wait()
    copies = []
    for j, cols in enumerate(spread(back_ref.shape[1])):
        back = back_ref[:, cols]
        out_ref[:, cols] = (matmul(select_ref[0], back) + matmul(select_ref[1], back)).astype(BF16)
        copy = pltpu.make_async_copy(out_ref.at[:, cols], out_hbm.at[:, cols], sems.at[0, j])
        copy.start()
        copies.append(copy)
        grad_ref[:, cols] = matmul(select_ref[2], back).astype(BF16)
        copy = pltpu.make_async_copy(grad_ref.at[:, cols], grad_hbm.at[:, cols], sems.at[1, j])
        copy.start()
        copies.append(copy)
    for copy in copies:
        copy.wait()


def combine(back, select):
    width, depth = back.shape
    rows = select.shape[1]
    return pl.pallas_call(
        combine_kernel,
        in_specs=[WHOLE, REMOTE],
        out_specs=[REMOTE, REMOTE],
        out_shape=[pltpu.HBM((rows, depth), BF16)] * 2,
        scratch_shapes=[
            pltpu.VMEM(select.shape, BF16),
            pltpu.VMEM((rows, depth), BF16),
            pltpu.VMEM((rows, depth), BF16),
            pltpu.SemaphoreType.DMA,
            pltpu.SemaphoreType.DMA((2, depth // COLS)),
        ],
        compiler_params=pltpu.CompilerParams(vmem_limit_bytes=8 * MIB),
        name="combine",
    )(*in_vmem(back), *in_hbm(select))


def per_device(tokens, cotangent, expert_ids, route_weight, gate_weight, up_weight, down_weight):
    experts = lax.axis_size("ep")
    cap = tokens.shape[0] // 32
    depth = tokens.shape[1]
    swap = [(0, 1), (1, 0)]
    send, select = route(expert_ids.T, route_weight.T, tokens, cotangent, experts, cap)

    def exchange(rows):
        blocks = rows.reshape(experts, 2 * cap, depth)
        return lax.all_to_all(blocks, "ep", split_axis=0, concat_axis=0, tiled=True).reshape(rows.shape)

    mine = exchange(send)
    theirs = lax.ppermute(mine, "edp", swap)
    (gate,) = load(mine, [gate_weight[0]])
    own_early, other_early, hidden, gate_cot, up_cot, stack, up, down = expert(
        mine, theirs, gate, up_weight[0], down_weight[0], cap
    )
    arrived_early = lax.ppermute(other_early, "edp", swap)
    own_late, other_late = late_rows(stack, gate, up, down)
    other_late, arrived_early = lax.optimization_barrier((other_late, arrived_early))
    arrived_late = lax.ppermute(other_late, "edp", swap)
    back = exchange(add_rows(own_early, arrived_early, own_late, arrived_late))
    grad_gate, grad_up, grad_down = grads(mine, theirs, hidden, gate_cot, up_cot)
    routed_out, token_grad = combine(back, select)
    return (routed_out, token_grad, grad_gate[None], grad_up[None], grad_down[None])


def solution(mesh):
    in_specs = (
        P(("edp", "ep"), None),
        P(("edp", "ep"), None),
        P(("edp", "ep"), None),
        P(("edp", "ep"), None),
        P("ep", None, "edp"),
        P("ep", None, "edp"),
        P("ep", "edp", None),
    )
    out_specs = (
        P(("edp", "ep"), None),
        P(("edp", "ep"), None),
        P("ep", None, "edp"),
        P("ep", None, "edp"),
        P("ep", "edp", None),
    )
    return jax.shard_map(
        per_device, mesh=mesh, in_specs=in_specs, out_specs=out_specs, check_vma=False
    )
```

time: 96.1 us -> 78.9 us (0.82)
  Pallas kernels: 32.8 us -> 23.7 us
  local copies, waits for them, and re-layouts: 4.68 us -> 0 us
  other arithmetic: 2.32 us -> 0 us
  waiting for transfers between devices: 18.9 us -> 17.9 us
    pallas_call x4 -> x7, Pallas kernels: 32.8 us -> 23.7 us  [the longest x1 6.36 us: grads(): pl.pallas_call(grads_kernel, grid=(depth // COLS,), in_specs=[WHOLE] * 5,...]
    unnamed x8 -> x0, local copies, waits for them, and re-layouts: 4.68 us -> none
    reshape x1 -> x0, other arithmetic: 2.32 us -> none  [exchange(): blocks = rows.reshape(experts, 2 * cap, depth)]
    all_to_all x1, waiting for transfers between devices: 13.9 us -> 16 us  [exchange(): lax.all_to_all(blocks, 'ep', split_axis=0, concat_axis=0, tiled=True)]
    ppermute x1, waiting for transfers between devices: 2.47 us -> 0.42 us  [per_device(): theirs = lax.ppermute(mine, 'edp', swap)]
    ppermute x1 -> x2, waiting for transfers between devices: 2.56 us -> 1.54 us  [the longest x1 1.54 us: per_device(): arrived_late = lax.ppermute(other_late, 'edp', swap)]
  transfers between devices with their start and end apart: 3 -> 4, of which waited for: 3 -> 3; matrix products, arithmetic and copies ran while one was open for 0% -> 0% of each run, Pallas kernels for 9% -> 13%
where the time goes in v2:
time: 78.9 us; the launch traced here: 78.5 us
  blocking collectives  31.9 us (40%)
  Pallas kernels  23.7 us (30%)
  waiting for transfers between devices  17.9 us (23%)
  starting transfers between devices  4.31 us (5%)
    all_to_all x1, blocking collectives, exchange(): lax.all_to_all(blocks, 'ep', split_axis=0, concat_axis=0, tiled=True)  31.9 us
    all_to_all x1, waiting for transfers between devices, exchange(): lax.all_to_all(blocks, 'ep', split_axis=0, concat_axis=0, tiled=True)  16 us
    pallas_call x1, Pallas kernels, grads(): pl.pallas_call(grads_kernel, grid=(depth // COLS,), in_specs=[WHOLE] * 5,...  6.36 us
    pallas_call x1, Pallas kernels, expert(): pl.pallas_call(lambda *refs: expert_kernel(cap, *refs), in_specs=[WHOLE]...  6.04 us
    pallas_call x1, Pallas kernels, route(): pl.pallas_call(lambda *refs: route_kernel(cap, *refs), in_specs=[REMOTE]...  3.85 us
    all_to_all x1, starting transfers between devices, exchange(): lax.all_to_all(blocks, 'ep', split_axis=0, concat_axis=0, tiled=True)  3.66 us
    pallas_call x1, Pallas kernels, combine(): pl.pallas_call(combine_kernel, in_specs=[WHOLE, REMOTE], out_specs=[REMOT...  2.55 us
    pallas_call x1, Pallas kernels, load(): pl.pallas_call(load_kernel, in_specs=[REMOTE] * (1 + len(arrays)), out_sp...  2.05 us
  transfers between devices with their start and end apart: 4, of which 3 were waited for; matrix products, arithmetic and copies ran while one was open for 0% of the time, Pallas kernels for 13%

profile of v2, /device:TPU:0, one launch (start us, length us, event | category | flops | bytes accessed | tf_op | source)
XLA Modules:
  0.0 78.5 jit_solution(8594463980630571079)
XLA Ops:
  0.6 3.8 %route.1 = (bf16[128,3584]{1,0:T(8,128)(2,1)S(1)}, bf16[3,128,128]{2,1,0:T(8,128)(2,1)}) custom-call(s32[8,128]{1,0:T(8,128)} %bitcast.22, f32[8,128]{1,0:T(8,128)} %bitcast.23, bf16[128,3584]{1,0:T(8,128)(2,1)} %refs_2_.1, bf16[128,3584]{1,0:T(8,128)(2,1)} %refs_3_.1), custom_call_target="tpu_custom_call" | custom-call | tf_op jit(solution)/shard_map/route/pallas_call | solution.py:100
  4.5 31.9 %all_to_all.10 = bf16[16,8,3584]{2,1,0:T(8,128)(2,1)S(1)} all-to-all(bf16[16,8,3584]{2,1,0:T(8,128)(2,1)S(1)} %bitcast.17), channel_id=1, replica_groups=mesh['edp'=2,'ep'=16] {'ep'}, dimensions={0} | all-to-all | bytes 1835008 | tf_op jit(solution)/shard_map/all_to_all | solution.py:344
  36.4 0.0 collective-permute-start
  36.4 2.0 %load_weights.1.refs_2_.gate_ref = bf16[3584,512]{1,0:T(8,128)(2,1)S(1)} custom-call(bf16[128,3584]{1,0:T(8,128)(2,1)S(1)} %bitcast.13, bf16[3584,512]{1,0:T(8,128)(2,1)} %bitcast.18), custom_call_target="tpu_custom_call" | custom-call | tf_op jit(solution)/shard_map/load_weights/pallas_call | solution.py:130
  38.5 0.4 collective-permute-done.refs_1_.theirs_ref
  38.9 6.0 %expert.1 = (bf16[128,1536]{1,0:T(8,128)(2,1)S(1)}, bf16[128,1536]{1,0:T(8,128)(2,1)S(1)}, bf16[256,512]{1,0:T(8,128)(2,1)S(1)}, bf16[256,512]{1,0:T(8,128)(2,1)...) custom-call(bf16[128,3584]{1,0:T(8,128)(2,1)S(1)} %bitcast.14, ...), custom_call_target="tpu_custom_call" | custom-call | tf_op jit(solution)/shard_map/expert/pallas_call | solution.py:194
  45.0 0.2 collective-permute-start.1
  45.2 1.8 %late_rows.1 = (bf16[128,2048]{1,0:T(8,128)(2,1)S(1)}, bf16[128,2048]{1,0:T(8,128)(2,1)S(1)}) custom-call(bf16[3,256,512]{2,1,0:T(8,128)(2,1)S(1)} %get-tuple-element.26.stack_ref, bf16[3584,512]{1,0:T(8,128)(2,1)S(1)} %load_weights.1.refs_2_.gate_ref, bf16[3584,512]{1,0:T(8,128)(2,1)S(1)} %get-tuple-element.27.up_ref, ...), custom_call_target="tpu_custom_call" | custom-call | tf_op jit(solution)/shard_map/late_rows/pallas_call | solution.py:223
  47.0 0.0 collective-permute-done.1.other_early
  47.0 0.4 collective-permute-start.2
  47.4 1.5 %collective-permute-done.2.other_late = bf16[128,2048]{1,0:T(8,128)(2,1)S(1)} collective-permute-done((bf16[128,2048]{1,0:T(8,128)(2,1)S(1)}, bf16[128,2048]{1,0:T(8,128)(2,1)S(1)}, u32[]{:S(2)}, u32[]{:S(2)}) %collective-permute-start.2) | collective-permute-done | bytes 524320 | tf_op jit(solution)/shard_map/ppermute | solution.py:355
  49.0 1.0 %add_rows.1 = bf16[128,3584]{1,0:T(8,128)(2,1)} custom-call(bf16[128,1536]{1,0:T(8,128)(2,1)S(1)} %get-tuple-element.25.own_early, bf16[128,1536]{1,0:T(8,128)(2,1)S(1)} %collective-permute-done.1.other_early, bf16[128,2048]{1,0:T(8,128)(2,1)S(1)} %get-tuple-element.32.own_late, bf16[128,2048]{1,0:T(8,128)(2,1)S(1)} %collective-permute-done.2.other_late), custom_call_target="tpu_custom_call" | custom-call | tf_op jit(solution)/shard_map/add_rows/pallas_call | solution.py:252
  50.0 3.7 %all-to-all-start.1 = ((bf16[16,8,3584]{2,1,0:T(8,128)(2,1)}), bf16[16,8,3584]{2,1,0:T(8,128)(2,1)S(1)}, u32[]{:S(2)}, u32[]{:S(2)}) async-start(bf16[16,8,3584]{2,1,0:T(8,128)(2,1)} %bitcast.21), calls=%async_computation.1 | async-start | bytes 1835008 | tf_op jit(solution)/shard_map/all_to_all | solution.py:344
  53.6 6.4 %weight_grads.1 = (bf16[3584,512]{1,0:T(8,128)(2,1)}, bf16[3584,512]{1,0:T(8,128)(2,1)}, bf16[512,3584]{1,0:T(8,128)(2,1)}) custom-call(bf16[128,3584]{1,0:T(8,128)(2,1)S(1)} %bitcast.15, bf16[128,3584]{1,0:T(8,128)(2,1)S(1)} %collective-permute-done.refs_1_.theirs_ref, bf16[256,512]{1,0:T(8,128)(2,1)S(1)} %get-tuple-element.37.hid_ref, ...), custom_call_target="tpu_custom_call" | custom-call | tf_op jit(solution)/shard_map/weight_grads/pallas_call | solution.py:277
  60.0 16.0 %all-to-all-done.1 = bf16[16,8,3584]{2,1,0:T(8,128)(2,1)S(1)} async-done(((bf16[16,8,3584]{2,1,0:T(8,128)(2,1)}), bf16[16,8,3584]{2,1,0:T(8,128)(2,1)S(1)}, u32[]{:S(2)}, u32[]{:S(2)}) %all-to-all-start.1) | async-done | bytes 917536 | tf_op jit(solution)/shard_map/all_to_all | solution.py:344
  76.0 2.6 %combine.1 = (bf16[128,3584]{1,0:T(8,128)(2,1)}, bf16[128,3584]{1,0:T(8,128)(2,1)}) custom-call(bf16[128,3584]{1,0:T(8,128)(2,1)S(1)} %bitcast.16, bf16[3,128,128]{2,1,0:T(8,128)(2,1)} %get-tuple-element.34.select_hbm), custom_call_target="tpu_custom_call" | custom-call | tf_op jit(solution)/shard_map/combine/pallas_call | solution.py:318
Async XLA Ops:
  36.4 2.5 %collective-permute-start = (bf16[128,3584]{1,0:T(8,128)(2,1)S(1)}, bf16[128,3584]{1,0:T(8,128)(2,1)S(1)}, u32[]{:S(2)}, u32[]{:S(2)}) collective-permute-start(bf16[128,3584]{1,0:T(8,128)(2,1)S(1)} %bitcast.12), channel_id=1, source_target_pairs={{0,16},{16,0},{1,17},{17,1},{2,18},{18,2},{3,19},{19,3},{4,20},{20... | collective-permute-start | bytes 2752520 | tf_op jit(solution)/shard_map/ppermute | solution.py:347
  45.0 2.0 %collective-permute-start.1 = (bf16[128,1536]{1,0:T(8,128)(2,1)S(1)}, bf16[128,1536]{1,0:T(8,128)(2,1)S(1)}, u32[]{:S(2)}, u32[]{:S(2)}) collective-permute-start(bf16[128,1536]{1,0:T(8,128)(2,1)S(1)} %get-tuple-element.30), channel_id=1, source_target_pairs={{0,16},{16,0},{1,17},{17,1},{2,18},{18,2},{3,19},{19,3},{4,20},{20... | collective-permute-start | bytes 1179656 | tf_op jit(solution)/shard_map/ppermute | solution.py:352
  47.0 2.0 %collective-permute-start.2 = (bf16[128,2048]{1,0:T(8,128)(2,1)S(1)}, bf16[128,2048]{1,0:T(8,128)(2,1)S(1)}, u32[]{:S(2)}, u32[]{:S(2)}) collective-permute-start(bf16[128,2048]{1,0:T(8,128)(2,1)S(1)} %get-tuple-element.33), channel_id=1, source_target_pairs={{0,16},{16,0},{1,17},{17,1},{2,18},{18,2},{3,19},{19,3},{4,20},{20... | collective-permute-start | bytes 1572872 | tf_op jit(solution)/shard_map/ppermute | solution.py:355
  50.0 26.0 %all-to-all-start.1 = ((bf16[16,8,3584]{2,1,0:T(8,128)(2,1)}), bf16[16,8,3584]{2,1,0:T(8,128)(2,1)S(1)}, u32[]{:S(2)}, u32[]{:S(2)}) async-start(bf16[16,8,3584]{2,1,0:T(8,128)(2,1)} %bitcast.21), calls=%async_computation.1 | async-start | bytes 1835008 | tf_op jit(solution)/shard_map/all_to_all | solution.py:344

commit v3 on v2

v3 whole, which is shorter than its diff:
```python
import jax
import jax.numpy as jnp
from jax import lax
from jax.experimental import pallas as pl
from jax.experimental.pallas import tpu as pltpu
from jax.sharding import PartitionSpec as P

F32 = jnp.float32
BF16 = jnp.bfloat16
MIB = 1024 * 1024
SCOPED = 16 * MIB
ROWS_FIRST = (((0,), (0,)), ((), ()))
ROWS_LAST = (((1,), (1,)), ((), ()))
COLS = 512


def matmul(a, b, dims=(((1,), (0,)), ((), ()))):
    return lax.dot_general(a, b, dims, preferred_element_type=F32)


WHOLE = pl.BlockSpec(memory_space=pltpu.VMEM)
REMOTE = pl.BlockSpec(memory_space=pl.ANY)


def spread(depth):
    return [pl.ds(j * COLS, COLS) for j in range(depth // COLS)]


def in_hbm(*arrays):
    return [pltpu.with_memory_space_constraint(a, pltpu.HBM) for a in arrays]


def in_vmem(*arrays):
    return [pltpu.with_memory_space_constraint(a, pltpu.VMEM) for a in arrays]


def slots(cap, width, ids_ref, weight_ref, waits):
    tokens = ids_ref.shape[1]
    slot = lax.broadcasted_iota(jnp.int32, (width, tokens), 0)
    expert = slot // (2 * cap)
    place = slot % (2 * cap)
    before = lax.broadcasted_iota(jnp.int32, (tokens, tokens), 0) < lax.broadcasted_iota(
        jnp.int32, (tokens, tokens), 1
    )
    before = jnp.where(before, 1.0, 0.0).astype(BF16)
    for copy in waits:
        copy.wait()
    member = jnp.zeros((width, tokens), F32)
    weight = jnp.zeros((width, tokens), F32)
    for k in range(ids_ref.shape[0]):
        hit = ids_ref[k : k + 1, :] == expert
        member = jnp.where(hit, 1.0, member)
        weight = jnp.where(hit, weight_ref[k : k + 1, :], weight)
    rank = matmul(member.astype(BF16), before)
    chosen = jnp.where(rank == (place % cap).astype(F32), member, 0.0)
    forward = jnp.where(place < cap, chosen, 0.0)
    return forward, chosen - forward, weight


def route_kernel(
    cap, ids_hbm, weight_hbm, tok_hbm, cot_hbm, send_ref, ids_ref, weight_ref, tok_ref, cot_ref, small_sems, sems
):
    parts = spread(tok_hbm.shape[1])
    small = [
        pltpu.make_async_copy(ids_hbm, ids_ref, small_sems.at[0]),
        pltpu.make_async_copy(weight_hbm, weight_ref, small_sems.at[1]),
    ]
    copies = [
        (
            pltpu.make_async_copy(tok_hbm.at[:, cols], tok_ref.at[:, cols], sems.at[0, j]),
            pltpu.make_async_copy(cot_hbm.at[:, cols], cot_ref.at[:, cols], sems.at[1, j]),
        )
        for j, cols in enumerate(parts)
    ]
    for copy in small:
        copy.start()
    for pair in copies:
        for copy in pair:
            copy.start()
    forward, backward, weight = slots(cap, send_ref.shape[0], ids_ref, weight_ref, small)
    scale = jnp.sum(forward + backward * weight, axis=1, keepdims=True)
    picks = jnp.concatenate([forward, backward], axis=1).astype(BF16)
    for pair, cols in zip(copies, parts):
        for copy in pair:
            copy.wait()
        rows = matmul(picks, jnp.concatenate([tok_ref[:, cols], cot_ref[:, cols]], axis=0))
        send_ref[:, cols] = (rows * scale).astype(BF16)


def route(ids, weight, tokens, cotangent, experts, cap):
    rows, depth = tokens.shape
    width = experts * 2 * cap
    return pl.pallas_call(
        lambda *refs: route_kernel(cap, *refs),
        in_specs=[REMOTE] * 4,
        out_specs=WHOLE,
        out_shape=pltpu.VMEM((width, depth), BF16),
        scratch_shapes=[
            pltpu.VMEM(ids.shape, jnp.int32),
            pltpu.VMEM(weight.shape, F32),
            pltpu.VMEM((rows, depth), BF16),
            pltpu.VMEM((rows, depth), BF16),
            pltpu.SemaphoreType.DMA((2,)),
            pltpu.SemaphoreType.DMA((2, depth // COLS)),
        ],
        compiler_params=pltpu.CompilerParams(vmem_limit_bytes=16 * MIB),
        name="route",
    )(*in_hbm(ids, weight, tokens, cotangent))


def select_kernel(cap, ids_hbm, weight_hbm, select_hbm, ids_ref, weight_ref, select_ref, sems):
    small = [
        pltpu.make_async_copy(ids_hbm, ids_ref, sems.at[0]),
        pltpu.make_async_copy(weight_hbm, weight_ref, sems.at[1]),
    ]
    for copy in small:
        copy.start()
    forward, backward, weight = slots(cap, select_ref.shape[1], ids_ref, weight_ref, small)
    weighted = jnp.transpose(forward * weight)
    high = weighted.astype(BF16)
    count = high.shape[0]
    select_ref[:count] = high
    select_ref[count : 2 * count] = (weighted - high.astype(F32)).astype(BF16)
    select_ref[2 * count :] = jnp.transpose(backward).astype(BF16)
    copy = pltpu.make_async_copy(select_ref, select_hbm, sems.at[2])
    copy.start()
    copy.wait()


def selectors(ids, weight, experts, cap):
    shape = (3 * ids.shape[1], experts * 2 * cap)
    return pl.pallas_call(
        lambda *refs: select_kernel(cap, *refs),
        in_specs=[REMOTE] * 2,
        out_specs=REMOTE,
        out_shape=pltpu.HBM(shape, BF16),
        scratch_shapes=[
            pltpu.VMEM(ids.shape, jnp.int32),
            pltpu.VMEM(weight.shape, F32),
            pltpu.VMEM(shape, BF16),
            pltpu.SemaphoreType.DMA((3,)),
        ],
        compiler_params=pltpu.CompilerParams(vmem_limit_bytes=8 * MIB),
        name="selectors",
    )(*in_hbm(ids, weight))


def compact_kernel(cap, rows_ref, tok_ref, cot_ref):
    groups = rows_ref.shape[0] // (2 * cap)
    half = tok_ref.shape[0]
    for cols in spread(rows_ref.shape[1]):
        both = rows_ref[:, cols].astype(F32).reshape(groups, 2, cap, COLS)
        tok_ref[:, cols] = both[:, 0].reshape(half, COLS).astype(BF16)
        cot_ref[:, cols] = both[:, 1].reshape(half, COLS).astype(BF16)


def compact(rows, cap):
    half, depth = rows.shape[0] // 2, rows.shape[1]
    return pl.pallas_call(
        lambda *refs: compact_kernel(cap, *refs),
        in_specs=[WHOLE],
        out_specs=[WHOLE] * 2,
        out_shape=[pltpu.VMEM((half, depth), BF16)] * 2,
        compiler_params=pltpu.CompilerParams(vmem_limit_bytes=8 * MIB),
        name="compact",
    )(*in_vmem(rows))


def split_store(value, own_ref, other_ref, cols):
    half = own_ref.shape[0]
    own_ref[:, cols] = value[:half].astype(BF16)
    other_ref[:, cols] = value[half:].astype(BF16)


def forward_kernel(
    mine_ref, theirs_ref, gate_ref, up_ref, down_ref, own_ref, other_ref, hid_ref, gate_act_ref, up_act_ref
):
    rows = jnp.concatenate([mine_ref[...], theirs_ref[...]], axis=0)
    gate_act = matmul(rows, gate_ref[...])
    up_act = matmul(rows, up_ref[...])
    gate_act_ref[...] = gate_act
    up_act_ref[...] = up_act
    hidden = (gate_act * jax.nn.sigmoid(gate_act) * up_act).astype(BF16)
    hid_ref[...] = hidden
    for cols in spread(mine_ref.shape[1]):
        split_store(matmul(hidden, down_ref[:, cols]), own_ref, other_ref, cols)


def forward(mine, theirs, gate, up, down):
    half, depth = mine.shape
    width = gate.shape[1]
    return pl.pallas_call(
        forward_kernel,
        in_specs=[WHOLE] * 5,
        out_specs=[WHOLE] * 5,
        out_shape=[
            pltpu.VMEM((half, depth), BF16),
            pltpu.VMEM((half, depth), BF16),
            pltpu.VMEM((2 * half, width), BF16),
            pltpu.VMEM((2 * half, width), F32),
            pltpu.VMEM((2 * half, width), F32),
        ],
        compiler_params=pltpu.CompilerParams(vmem_limit_bytes=SCOPED),
        name="expert_forward",
    )(*in_vmem(mine, theirs, gate, up, down))


def row_grads(gate_cot, up_cot, gate_ref, up_ref, own_ref, other_ref, first):
    for j in range(own_ref.shape[1] // COLS):
        cols = pl.ds((first + j) * COLS, COLS)
        back = matmul(gate_cot, gate_ref[cols, :], ROWS_LAST)
        back = back + matmul(up_cot, up_ref[cols, :], ROWS_LAST)
        split_store(back, own_ref, other_ref, pl.ds(j * COLS, COLS))


def backward_kernel(
    mine_ref, theirs_ref, gate_ref, up_ref, down_ref, gate_act_ref, up_act_ref,
    own_ref, other_ref, gate_cot_ref, up_cot_ref,
):
    rows = jnp.concatenate([mine_ref[...], theirs_ref[...]], axis=0)
    hidden_cot = matmul(rows, down_ref[...], ROWS_LAST)
    gate_act = gate_act_ref[...]
    sigma = jax.nn.sigmoid(gate_act)
    gate_cot = (hidden_cot * up_act_ref[...] * sigma * (1.0 + gate_act * (1.0 - sigma))).astype(BF16)
    up_cot = (hidden_cot * (gate_act * sigma)).astype(BF16)
    gate_cot_ref[...] = gate_cot
    up_cot_ref[...] = up_cot
    row_grads(gate_cot, up_cot, gate_ref, up_ref, own_ref, other_ref, 0)


def early_cols(depth):
    return depth // COLS * 4 // 7 * COLS


def backward(mine, theirs, gate, up, down, gate_act, up_act):
    half, depth = mine.shape
    width = gate.shape[1]
    early = early_cols(depth)
    return pl.pallas_call(
        backward_kernel,
        in_specs=[WHOLE] * 7,
        out_specs=[WHOLE] * 4,
        out_shape=[pltpu.VMEM((half, early), BF16)] * 2 + [pltpu.VMEM((2 * half, width), BF16)] * 2,
        compiler_params=pltpu.CompilerParams(vmem_limit_bytes=SCOPED),
        name="expert_backward",
    )(*in_vmem(mine, theirs, gate, up, down, gate_act, up_act))


def late_kernel(gate_cot_ref, up_cot_ref, gate_ref, up_ref, own_ref, other_ref):
    first = (gate_ref.shape[0] - own_ref.shape[1]) // COLS
    row_grads(gate_cot_ref[...], up_cot_ref[...], gate_ref, up_ref, own_ref, other_ref, first)


def late_rows(gate_cot, up_cot, gate, up):
    half = gate_cot.shape[0] // 2
    depth = gate.shape[0]
    late = depth - early_cols(depth)
    return pl.pallas_call(
        late_kernel,
        in_specs=[WHOLE] * 4,
        out_specs=[WHOLE] * 2,
        out_shape=[pltpu.VMEM((half, late), BF16)] * 2,
        compiler_params=pltpu.CompilerParams(vmem_limit_bytes=8 * MIB),
        name="late_rows",
    )(*in_vmem(gate_cot, up_cot, gate, up))


def add_kernel(cap, *refs):
    own_out, arrived_out, own_early, arrived_early, own_late, arrived_late, out_hbm, out_ref, sems = refs
    early = own_early.shape[1]
    rows = out_ref.shape[0]
    groups = rows // (2 * cap)
    copies = []
    for j, cols in enumerate(spread(out_ref.shape[1])):
        if j * COLS < early:
            a, b, here = own_early, arrived_early, pl.ds(j * COLS, COLS)
        else:
            a, b, here = own_late, arrived_late, pl.ds(j * COLS - early, COLS)
        out = own_out[:, cols].astype(F32) + arrived_out[:, cols].astype(F32)
        grad = a[:, here].astype(F32) + b[:, here].astype(F32)
        both = jnp.concatenate([out.reshape(groups, cap, COLS), grad.reshape(groups, cap, COLS)], axis=1)
        out_ref[:, cols] = both.reshape(rows, COLS).astype(BF16)
        copy = pltpu.make_async_copy(out_ref.at[:, cols], out_hbm.at[:, cols], sems.at[j])
        copy.start()
        copies.append(copy)
    for copy in copies:
        copy.wait()


def add_rows(cap, *arrays):
    half, depth = arrays[0].shape
    return pl.pallas_call(
        lambda *refs: add_kernel(cap, *refs),
        in_specs=[WHOLE] * 6,
        out_specs=REMOTE,
        out_shape=pltpu.HBM((2 * half, depth), BF16),
        scratch_shapes=[pltpu.VMEM((2 * half, depth), BF16), pltpu.SemaphoreType.DMA((depth // COLS,))],
        compiler_params=pltpu.CompilerParams(vmem_limit_bytes=16 * MIB),
        name="add_rows",
    )(*in_vmem(*arrays))


def grads_kernel(
    tok_mine, tok_theirs, cot_mine, cot_theirs, hid_ref, gate_cot_ref, up_cot_ref, gate_ref, up_ref, down_ref
):
    cols = pl.ds(pl.multiple_of(pl.program_id(0) * COLS, COLS), COLS)
    width = gate_ref.shape[1]
    pair = jnp.concatenate([gate_cot_ref[...], up_cot_ref[...]], axis=1)
    tokens = jnp.concatenate([tok_mine[:, cols], tok_theirs[:, cols]], axis=0)
    both = matmul(tokens, pair, ROWS_FIRST)
    gate_ref[...] = both[:, :width].astype(BF16)
    up_ref[...] = both[:, width:].astype(BF16)
    cotangent = jnp.concatenate([cot_mine[:, cols], cot_theirs[:, cols]], axis=0)
    down_ref[...] = matmul(hid_ref[...], cotangent, ROWS_FIRST).astype(BF16)


def grads(tok_mine, tok_theirs, cot_mine, cot_theirs, hidden, gate_cot, up_cot):
    depth = tok_mine.shape[1]
    width = hidden.shape[1]
    return pl.pallas_call(
        grads_kernel,
        grid=(depth // COLS,),
        in_specs=[WHOLE] * 7,
        out_specs=[
            pl.BlockSpec((COLS, width), lambda j: (j, 0)),
            pl.BlockSpec((COLS, width), lambda j: (j, 0)),
            pl.BlockSpec((width, COLS), lambda j: (0, j)),
        ],
        out_shape=[
            jax.ShapeDtypeStruct((depth, width), BF16),
            jax.ShapeDtypeStruct((depth, width), BF16),
            jax.ShapeDtypeStruct((width, depth), BF16),
        ],
        compiler_params=pltpu.CompilerParams(vmem_limit_bytes=SCOPED),
        name="weight_grads",
    )(*in_vmem(tok_mine, tok_theirs, cot_mine, cot_theirs, hidden, gate_cot, up_cot))


def combine_kernel(back_ref, select_hbm, out_hbm, grad_hbm, select_ref, out_ref, grad_ref, select_sem, sems):
    load_select = pltpu.make_async_copy(select_hbm, select_ref, select_sem)
    load_select.start()
    load_select.wait()
    count = out_ref.shape[0]
    copies = []
    for j, cols in enumerate(spread(back_ref.shape[1])):
        sums = matmul(select_ref[...], back_ref[:, cols])
        out_ref[:, cols] = (sums[:count] + sums[count : 2 * count]).astype(BF16)
        grad_ref[:, cols] = sums[2 * count :].astype(BF16)
        pair = [
            pltpu.make_async_copy(out_ref.at[:, cols], out_hbm.at[:, cols], sems.at[0, j]),
            pltpu.make_async_copy(grad_ref.at[:, cols], grad_hbm.at[:, cols], sems.at[1, j]),
        ]
        for copy in pair:
            copy.start()
        copies.extend(pair)
    for copy in copies:
        copy.wait()


def combine(back, select):
    width, depth = back.shape
    rows = select.shape[0] // 3
    return pl.pallas_call(
        combine_kernel,
        in_specs=[WHOLE, REMOTE],
        out_specs=[REMOTE, REMOTE],
        out_shape=[pltpu.HBM((rows, depth), BF16)] * 2,
        scratch_shapes=[
            pltpu.VMEM(select.shape, BF16),
            pltpu.VMEM((rows, depth), BF16),
            pltpu.VMEM((rows, depth), BF16),
            pltpu.SemaphoreType.DMA,
            pltpu.SemaphoreType.DMA((2, depth // COLS)),
        ],
        compiler_params=pltpu.CompilerParams(vmem_limit_bytes=8 * MIB),
        name="combine",
    )(*in_vmem(back), *in_hbm(select))


def per_device(tokens, cotangent, expert_ids, route_weight, gate_weight, up_weight, down_weight):
    experts = lax.axis_size("ep")
    cap = tokens.shape[0] // 32
    depth = tokens.shape[1]
    swap = [(0, 1), (1, 0)]
    ids, weight = expert_ids.T, route_weight.T
    send = route(ids, weight, tokens, cotangent, experts, cap)
    select = selectors(ids, weight, experts, cap)

    def exchange(rows):
        blocks = rows.reshape(experts, 2 * cap, depth)
        return lax.all_to_all(blocks, "ep", split_axis=0, concat_axis=0, tiled=True).reshape(rows.shape)

    def swapped(rows, after=None):
        if after is not None:
            rows, after = lax.optimization_barrier((rows, after))
        return lax.ppermute(rows, "edp", swap), after

    gate, up, down = [
        lax.ppermute(w[0], "edp", swap) for w in (gate_weight, up_weight, down_weight)
    ]
    tok_mine, cot_mine = compact(exchange(send), cap)
    tok_theirs, _ = swapped(tok_mine)
    cot_theirs, tok_theirs = swapped(cot_mine, tok_theirs)
    own_out, other_out, hidden, gate_act, up_act = forward(tok_mine, tok_theirs, gate, up, down)
    arrived_out, cot_theirs = swapped(other_out, cot_theirs)
    own_early, other_early, gate_cot, up_cot = backward(
        cot_mine, cot_theirs, gate, up, down, gate_act, up_act
    )
    arrived_early, arrived_out = swapped(other_early, arrived_out)
    own_late, other_late = late_rows(gate_cot, up_cot, gate, up)
    arrived_late, arrived_early = swapped(other_late, arrived_early)
    back = exchange(
        add_rows(cap, own_out, arrived_out, own_early, arrived_early, own_late, arrived_late)
    )
    hidden, gate_cot, up_cot = [lax.ppermute(a, "edp", swap) for a in (hidden, gate_cot, up_cot)]
    grad_gate, grad_up, grad_down = grads(
        tok_theirs, tok_mine, cot_theirs, cot_mine, hidden, gate_cot, up_cot
    )
    routed_out, token_grad = combine(back, select)
    return (routed_out, token_grad, grad_gate[None], grad_up[None], grad_down[None])


def solution(mesh):
    in_specs = (
        P(("edp", "ep"), None),
        P(("edp", "ep"), None),
        P(("edp", "ep"), None),
        P(("edp", "ep"), None),
        P("ep", None, "edp"),
        P("ep", None, "edp"),
        P("ep", "edp", None),
    )
    out_specs = (
        P(("edp", "ep"), None),
        P(("edp", "ep"), None),
        P("ep", None, "edp"),
        P("ep", None, "edp"),
        P("ep", "edp", None),
    )
    return jax.shard_map(
        per_device, mesh=mesh, in_specs=in_specs, out_specs=out_specs, check_vma=False
    )
```

time: 78.9 us -> 77.1 us (0.977)
  Pallas kernels: 23.7 us -> 20.5 us
  starting transfers between devices: 4.31 us -> 6.46 us
  waiting for transfers between devices: 17.9 us -> 16.9 us
    all_to_all x1, waiting for transfers between devices: 16 us -> 13.6 us  [exchange(): lax.all_to_all(blocks, 'ep', split_axis=0, concat_axis=0, tiled=True)]
    ppermute x3 -> x11, starting transfers between devices: 0.65 us -> 2.8 us  [the longest x3 1.03 us: per_device(): lax.ppermute(w[0], 'edp', swap)]
    pallas_call x4 -> x6, Pallas kernels: 15.5 us -> 13.7 us  [the longest x1 6.36 us: grads(): pl.pallas_call(grads_kernel, grid=(depth // COLS,), in_specs=[WHOLE] * 7,...]
    ppermute x3 -> x11, waiting for transfers between devices: 1.95 us -> 3.33 us  [the longest x5 3.31 us: swapped(): return (lax.ppermute(rows, 'edp', swap), after)]
  transfers between devices with their start and end apart: 4 -> 12, of which waited for: 3 -> 4; matrix products, arithmetic and copies ran while one was open for 0% -> 0% of each run, Pallas kernels for 13% -> 22%
where the time goes in v3:
time: 77.1 us; the launch traced here: 76.8 us
  blocking collectives  32.2 us (42%)
  Pallas kernels  20.5 us (27%)
  waiting for transfers between devices  16.9 us (22%)
  starting transfers between devices  6.46 us (8%)
    all_to_all x1, blocking collectives, exchange(): lax.all_to_all(blocks, 'ep', split_axis=0, concat_axis=0, tiled=True)  32.2 us
    all_to_all x1, waiting for transfers between devices, exchange(): lax.all_to_all(blocks, 'ep', split_axis=0, concat_axis=0, tiled=True)  13.6 us
    pallas_call x1, Pallas kernels, grads(): pl.pallas_call(grads_kernel, grid=(depth // COLS,), in_specs=[WHOLE] * 7,...  6.36 us
    all_to_all x1, starting transfers between devices, exchange(): lax.all_to_all(blocks, 'ep', split_axis=0, concat_axis=0, tiled=True)  3.66 us
    ppermute x5, waiting for transfers between devices, swapped(): return (lax.ppermute(rows, 'edp', swap), after)  3.31 us
    pallas_call x1, Pallas kernels, route(): pl.pallas_call(lambda *refs: route_kernel(cap, *refs), in_specs=[REMOTE]...  3.08 us
    pallas_call x1, Pallas kernels, backward(): pl.pallas_call(backward_kernel, in_specs=[WHOLE] * 7, out_specs=[WHOLE] *...  2.7 us
    pallas_call x1, Pallas kernels, combine(): pl.pallas_call(combine_kernel, in_specs=[WHOLE, REMOTE], out_specs=[REMOT...  2.55 us
  transfers between devices with their start and end apart: 12, of which 4 were waited for; matrix products, arithmetic and copies ran while one was open for 0% of the time, Pallas kernels for 22%

profile of v3, /device:TPU:0, one launch (start us, length us, event | category | flops | bytes accessed | tf_op | source)
XLA Modules:
  0.0 76.8 jit_solution(8743828337718788424)
XLA Ops:
  0.6 0.5 collective-permute-start.1
  1.2 0.1 collective-permute-start.2
  1.2 0.4 collective-permute-start.3
  1.7 3.1 %route.1 = bf16[128,3584]{1,0:T(8,128)(2,1)S(1)} custom-call(s32[8,128]{1,0:T(8,128)} %bitcast.16, f32[8,128]{1,0:T(8,128)} %bitcast.18, bf16[128,3584]{1,0:T(8,128)(2,1)} %refs_2_.1, bf16[128,3584]{1,0:T(8,128)(2,1)} %refs_3_.1), custom_call_target="tpu_custom_call" | custom-call | tf_op jit(solution)/shard_map/route/pallas_call | solution.py:93
  4.8 32.2 %all_to_all.10 = bf16[16,8,3584]{2,1,0:T(8,128)(2,1)S(1)} all-to-all(bf16[16,8,3584]{2,1,0:T(8,128)(2,1)S(1)} %bitcast.14), channel_id=1, replica_groups=mesh['edp'=2,'ep'=16] {'ep'}, dimensions={0} | all-to-all | bytes 1835008 | tf_op jit(solution)/shard_map/all_to_all | solution.py:391
  36.9 0.2 compact.1
  37.1 0.1 collective-permute-start
  37.2 1.8 %collective-permute-done.theirs_ref.tok_mine = bf16[64,3584]{1,0:T(8,128)(2,1)S(1)} collective-permute-done((bf16[64,3584]{1,0:T(8,128)(2,1)S(1)}, bf16[64,3584]{1,0:T(8,128)(2,1)S(1)}, u32[]{:S(2)}, u32[]{:S(2)}) %collective-permute-start) | collective-permute-done | bytes 458784 | tf_op jit(solution)/shard_map/ppermute | solution.py:396
  39.0 0.1 collective-permute-start.4
  39.1 0.0 collective-permute-done.1.gate_ref
  39.1 0.0 collective-permute-done.2.up_ref
  39.1 0.0 collective-permute-done.3.down_ref
  39.1 1.7 %expert_forward.1 = (bf16[64,3584]{1,0:T(8,128)(2,1)S(1)}, bf16[64,3584]{1,0:T(8,128)(2,1)S(1)}, bf16[128,512]{1,0:T(8,128)(2,1)S(1)}, f32[128,512]{1,0:T(8,128)S(1)}, f32[128,512]{1,0:T(8,128)S(1)}) custom-call(bf16[64,3584]{1,0:T(8,128)(2,1)S(1)} %get-tuple-element.31.mine_ref.tok_theirs, bf16[64,3584]{1,0:T(8,128)(2,1)S(1)} %collective-permute-done.theirs_ref.tok_mine, ...), custom_call_target="tpu_custom_call" | custom-call | tf_op jit(solution)/shard_map/expert_forward/pallas_call | solution.py:192
  40.9 0.0 collective-permute-done.4.theirs_ref.cot_mine
  40.9 0.4 collective-permute-start.5
  41.3 2.7 %expert_backward.1 = (bf16[64,2048]{1,0:T(8,128)(2,1)S(1)}, bf16[64,2048]{1,0:T(8,128)(2,1)S(1)}, bf16[128,512]{1,0:T(8,128)(2,1)S(1)}, bf16[128,512]{1,0:T(8,128)(2,1)S(1)}) custom-call(bf16[64,3584]{1,0:T(8,128)(2,1)S(1)} %get-tuple-element.36.mine_ref.cot_theirs, bf16[64,3584]{1,0:T(8,128)(2,1)S(1)} %collective-permute-done.4.theirs_ref.cot_mine, ...), custom_call_target="tpu_custom_call" | custom-call | tf_op jit(solution)/shard_map/expert_backward/pallas_call | solution.py:239
  44.0 0.0 collective-permute-done.5.refs_1_
  44.0 0.2 collective-permute-start.6
  44.2 1.1 %late_rows.1 = (bf16[64,1536]{1,0:T(8,128)(2,1)S(1)}, bf16[64,1536]{1,0:T(8,128)(2,1)S(1)}) custom-call(bf16[128,512]{1,0:T(8,128)(2,1)S(1)} %get-tuple-element.44.gate_cot_ref, bf16[128,512]{1,0:T(8,128)(2,1)S(1)} %get-tuple-element.45.up_cot_ref, bf16[3584,512]{1,0:T(8,128)(2,1)S(1)} %collective-permute-done.1.gate_ref, ...), custom_call_target="tpu_custom_call" | custom-call | tf_op jit(solution)/shard_map/late_rows/pallas_call | solution.py:258
  45.4 0.3 collective-permute-done.6.refs_3_
  45.6 0.2 collective-permute-start.7
  45.8 1.3 %collective-permute-done.7.refs_5_ = bf16[64,1536]{1,0:T(8,128)(2,1)S(1)} collective-permute-done((bf16[64,1536]{1,0:T(8,128)(2,1)S(1)}, bf16[64,1536]{1,0:T(8,128)(2,1)S(1)}, u32[]{:S(2)}, u32[]{:S(2)}) %collective-permute-start.7) | collective-permute-done | bytes 196640 | tf_op jit(solution)/shard_map/ppermute | solution.py:396
  47.1 1.1 %add_rows.1 = bf16[128,3584]{1,0:T(8,128)(2,1)} custom-call(bf16[64,3584]{1,0:T(8,128)(2,1)S(1)} %get-tuple-element.34.refs_0_, bf16[64,3584]{1,0:T(8,128)(2,1)S(1)} %collective-permute-done.5.refs_1_, bf16[64,2048]{1,0:T(8,128)(2,1)S(1)} %get-tuple-element.43.refs_2_, bf16[64,2048]{1,0:T(8,128)(2,1)S(1)} %collective-permute-done.6.refs_3_, ...), custom_call_target="tpu_custom_call" | custom-call | tf_op jit(solution)/shard_map/add_rows/pallas_call | solution.py:292
  48.2 3.7 %all-to-all-start.1 = ((bf16[16,8,3584]{2,1,0:T(8,128)(2,1)}), bf16[16,8,3584]{2,1,0:T(8,128)(2,1)S(1)}, u32[]{:S(2)}, u32[]{:S(2)}) async-start(bf16[16,8,3584]{2,1,0:T(8,128)(2,1)} %bitcast.15), calls=%async_computation.1 | async-start | bytes 1835008 | tf_op jit(solution)/shard_map/all_to_all | solution.py:391
  51.9 0.2 collective-permute-start.8
  52.1 0.3 collective-permute-start.9
  52.4 0.2 collective-permute-start.10
  52.6 1.6 %selectors.1.select_hbm = bf16[384,128]{1,0:T(8,128)(2,1)} custom-call(s32[8,128]{1,0:T(8,128)} %bitcast.17, f32[8,128]{1,0:T(8,128)} %bitcast.19), custom_call_target="tpu_custom_call" | custom-call | tf_op jit(solution)/shard_map/selectors/pallas_call | solution.py:132
  54.2 0.0 collective-permute-done.8.hid_ref
  54.3 0.0 collective-permute-done.9.gate_cot_ref
  54.3 0.0 collective-permute-done.10.up_cot_ref
  54.3 6.4 %weight_grads.1 = (bf16[3584,512]{1,0:T(8,128)(2,1)}, bf16[3584,512]{1,0:T(8,128)(2,1)}, bf16[512,3584]{1,0:T(8,128)(2,1)}) custom-call(bf16[64,3584]{1,0:T(8,128)(2,1)S(1)} %collective-permute-done.theirs_ref.tok_mine, bf16[64,3584]{1,0:T(8,128)(2,1)S(1)} %get-tuple-element.31.mine_ref.tok_theirs, ...), custom_call_target="tpu_custom_call" | custom-call | tf_op jit(solution)/shard_map/weight_grads/pallas_call | solution.py:320
  60.6 13.6 %all-to-all-done.1 = bf16[16,8,3584]{2,1,0:T(8,128)(2,1)S(1)} async-done(((bf16[16,8,3584]{2,1,0:T(8,128)(2,1)}), bf16[16,8,3584]{2,1,0:T(8,128)(2,1)S(1)}, u32[]{:S(2)}, u32[]{:S(2)}) %all-to-all-start.1) | async-done | bytes 917536 | tf_op jit(solution)/shard_map/all_to_all | solution.py:391
  74.2 2.5 %combine.1 = (bf16[128,3584]{1,0:T(8,128)(2,1)}, bf16[128,3584]{1,0:T(8,128)(2,1)}) custom-call(bf16[128,3584]{1,0:T(8,128)(2,1)S(1)} %bitcast.13, bf16[384,128]{1,0:T(8,128)(2,1)} %selectors.1.select_hbm), custom_call_target="tpu_custom_call" | custom-call | tf_op jit(solution)/shard_map/combine/pallas_call | solution.py:363
Async XLA Ops:
  0.6 38.5 %collective-permute-start.1 = (bf16[3584,512]{1,0:T(8,128)(2,1)}, bf16[3584,512]{1,0:T(8,128)(2,1)S(1)}, u32[]{:S(2)}, u32[]{:S(2)}) collective-permute-start(bf16[3584,512]{1,0:T(8,128)(2,1)} %bitcast.20), channel_id=1, source_target_pairs={{0,16},{16,0},{1,17},{17,1},{2,18},{18,2},{3,19},{19,3},{4,20},{20... | collective-permute-start | bytes 11010056 | tf_op jit(solution)/shard_map/ppermute | solution.py:399
  1.2 38.0 %collective-permute-start.2 = (bf16[3584,512]{1,0:T(8,128)(2,1)}, bf16[3584,512]{1,0:T(8,128)(2,1)S(1)}, u32[]{:S(2)}, u32[]{:S(2)}) collective-permute-start(bf16[3584,512]{1,0:T(8,128)(2,1)} %bitcast.21), channel_id=1, source_target_pairs={{0,16},{16,0},{1,17},{17,1},{2,18},{18,2},{3,19},{19,3},{4,20},{20... | collective-permute-start | bytes 11010056 | tf_op jit(solution)/shard_map/ppermute | solution.py:399
  1.2 37.9 %collective-permute-start.3 = (bf16[512,3584]{1,0:T(8,128)(2,1)}, bf16[512,3584]{1,0:T(8,128)(2,1)S(1)}, u32[]{:S(2)}, u32[]{:S(2)}) collective-permute-start(bf16[512,3584]{1,0:T(8,128)(2,1)} %bitcast.22), channel_id=1, source_target_pairs={{0,16},{16,0},{1,17},{17,1},{2,18},{18,2},{3,19},{19,3},{4,20},{20... | collective-permute-start | bytes 11010056 | tf_op jit(solution)/shard_map/ppermute | solution.py:399
  37.1 1.9 %collective-permute-start = (bf16[64,3584]{1,0:T(8,128)(2,1)S(1)}, bf16[64,3584]{1,0:T(8,128)(2,1)S(1)}, u32[]{:S(2)}, u32[]{:S(2)}) collective-permute-start(bf16[64,3584]{1,0:T(8,128)(2,1)S(1)} %get-tuple-element.31.mine_ref.tok_theirs), channel_id=1, source_target_pairs={{0,16},{16,0},{1,17},{17,1},{2,18},{18,2},{3,19},{19,3},{4,20},{20... | collective-permute-start | bytes 1376264 | tf_op jit(solution)/shard_map/ppermute | solution.py:396
  39.0 1.9 %collective-permute-start.4 = (bf16[64,3584]{1,0:T(8,128)(2,1)S(1)}, bf16[64,3584]{1,0:T(8,128)(2,1)S(1)}, u32[]{:S(2)}, u32[]{:S(2)}) collective-permute-start(bf16[64,3584]{1,0:T(8,128)(2,1)S(1)} %get-tuple-element.36.mine_ref.cot_theirs), channel_id=1, source_target_pairs={{0,16},{16,0},{1,17},{17,1},{2,18},{18,2},{3,19},{19,3},{4,20},{20... | collective-permute-start | bytes 1376264 | tf_op jit(solution)/shard_map/ppermute | solution.py:396
  40.9 3.1 %collective-permute-start.5 = (bf16[64,3584]{1,0:T(8,128)(2,1)S(1)}, bf16[64,3584]{1,0:T(8,128)(2,1)S(1)}, u32[]{:S(2)}, u32[]{:S(2)}) collective-permute-start(bf16[64,3584]{1,0:T(8,128)(2,1)S(1)} %get-tuple-element.41), channel_id=1, source_target_pairs={{0,16},{16,0},{1,17},{17,1},{2,18},{18,2},{3,19},{19,3},{4,20},{20... | collective-permute-start | bytes 1376264 | tf_op jit(solution)/shard_map/ppermute | solution.py:396
  44.0 1.6 %collective-permute-start.6 = (bf16[64,2048]{1,0:T(8,128)(2,1)S(1)}, bf16[64,2048]{1,0:T(8,128)(2,1)S(1)}, u32[]{:S(2)}, u32[]{:S(2)}) collective-permute-start(bf16[64,2048]{1,0:T(8,128)(2,1)S(1)} %get-tuple-element.47), channel_id=1, source_target_pairs={{0,16},{16,0},{1,17},{17,1},{2,18},{18,2},{3,19},{19,3},{4,20},{20... | collective-permute-start | bytes 786440 | tf_op jit(solution)/shard_map/ppermute | solution.py:396
  45.6 1.4 %collective-permute-start.7 = (bf16[64,1536]{1,0:T(8,128)(2,1)S(1)}, bf16[64,1536]{1,0:T(8,128)(2,1)S(1)}, u32[]{:S(2)}, u32[]{:S(2)}) collective-permute-start(bf16[64,1536]{1,0:T(8,128)(2,1)S(1)} %get-tuple-element.50), channel_id=1, source_target_pairs={{0,16},{16,0},{1,17},{17,1},{2,18},{18,2},{3,19},{19,3},{4,20},{20... | collective-permute-start | bytes 589832 | tf_op jit(solution)/shard_map/ppermute | solution.py:396
  48.2 26.0 %all-to-all-start.1 = ((bf16[16,8,3584]{2,1,0:T(8,128)(2,1)}), bf16[16,8,3584]{2,1,0:T(8,128)(2,1)S(1)}, u32[]{:S(2)}, u32[]{:S(2)}) async-start(bf16[16,8,3584]{2,1,0:T(8,128)(2,1)} %bitcast.15), calls=%async_computation.1 | async-start | bytes 1835008 | tf_op jit(solution)/shard_map/all_to_all | solution.py:391
  51.9 2.4 %collective-permute-start.8 = (bf16[128,512]{1,0:T(8,128)(2,1)S(1)}, bf16[128,512]{1,0:T(8,128)(2,1)S(1)}, u32[]{:S(2)}, u32[]{:S(2)}) collective-permute-start(bf16[128,512]{1,0:T(8,128)(2,1)S(1)} %get-tuple-element.53), channel_id=1, source_target_pairs={{0,16},{16,0},{1,17},{17,1},{2,18},{18,2},{3,19},{19,3},{4,20},{20... | collective-permute-start | bytes 393224 | tf_op jit(solution)/shard_map/ppermute | solution.py:415
  52.1 2.2 %collective-permute-start.9 = (bf16[128,512]{1,0:T(8,128)(2,1)S(1)}, bf16[128,512]{1,0:T(8,128)(2,1)S(1)}, u32[]{:S(2)}, u32[]{:S(2)}) collective-permute-start(bf16[128,512]{1,0:T(8,128)(2,1)S(1)} %get-tuple-element.44.gate_cot_ref), channel_id=1, source_target_pairs={{0,16},{16,0},{1,17},{17,1},{2,18},{18,2},{3,19},{19,3},{4,20},{20... | collective-permute-start | bytes 393224 | tf_op jit(solution)/shard_map/ppermute | solution.py:415
  52.4 1.8 %collective-permute-start.10 = (bf16[128,512]{1,0:T(8,128)(2,1)S(1)}, bf16[128,512]{1,0:T(8,128)(2,1)S(1)}, u32[]{:S(2)}, u32[]{:S(2)}) collective-permute-start(bf16[128,512]{1,0:T(8,128)(2,1)S(1)} %get-tuple-element.45.up_cot_ref), channel_id=1, source_target_pairs={{0,16},{16,0},{1,17},{17,1},{2,18},{18,2},{3,19},{19,3},{4,20},{20... | collective-permute-start | bytes 393224 | tf_op jit(solution)/shard_map/ppermute | solution.py:415

commit v4 on v3

--- a/solution.py
+++ b/solution.py
@@ -10,8 +10,9 @@
 MIB = 1024 * 1024
 SCOPED = 16 * MIB
 ROWS_FIRST = (((0,), (0,)), ((), ()))
-ROWS_LAST = (((1,), (1,)), ((), ()))
 COLS = 512
+ROUTE_COLS = 3584
+COMBINE_COLS = 896
 
 
 def matmul(a, b, dims=(((1,), (0,)), ((), ()))):
@@ -22,8 +23,8 @@
 REMOTE = pl.BlockSpec(memory_space=pl.ANY)
 
 
-def spread(depth):
-    return [pl.ds(j * COLS, COLS) for j in range(depth // COLS)]
+def spread(depth, size=COLS):
+    return [pl.ds(j * size, size) for j in range(depth // size)]
 
 
 def in_hbm(*arrays):
@@ -60,7 +61,7 @@
 def route_kernel(
     cap, ids_hbm, weight_hbm, tok_hbm, cot_hbm, send_ref, ids_ref, weight_ref, tok_ref, cot_ref, small_sems, sems
 ):
-    parts = spread(tok_hbm.shape[1])
+    parts = spread(tok_hbm.shape[1], ROUTE_COLS)
     small = [
         pltpu.make_async_copy(ids_hbm, ids_ref, small_sems.at[0]),
         pltpu.make_async_copy(weight_hbm, weight_ref, small_sems.at[1]),
@@ -101,7 +102,7 @@
             pltpu.VMEM((rows, depth), BF16),
             pltpu.VMEM((rows, depth), BF16),
             pltpu.SemaphoreType.DMA((2,)),
-            pltpu.SemaphoreType.DMA((2, depth // COLS)),
+            pltpu.SemaphoreType.DMA((2, depth // ROUTE_COLS)),
         ],
         compiler_params=pltpu.CompilerParams(vmem_limit_bytes=16 * MIB),
         name="route",
@@ -133,7 +134,7 @@
         lambda *refs: select_kernel(cap, *refs),
         in_specs=[REMOTE] * 2,
         out_specs=REMOTE,
-        out_shape=pltpu.HBM(shape, BF16),
+        out_shape=jax.ShapeDtypeStruct(shape, BF16),
         scratch_shapes=[
             pltpu.VMEM(ids.shape, jnp.int32),
             pltpu.VMEM(weight.shape, F32),
@@ -166,6 +167,22 @@
     )(*in_vmem(rows))
 
 
+def flip_kernel(after_ref, down_ref, flipped_ref):
+    for cols in spread(down_ref.shape[1]):
+        flipped_ref[cols, :] = jnp.transpose(down_ref[:, cols])
+
+
+def flip(after, down):
+    return pl.pallas_call(
+        flip_kernel,
+        in_specs=[REMOTE, WHOLE],
+        out_specs=WHOLE,
+        out_shape=pltpu.VMEM(down.shape[::-1], BF16),
+        compiler_params=pltpu.CompilerParams(vmem_limit_bytes=8 * MIB),
+        name="flip_down",
+    )(*in_vmem(after, down))
+
+
 def split_store(value, own_ref, other_ref, cols):
     half = own_ref.shape[0]
     own_ref[:, cols] = value[:half].astype(BF16)
@@ -173,17 +190,23 @@
 
 
 def forward_kernel(
-    mine_ref, theirs_ref, gate_ref, up_ref, down_ref, own_ref, other_ref, hid_ref, gate_act_ref, up_act_ref
+    mine_ref, theirs_ref, gate_ref, up_ref, down_ref,
+    own_ref, other_ref, hid_ref, gate_act_ref, up_act_ref, gate_flip_ref, up_flip_ref,
 ):
-    rows = jnp.concatenate([mine_ref[...], theirs_ref[...]], axis=0)
-    gate_act = matmul(rows, gate_ref[...])
-    up_act = matmul(rows, up_ref[...])
+    gate_act = jnp.zeros(gate_act_ref.shape, F32)
+    up_act = jnp.zeros(up_act_ref.shape, F32)
+    for cols in spread(mine_ref.shape[1]):
+        rows = jnp.concatenate([mine_ref[:, cols], theirs_ref[:, cols]], axis=0)
+        gate_act = gate_act + matmul(rows, gate_ref[cols, :])
+        up_act = up_act + matmul(rows, up_ref[cols, :])
+        gate_flip_ref[:, cols] = jnp.transpose(gate_ref[cols, :])
     gate_act_ref[...] = gate_act
     up_act_ref[...] = up_act
     hidden = (gate_act * jax.nn.sigmoid(gate_act) * up_act).astype(BF16)
     hid_ref[...] = hidden
     for cols in spread(mine_ref.shape[1]):
         split_store(matmul(hidden, down_ref[:, cols]), own_ref, other_ref, cols)
+        up_flip_ref[:, cols] = jnp.transpose(up_ref[cols, :])
 
 
 def forward(mine, theirs, gate, up, down):
@@ -192,13 +215,15 @@
     return pl.pallas_call(
         forward_kernel,
         in_specs=[WHOLE] * 5,
-        out_specs=[WHOLE] * 5,
+        out_specs=[WHOLE] * 7,
         out_shape=[
             pltpu.VMEM((half, depth), BF16),
             pltpu.VMEM((half, depth), BF16),
             pltpu.VMEM((2 * half, width), BF16),
             pltpu.VMEM((2 * half, width), F32),
             pltpu.VMEM((2 * half, width), F32),
+            pltpu.VMEM((width, depth), BF16),
+            pltpu.VMEM((width, depth), BF16),
         ],
         compiler_params=pltpu.CompilerParams(vmem_limit_bytes=SCOPED),
         name="expert_forward",
@@ -208,8 +233,7 @@
 def row_grads(gate_cot, up_cot, gate_ref, up_ref, own_ref, other_ref, first):
     for j in range(own_ref.shape[1] // COLS):
         cols = pl.ds((first + j) * COLS, COLS)
-        back = matmul(gate_cot, gate_ref[cols, :], ROWS_LAST)
-        back = back + matmul(up_cot, up_ref[cols, :], ROWS_LAST)
+        back = matmul(gate_cot, gate_ref[:, cols]) + matmul(up_cot, up_ref[:, cols])
         split_store(back, own_ref, other_ref, pl.ds(j * COLS, COLS))
 
 
@@ -218,7 +242,7 @@
     own_ref, other_ref, gate_cot_ref, up_cot_ref,
 ):
     rows = jnp.concatenate([mine_ref[...], theirs_ref[...]], axis=0)
-    hidden_cot = matmul(rows, down_ref[...], ROWS_LAST)
+    hidden_cot = matmul(rows, down_ref[...])
     gate_act = gate_act_ref[...]
     sigma = jax.nn.sigmoid(gate_act)
     gate_cot = (hidden_cot * up_act_ref[...] * sigma * (1.0 + gate_act * (1.0 - sigma))).astype(BF16)
@@ -234,7 +258,7 @@
 
 def backward(mine, theirs, gate, up, down, gate_act, up_act):
     half, depth = mine.shape
-    width = gate.shape[1]
+    width = gate.shape[0]
     early = early_cols(depth)
     return pl.pallas_call(
         backward_kernel,
@@ -247,13 +271,13 @@
 
 
 def late_kernel(gate_cot_ref, up_cot_ref, gate_ref, up_ref, own_ref, other_ref):
-    first = (gate_ref.shape[0] - own_ref.shape[1]) // COLS
+    first = (gate_ref.shape[1] - own_ref.shape[1]) // COLS
     row_grads(gate_cot_ref[...], up_cot_ref[...], gate_ref, up_ref, own_ref, other_ref, first)
 
 
 def late_rows(gate_cot, up_cot, gate, up):
     half = gate_cot.shape[0] // 2
-    depth = gate.shape[0]
+    depth = gate.shape[1]
     late = depth - early_cols(depth)
     return pl.pallas_call(
         late_kernel,
@@ -265,39 +289,37 @@
     )(*in_vmem(gate_cot, up_cot, gate, up))
 
 
-def add_kernel(cap, *refs):
-    own_out, arrived_out, own_early, arrived_early, own_late, arrived_late, out_hbm, out_ref, sems = refs
-    early = own_early.shape[1]
+def add_kernel(cap, first, own_out, arrived_out, own_ref, arrived_ref, *refs):
+    out_hbm, out_ref, sems = refs[-3:]
     rows = out_ref.shape[0]
     groups = rows // (2 * cap)
     copies = []
-    for j, cols in enumerate(spread(out_ref.shape[1])):
-        if j * COLS < early:
-            a, b, here = own_early, arrived_early, pl.ds(j * COLS, COLS)
-        else:
-            a, b, here = own_late, arrived_late, pl.ds(j * COLS - early, COLS)
+    for j, here in enumerate(spread(out_ref.shape[1])):
+        cols = pl.ds((first + j) * COLS, COLS)
         out = own_out[:, cols].astype(F32) + arrived_out[:, cols].astype(F32)
-        grad = a[:, here].astype(F32) + b[:, here].astype(F32)
+        grad = own_ref[:, here].astype(F32) + arrived_ref[:, here].astype(F32)
         both = jnp.concatenate([out.reshape(groups, cap, COLS), grad.reshape(groups, cap, COLS)], axis=1)
-        out_ref[:, cols] = both.reshape(rows, COLS).astype(BF16)
-        copy = pltpu.make_async_copy(out_ref.at[:, cols], out_hbm.at[:, cols], sems.at[j])
-        copy.start()
-        copies.append(copy)
+        out_ref[:, here] = both.reshape(rows, COLS).astype(BF16)
+        copies.append(pltpu.make_async_copy(out_ref.at[:, here], out_hbm.at[:, cols], sems.at[j]))
+        copies[j].start()
     for copy in copies:
         copy.wait()
 
 
-def add_rows(cap, *arrays):
-    half, depth = arrays[0].shape
-    return pl.pallas_call(
-        lambda *refs: add_kernel(cap, *refs),
-        in_specs=[WHOLE] * 6,
+def add_rows(cap, first, own_out, arrived_out, own, arrived, filled=None):
+    half, depth = own_out.shape
+    cols = own.shape[1]
+    more = [] if filled is None else in_hbm(filled)
+    return pl.pallas_call(
+        lambda *refs: add_kernel(cap, first, *refs),
+        in_specs=[WHOLE] * 4 + [REMOTE] * len(more),
         out_specs=REMOTE,
         out_shape=pltpu.HBM((2 * half, depth), BF16),
-        scratch_shapes=[pltpu.VMEM((2 * half, depth), BF16), pltpu.SemaphoreType.DMA((depth // COLS,))],
+        scratch_shapes=[pltpu.VMEM((2 * half, cols), BF16), pltpu.SemaphoreType.DMA((cols // COLS,))],
+        input_output_aliases={4: 0} if more else {},
         compiler_params=pltpu.CompilerParams(vmem_limit_bytes=16 * MIB),
-        name="add_rows",
-    )(*in_vmem(*arrays))
+        name="add_late" if more else "add_early",
+    )(*in_vmem(own_out, arrived_out, own, arrived), *more)
 
 
 def grads_kernel(
@@ -336,13 +358,10 @@
     )(*in_vmem(tok_mine, tok_theirs, cot_mine, cot_theirs, hidden, gate_cot, up_cot))
 
 
-def combine_kernel(back_ref, select_hbm, out_hbm, grad_hbm, select_ref, out_ref, grad_ref, select_sem, sems):
-    load_select = pltpu.make_async_copy(select_hbm, select_ref, select_sem)
-    load_select.start()
-    load_select.wait()
+def combine_kernel(back_ref, select_ref, out_hbm, grad_hbm, out_ref, grad_ref, sems):
     count = out_ref.shape[0]
     copies = []
-    for j, cols in enumerate(spread(back_ref.shape[1])):
+    for j, cols in enumerate(spread(back_ref.shape[1], COMBINE_COLS)):
         sums = matmul(select_ref[...], back_ref[:, cols])
         out_ref[:, cols] = (sums[:count] + sums[count : 2 * count]).astype(BF16)
         grad_ref[:, cols] = sums[2 * count :].astype(BF16)
@@ -362,19 +381,17 @@
     rows = select.shape[0] // 3
     return pl.pallas_call(
         combine_kernel,
-        in_specs=[WHOLE, REMOTE],
+        in_specs=[WHOLE, WHOLE],
         out_specs=[REMOTE, REMOTE],
         out_shape=[pltpu.HBM((rows, depth), BF16)] * 2,
         scratch_shapes=[
-            pltpu.VMEM(select.shape, BF16),
             pltpu.VMEM((rows, depth), BF16),
             pltpu.VMEM((rows, depth), BF16),
-            pltpu.SemaphoreType.DMA,
-            pltpu.SemaphoreType.DMA((2, depth // COLS)),
+            pltpu.SemaphoreType.DMA((2, depth // COMBINE_COLS)),
         ],
         compiler_params=pltpu.CompilerParams(vmem_limit_bytes=8 * MIB),
         name="combine",
-    )(*in_vmem(back), *in_hbm(select))
+    )(*in_vmem(back), select)
 
 
 def per_device(tokens, cotangent, expert_ids, route_weight, gate_weight, up_weight, down_weight):
@@ -400,18 +417,21 @@
     ]
     tok_mine, cot_mine = compact(exchange(send), cap)
     tok_theirs, _ = swapped(tok_mine)
-    cot_theirs, tok_theirs = swapped(cot_mine, tok_theirs)
-    own_out, other_out, hidden, gate_act, up_act = forward(tok_mine, tok_theirs, gate, up, down)
+    down_flip = flip(tok_mine, down)
+    cot_theirs, (tok_theirs, down_flip) = swapped(cot_mine, (tok_theirs, down_flip))
+    own_out, other_out, hidden, gate_act, up_act, gate_flip, up_flip = forward(
+        tok_mine, tok_theirs, gate, up, down
+    )
     arrived_out, cot_theirs = swapped(other_out, cot_theirs)
     own_early, other_early, gate_cot, up_cot = backward(
-        cot_mine, cot_theirs, gate, up, down, gate_act, up_act
-    )
-    arrived_early, arrived_out = swapped(other_early, arrived_out)
-    own_late, other_late = late_rows(gate_cot, up_cot, gate, up)
-    arrived_late, arrived_early = swapped(other_late, arrived_early)
-    back = exchange(
-        add_rows(cap, own_out, arrived_out, own_early, arrived_early, own_late, arrived_late)
-    )
+        cot_mine, cot_theirs, gate_flip, up_flip, down_flip, gate_act, up_act
+    )
+    arrived_early, _ = swapped(other_early)
+    own_late, other_late = late_rows(gate_cot, up_cot, gate_flip, up_flip)
+    arrived_late, _ = swapped(other_late)
+    sums = add_rows(cap, 0, own_out, arrived_out, own_early, arrived_early)
+    sums = add_rows(cap, own_early.shape[1] // COLS, own_out, arrived_out, own_late, arrived_late, sums)
+    back = exchange(sums)
     hidden, gate_cot, up_cot = [lax.ppermute(a, "edp", swap) for a in (hidden, gate_cot, up_cot)]
     grad_gate, grad_up, grad_down = grads(
         tok_theirs, tok_mine, cot_theirs, cot_mine, hidden, gate_cot, up_cot

time: 77.1 us -> 73.3 us (0.951)
  Pallas kernels: 20.5 us -> 18 us
  waiting for transfers between devices: 16.9 us -> 15.4 us
    ppermute x5, waiting for transfers between devices: 3.31 us -> 1.18 us  [swapped(): return (lax.ppermute(rows, 'edp', swap), after)]
    pallas_call x1, Pallas kernels: 2.7 us -> 1.33 us  [backward(): pl.pallas_call(backward_kernel, in_specs=[WHOLE] * 7, out_specs=[WHOLE] *...]
    pallas_call x1, Pallas kernels: 3.08 us -> 1.94 us  [route(): pl.pallas_call(lambda *refs: route_kernel(cap, *refs), in_specs=[REMOTE]...]
    pallas_call x2 -> x4, Pallas kernels: 3.65 us -> 4.44 us  [the longest x2 1.77 us: add_rows(): pl.pallas_call(lambda *refs: add_kernel(cap, first, *refs), in_specs=[WHO...]
  transfers between devices with their start and end apart: 12 -> 12, of which waited for: 4 -> 4; matrix products, arithmetic and copies ran while one was open for 0% -> 0% of each run, Pallas kernels for 22% -> 21%
where the time goes in v4:
time: 73.3 us; the launch traced here: 73 us
  blocking collectives  32.2 us (44%)
  Pallas kernels  18 us (25%)
  waiting for transfers between devices  15.4 us (21%)
  starting transfers between devices  6.68 us (9%)
  between operations  0.77 us (1%)
    all_to_all x1, blocking collectives, exchange(): lax.all_to_all(blocks, 'ep', split_axis=0, concat_axis=0, tiled=True)  32.2 us
    all_to_all x1, waiting for transfers between devices, exchange(): lax.all_to_all(blocks, 'ep', split_axis=0, concat_axis=0, tiled=True)  14.1 us
    pallas_call x1, Pallas kernels, grads(): pl.pallas_call(grads_kernel, grid=(depth // COLS,), in_specs=[WHOLE] * 7,...  6.33 us
    all_to_all x1, starting transfers between devices, exchange(): lax.all_to_all(blocks, 'ep', split_axis=0, concat_axis=0, tiled=True)  3.66 us
    pallas_call x1, Pallas kernels, forward(): pl.pallas_call(forward_kernel, in_specs=[WHOLE] * 5, out_specs=[WHOLE] *...  2.06 us
    pallas_call x1, Pallas kernels, route(): pl.pallas_call(lambda *refs: route_kernel(cap, *refs), in_specs=[REMOTE]...  1.94 us
    pallas_call x2, Pallas kernels, add_rows(): pl.pallas_call(lambda *refs: add_kernel(cap, first, *refs), in_specs=[WHO...  1.77 us
    pallas_call x1, Pallas kernels, combine(): pl.pallas_call(combine_kernel, in_specs=[WHOLE, WHOLE], out_specs=[REMOTE...  1.68 us
  transfers between devices with their start and end apart: 12, of which 4 were waited for; matrix products, arithmetic and copies ran while one was open for 0% of the time, Pallas kernels for 21%

profile of v4, /device:TPU:0, one launch (start us, length us, event | category | flops | bytes accessed | tf_op | source)
XLA Modules:
  0.0 73.0 jit_solution(17501699742325937506)
XLA Ops:
  0.6 0.5 collective-permute-start.1
  1.2 0.1 collective-permute-start.2
  1.2 0.4 collective-permute-start.3
  1.7 1.9 %route.1 = bf16[128,3584]{1,0:T(8,128)(2,1)S(1)} custom-call(s32[8,128]{1,0:T(8,128)} %bitcast.16, f32[8,128]{1,0:T(8,128)} %bitcast.18, bf16[128,3584]{1,0:T(8,128)(2,1)} %refs_2_.1, bf16[128,3584]{1,0:T(8,128)(2,1)} %refs_3_.1), custom_call_target="tpu_custom_call" | custom-call | tf_op jit(solution)/shard_map/route/pallas_call | solution.py:94
  3.6 32.2 %all_to_all.10 = bf16[16,8,3584]{2,1,0:T(8,128)(2,1)S(1)} all-to-all(bf16[16,8,3584]{2,1,0:T(8,128)(2,1)S(1)} %bitcast.14), channel_id=1, replica_groups=mesh['edp'=2,'ep'=16] {'ep'}, dimensions={0} | all-to-all | bytes 1835008 | tf_op jit(solution)/shard_map/all_to_all | solution.py:408
  35.8 0.2 compact.1
  36.0 0.1 collective-permute-start
  36.0 0.0 collective-permute-done.1.down_ref
  36.1 1.0 %flip_down.1.down_ref = bf16[3584,512]{1,0:T(8,128)(2,1)S(1)} custom-call(bf16[64,3584]{1,0:T(8,128)(2,1)S(1)} %get-tuple-element.30.after_ref.mine_ref.tok_theirs, bf16[512,3584]{1,0:T(8,128)(2,1)S(1)} %collective-permute-done.1.down_ref), custom_call_target="tpu_custom_call" | custom-call | tf_op jit(solution)/shard_map/flip_down/pallas_call | solution.py:176
  37.1 0.8 %collective-permute-done.theirs_ref.tok_mine = bf16[64,3584]{1,0:T(8,128)(2,1)S(1)} collective-permute-done((bf16[64,3584]{1,0:T(8,128)(2,1)S(1)}, bf16[64,3584]{1,0:T(8,128)(2,1)S(1)}, u32[]{:S(2)}, u32[]{:S(2)}) %collective-permute-start) | collective-permute-done | bytes 458784 | tf_op jit(solution)/shard_map/ppermute | solution.py:413
  37.8 0.1 collective-permute-start.4
  38.0 0.0 collective-permute-done.2.gate_ref
  38.0 0.0 collective-permute-done.3.up_ref
  38.0 2.1 %expert_forward.1 = (bf16[64,3584]{1,0:T(8,128)(2,1)S(1)}, bf16[64,3584]{1,0:T(8,128)(2,1)S(1)}, bf16[128,512]{1,0:T(8,128)(2,1)S(1)}, f32[128,512]{1,0:T(8,128)...) custom-call(bf16[64,3584]{1,0:T(8,128)(2,1)S(1)} %get-tuple-element.30.after_ref.mine_ref, ...), custom_call_target="tpu_custom_call" | custom-call | tf_op jit(solution)/shard_map/expert_forward/pallas_call | solution.py:215
  40.1 0.0 collective-permute-done.4.theirs_ref.cot_mine
  40.1 0.4 collective-permute-start.5
  40.5 1.3 %expert_backward.1 = (bf16[64,2048]{1,0:T(8,128)(2,1)S(1)}, bf16[64,2048]{1,0:T(8,128)(2,1)S(1)}, bf16[128,512]{1,0:T(8,128)(2,1)S(1)}, bf16[128,512]{1,0:T(8,128)(2,1)S(1)}) custom-call(bf16[64,3584]{1,0:T(8,128)(2,1)S(1)} %get-tuple-element.35.mine_ref.cot_theirs, bf16[64,3584]{1,0:T(8,128)(2,1)S(1)} %collective-permute-done.4.theirs_ref.cot_mine, ...), custom_call_target="tpu_custom_call" | custom-call | tf_op jit(solution)/shard_map/expert_backward/pallas_call | solution.py:263
  41.9 0.2 collective-permute-start.7
  42.0 0.6 late_rows.1
  42.6 0.4 collective-permute-start.6
  43.1 0.4 collective-permute-done.7.refs_3_
  43.5 0.0 collective-permute-done.5.refs_1_
  43.5 0.9 %add_early.1.refs_4_ = bf16[128,3584]{1,0:T(8,128)(2,1)} custom-call(bf16[64,3584]{1,0:T(8,128)(2,1)S(1)} %get-tuple-element.33.refs_0_, bf16[64,3584]{1,0:T(8,128)(2,1)S(1)} %collective-permute-done.5.refs_1_, bf16[64,2048]{1,0:T(8,128)(2,1)S(1)} %get-tuple-element.47.refs_2_, bf16[64,2048]{1,0:T(8,128)(2,1)S(1)} %collective-permute-done.7.refs_3_), custom_call_target="tpu_custom_call" | custom-call | tf_op jit(solution)/shard_map/add_early/pallas_call | solution.py:313
  44.4 0.0 collective-permute-done.6.refs_3_
  44.4 0.9 %add_late.1 = bf16[128,3584]{1,0:T(8,128)(2,1)} custom-call(bf16[64,3584]{1,0:T(8,128)(2,1)S(1)} %get-tuple-element.33.refs_0_, bf16[64,3584]{1,0:T(8,128)(2,1)S(1)} %collective-permute-done.5.refs_1_, bf16[64,1536]{1,0:T(8,128)(2,1)S(1)} %get-tuple-element.45.refs_2_, ...), custom_call_target="tpu_custom_call", output_to_operand_aliasing={{}: (4, {})} | custom-call | tf_op jit(solution)/shard_map/add_late/pallas_call | solution.py:313
  45.2 3.7 %all-to-all-start.1 = ((bf16[16,8,3584]{2,1,0:T(8,128)(2,1)}), bf16[16,8,3584]{2,1,0:T(8,128)(2,1)S(1)}, u32[]{:S(2)}, u32[]{:S(2)}) async-start(bf16[16,8,3584]{2,1,0:T(8,128)(2,1)} %bitcast.15), calls=%async_computation.1 | async-start | bytes 1835008 | tf_op jit(solution)/shard_map/all_to_all | solution.py:408
  48.9 0.2 collective-permute-start.8
  49.1 0.4 collective-permute-start.10
  49.5 0.1 collective-permute-start.9
  49.6 1.1 %selectors.1.select_ref = bf16[384,128]{1,0:T(8,128)(2,1)S(1)} custom-call(s32[8,128]{1,0:T(8,128)} %bitcast.17, f32[8,128]{1,0:T(8,128)} %bitcast.19), custom_call_target="tpu_custom_call" | custom-call | tf_op jit(solution)/shard_map/selectors/pallas_call | solution.py:133
  50.7 0.0 collective-permute-done.8.hid_ref
  50.7 0.0 collective-permute-done.10.up_cot_ref
  50.8 0.1 collective-permute-done.9.gate_cot_ref
  50.8 6.3 %weight_grads.1 = (bf16[3584,512]{1,0:T(8,128)(2,1)}, bf16[3584,512]{1,0:T(8,128)(2,1)}, bf16[512,3584]{1,0:T(8,128)(2,1)}) custom-call(bf16[64,3584]{1,0:T(8,128)(2,1)S(1)} %collective-permute-done.theirs_ref.tok_mine, bf16[64,3584]{1,0:T(8,128)(2,1)S(1)} %get-tuple-element.30.after_ref.mine_ref.tok_theirs, ...), custom_call_target="tpu_custom_call" | custom-call | tf_op jit(solution)/shard_map/weight_grads/pallas_call | solution.py:342
  57.2 14.1 %all-to-all-done.1 = bf16[16,8,3584]{2,1,0:T(8,128)(2,1)S(1)} async-done(((bf16[16,8,3584]{2,1,0:T(8,128)(2,1)}), bf16[16,8,3584]{2,1,0:T(8,128)(2,1)S(1)}, u32[]{:S(2)}, u32[]{:S(2)}) %all-to-all-start.1) | async-done | bytes 917536 | tf_op jit(solution)/shard_map/all_to_all | solution.py:408
  71.3 1.7 %combine.1 = (bf16[128,3584]{1,0:T(8,128)(2,1)}, bf16[128,3584]{1,0:T(8,128)(2,1)}) custom-call(bf16[128,3584]{1,0:T(8,128)(2,1)S(1)} %bitcast.13, bf16[384,128]{1,0:T(8,128)(2,1)S(1)} %selectors.1.select_ref), custom_call_target="tpu_custom_call" | custom-call | tf_op jit(solution)/shard_map/combine/pallas_call | solution.py:382
Async XLA Ops:
  0.6 35.4 %collective-permute-start.1 = (bf16[512,3584]{1,0:T(8,128)(2,1)}, bf16[512,3584]{1,0:T(8,128)(2,1)S(1)}, u32[]{:S(2)}, u32[]{:S(2)}) collective-permute-start(bf16[512,3584]{1,0:T(8,128)(2,1)} %bitcast.20), channel_id=1, source_target_pairs={{0,16},{16,0},{1,17},{17,1},{2,18},{18,2},{3,19},{19,3},{4,20},{20... | collective-permute-start | bytes 11010056 | tf_op jit(solution)/shard_map/ppermute | solution.py:416
  1.2 36.8 %collective-permute-start.2 = (bf16[3584,512]{1,0:T(8,128)(2,1)}, bf16[3584,512]{1,0:T(8,128)(2,1)S(1)}, u32[]{:S(2)}, u32[]{:S(2)}) collective-permute-start(bf16[3584,512]{1,0:T(8,128)(2,1)} %bitcast.21), channel_id=1, source_target_pairs={{0,16},{16,0},{1,17},{17,1},{2,18},{18,2},{3,19},{19,3},{4,20},{20... | collective-permute-start | bytes 11010056 | tf_op jit(solution)/shard_map/ppermute | solution.py:416
  1.2 36.8 %collective-permute-start.3 = (bf16[3584,512]{1,0:T(8,128)(2,1)}, bf16[3584,512]{1,0:T(8,128)(2,1)S(1)}, u32[]{:S(2)}, u32[]{:S(2)}) collective-permute-start(bf16[3584,512]{1,0:T(8,128)(2,1)} %bitcast.22), channel_id=1, source_target_pairs={{0,16},{16,0},{1,17},{17,1},{2,18},{18,2},{3,19},{19,3},{4,20},{20... | collective-permute-start | bytes 11010056 | tf_op jit(solution)/shard_map/ppermute | solution.py:416
  36.0 1.9 %collective-permute-start = (bf16[64,3584]{1,0:T(8,128)(2,1)S(1)}, bf16[64,3584]{1,0:T(8,128)(2,1)S(1)}, u32[]{:S(2)}, u32[]{:S(2)}) collective-permute-start(bf16[64,3584]{1,0:T(8,128)(2,1)S(1)} %get-tuple-element.30.after_ref.mine_ref.tok_theirs), channel_id=1, source_target_pairs={{0,16},{16,0},{1,17},{17,1},{2,18},{18,2},{3,19},{19,3},{4,20},{20... | collective-permute-start | bytes 1376264 | tf_op jit(solution)/shard_map/ppermute | solution.py:413
  37.8 2.2 %collective-permute-start.4 = (bf16[64,3584]{1,0:T(8,128)(2,1)S(1)}, bf16[64,3584]{1,0:T(8,128)(2,1)S(1)}, u32[]{:S(2)}, u32[]{:S(2)}) collective-permute-start(bf16[64,3584]{1,0:T(8,128)(2,1)S(1)} %get-tuple-element.35.mine_ref.cot_theirs), channel_id=1, source_target_pairs={{0,16},{16,0},{1,17},{17,1},{2,18},{18,2},{3,19},{19,3},{4,20},{20... | collective-permute-start | bytes 1376264 | tf_op jit(solution)/shard_map/ppermute | solution.py:413
  40.1 3.4 %collective-permute-start.5 = (bf16[64,3584]{1,0:T(8,128)(2,1)S(1)}, bf16[64,3584]{1,0:T(8,128)(2,1)S(1)}, u32[]{:S(2)}, u32[]{:S(2)}) collective-permute-start(bf16[64,3584]{1,0:T(8,128)(2,1)S(1)} %get-tuple-element.36), channel_id=1, source_target_pairs={{0,16},{16,0},{1,17},{17,1},{2,18},{18,2},{3,19},{19,3},{4,20},{20... | collective-permute-start | bytes 1376264 | tf_op jit(solution)/shard_map/ppermute | solution.py:413
  41.9 1.6 %collective-permute-start.7 = (bf16[64,2048]{1,0:T(8,128)(2,1)S(1)}, bf16[64,2048]{1,0:T(8,128)(2,1)S(1)}, u32[]{:S(2)}, u32[]{:S(2)}) collective-permute-start(bf16[64,2048]{1,0:T(8,128)(2,1)S(1)} %get-tuple-element.48), channel_id=1, source_target_pairs={{0,16},{16,0},{1,17},{17,1},{2,18},{18,2},{3,19},{19,3},{4,20},{20... | collective-permute-start | bytes 786440 | tf_op jit(solution)/shard_map/ppermute | solution.py:413
  42.6 1.8 %collective-permute-start.6 = (bf16[64,1536]{1,0:T(8,128)(2,1)S(1)}, bf16[64,1536]{1,0:T(8,128)(2,1)S(1)}, u32[]{:S(2)}, u32[]{:S(2)}) collective-permute-start(bf16[64,1536]{1,0:T(8,128)(2,1)S(1)} %get-tuple-element.46), channel_id=1, source_target_pairs={{0,16},{16,0},{1,17},{17,1},{2,18},{18,2},{3,19},{19,3},{4,20},{20... | collective-permute-start | bytes 589832 | tf_op jit(solution)/shard_map/ppermute | solution.py:413
  45.2 26.0 %all-to-all-start.1 = ((bf16[16,8,3584]{2,1,0:T(8,128)(2,1)}), bf16[16,8,3584]{2,1,0:T(8,128)(2,1)S(1)}, u32[]{:S(2)}, u32[]{:S(2)}) async-start(bf16[16,8,3584]{2,1,0:T(8,128)(2,1)} %bitcast.15), calls=%async_computation.1 | async-start | bytes 1835008 | tf_op jit(solution)/shard_map/all_to_all | solution.py:408
  48.9 1.8 %collective-permute-start.8 = (bf16[128,512]{1,0:T(8,128)(2,1)S(1)}, bf16[128,512]{1,0:T(8,128)(2,1)S(1)}, u32[]{:S(2)}, u32[]{:S(2)}) collective-permute-start(bf16[128,512]{1,0:T(8,128)(2,1)S(1)} %get-tuple-element.51), channel_id=1, source_target_pairs={{0,16},{16,0},{1,17},{17,1},{2,18},{18,2},{3,19},{19,3},{4,20},{20... | collective-permute-start | bytes 393224 | tf_op jit(solution)/shard_map/ppermute | solution.py:435
  49.1 1.6 %collective-permute-start.10 = (bf16[128,512]{1,0:T(8,128)(2,1)S(1)}, bf16[128,512]{1,0:T(8,128)(2,1)S(1)}, u32[]{:S(2)}, u32[]{:S(2)}) collective-permute-start(bf16[128,512]{1,0:T(8,128)(2,1)S(1)} %get-tuple-element.44.up_cot_ref), channel_id=1, source_target_pairs={{0,16},{16,0},{1,17},{17,1},{2,18},{18,2},{3,19},{19,3},{4,20},{20... | collective-permute-start | bytes 393224 | tf_op jit(solution)/shard_map/ppermute | solution.py:435
  49.5 1.3 %collective-permute-start.9 = (bf16[128,512]{1,0:T(8,128)(2,1)S(1)}, bf16[128,512]{1,0:T(8,128)(2,1)S(1)}, u32[]{:S(2)}, u32[]{:S(2)}) collective-permute-start(bf16[128,512]{1,0:T(8,128)(2,1)S(1)} %get-tuple-element.43.gate_cot_ref), channel_id=1, source_target_pairs={{0,16},{16,0},{1,17},{17,1},{2,18},{18,2},{3,19},{19,3},{4,20},{20... | collective-permute-start | bytes 393224 | tf_op jit(solution)/shard_map/ppermute | solution.py:435

commit v5 on v4

--- a/solution.py
+++ b/solution.py
@@ -35,10 +35,14 @@
     return [pltpu.with_memory_space_constraint(a, pltpu.VMEM) for a in arrays]
 
 
+def far_corner(experts):
+    return experts // 2 + experts // 8
+
+
 def slots(cap, width, ids_ref, weight_ref, waits):
     tokens = ids_ref.shape[1]
     slot = lax.broadcasted_iota(jnp.int32, (width, tokens), 0)
-    expert = slot // (2 * cap)
+    expert = (slot // (2 * cap)) ^ (lax.axis_index("edp") * far_corner(width // (2 * cap)))
     place = slot % (2 * cap)
     before = lax.broadcasted_iota(jnp.int32, (tokens, tokens), 0) < lax.broadcasted_iota(
         jnp.int32, (tokens, tokens), 1
@@ -403,9 +407,13 @@
     send = route(ids, weight, tokens, cotangent, experts, cap)
     select = selectors(ids, weight, experts, cap)
 
+    orders = [list(range(experts)), [experts + (i ^ far_corner(experts)) for i in range(experts)]]
+
     def exchange(rows):
         blocks = rows.reshape(experts, 2 * cap, depth)
-        return lax.all_to_all(blocks, "ep", split_axis=0, concat_axis=0, tiled=True).reshape(rows.shape)
+        return lax.all_to_all(
+            blocks, ("edp", "ep"), split_axis=0, concat_axis=0, tiled=True, axis_index_groups=orders
+        ).reshape(rows.shape)
 
     def swapped(rows, after=None):
         if after is not None:

time: 73.3 us -> 70.1 us (0.956)
  blocking collectives: 32.2 us -> 29.5 us
  waiting for transfers between devices: 15.4 us -> 12.7 us
  starting transfers between devices: 6.68 us -> 8.76 us
    all_to_all x1, blocking collectives: 32.2 us -> 29.5 us  [exchange(): lax.all_to_all(blocks, ('edp', 'ep'), split_axis=0, concat_axis=0, tiled=...]
    all_to_all x1, waiting for transfers between devices: 14.1 us -> 11.5 us  [exchange(): lax.all_to_all(blocks, ('edp', 'ep'), split_axis=0, concat_axis=0, tiled=...]
    all_to_all x1, starting transfers between devices: 3.66 us -> 5.41 us  [exchange(): lax.all_to_all(blocks, ('edp', 'ep'), split_axis=0, concat_axis=0, tiled=...]
  transfers between devices with their start and end apart: 12 -> 12, of which waited for: 4 -> 3; matrix products, arithmetic and copies ran while one was open for 0% -> 0% of each run, Pallas kernels for 21% -> 22%
where the time goes in v5:
time: 70.1 us; the launch traced here: 69.8 us
  blocking collectives  29.5 us (42%)
  Pallas kernels  18 us (26%)
  waiting for transfers between devices  12.7 us (18%)
  starting transfers between devices  8.76 us (12%)
  between operations  0.77 us (1%)
    all_to_all x1, blocking collectives, exchange(): lax.all_to_all(blocks, ('edp', 'ep'), split_axis=0, concat_axis=0, tiled=...  29.5 us
    all_to_all x1, waiting for transfers between devices, exchange(): lax.all_to_all(blocks, ('edp', 'ep'), split_axis=0, concat_axis=0, tiled=...  11.5 us
    pallas_call x1, Pallas kernels, grads(): pl.pallas_call(grads_kernel, grid=(depth // COLS,), in_specs=[WHOLE] * 7,...  6.35 us
    all_to_all x1, starting transfers between devices, exchange(): lax.all_to_all(blocks, ('edp', 'ep'), split_axis=0, concat_axis=0, tiled=...  5.41 us
    pallas_call x1, Pallas kernels, forward(): pl.pallas_call(forward_kernel, in_specs=[WHOLE] * 5, out_specs=[WHOLE] *...  2.06 us
    pallas_call x1, Pallas kernels, route(): pl.pallas_call(lambda *refs: route_kernel(cap, *refs), in_specs=[REMOTE]...  1.94 us
    pallas_call x2, Pallas kernels, add_rows(): pl.pallas_call(lambda *refs: add_kernel(cap, first, *refs), in_specs=[WHO...  1.77 us
    pallas_call x1, Pallas kernels, combine(): pl.pallas_call(combine_kernel, in_specs=[WHOLE, WHOLE], out_specs=[REMOTE...  1.68 us
  transfers between devices with their start and end apart: 12, of which 3 were waited for; matrix products, arithmetic and copies ran while one was open for 0% of the time, Pallas kernels for 22%

profile of v5, /device:TPU:0, one launch (start us, length us, event | category | flops | bytes accessed | tf_op | source)
XLA Modules:
  0.0 69.8 jit_solution(17582431594083157509)
XLA Ops:
  0.6 0.5 collective-permute-start.1
  1.2 0.1 collective-permute-start.2
  1.2 0.4 collective-permute-start.3
  1.7 1.9 %route.1 = bf16[128,3584]{1,0:T(8,128)(2,1)S(1)} custom-call(s32[8,128]{1,0:T(8,128)} %bitcast.16, f32[8,128]{1,0:T(8,128)} %bitcast.18, bf16[128,3584]{1,0:T(8,128)(2,1)} %refs_2_.1, bf16[128,3584]{1,0:T(8,128)(2,1)} %refs_3_.1), custom_call_target="tpu_custom_call" | custom-call | tf_op jit(solution)/shard_map/route/pallas_call | solution.py:98
  3.6 29.5 %all_to_all.10 = bf16[16,8,3584]{2,1,0:T(8,128)(2,1)S(1)} all-to-all(bf16[16,8,3584]{2,1,0:T(8,128)(2,1)S(1)} %bitcast.14), channel_id=1, replica_groups={{0,1,2,3,4,5,6,7,8,9,10,11,12,13,14,15},{26,27,24,25,30,31,28,29,18,19,..., dimensions={0} | all-to-all | bytes 1835008 | tf_op jit(solution)/shard_map/all_to_all | solution.py:414
  33.1 0.2 compact.1
  33.3 0.1 collective-permute-start
  33.4 0.0 collective-permute-done.1.down_ref
  33.4 1.0 %flip_down.1.down_ref = bf16[3584,512]{1,0:T(8,128)(2,1)S(1)} custom-call(bf16[64,3584]{1,0:T(8,128)(2,1)S(1)} %get-tuple-element.30.after_ref.mine_ref.tok_theirs, bf16[512,3584]{1,0:T(8,128)(2,1)S(1)} %collective-permute-done.1.down_ref), custom_call_target="tpu_custom_call" | custom-call | tf_op jit(solution)/shard_map/flip_down/pallas_call | solution.py:180
  34.4 0.8 %collective-permute-done.theirs_ref.tok_mine = bf16[64,3584]{1,0:T(8,128)(2,1)S(1)} collective-permute-done((bf16[64,3584]{1,0:T(8,128)(2,1)S(1)}, bf16[64,3584]{1,0:T(8,128)(2,1)S(1)}, u32[]{:S(2)}, u32[]{:S(2)}) %collective-permute-start) | collective-permute-done | bytes 458784 | tf_op jit(solution)/shard_map/ppermute | solution.py:421
  35.2 0.1 collective-permute-start.4
  35.3 0.0 collective-permute-done.2.gate_ref
  35.3 0.0 collective-permute-done.3.up_ref
  35.3 2.1 %expert_forward.1 = (bf16[64,3584]{1,0:T(8,128)(2,1)S(1)}, bf16[64,3584]{1,0:T(8,128)(2,1)S(1)}, bf16[128,512]{1,0:T(8,128)(2,1)S(1)}, f32[128,512]{1,0:T(8,128)...) custom-call(bf16[64,3584]{1,0:T(8,128)(2,1)S(1)} %get-tuple-element.30.after_ref.mine_ref, ...), custom_call_target="tpu_custom_call" | custom-call | tf_op jit(solution)/shard_map/expert_forward/pallas_call | solution.py:219
  37.4 0.0 collective-permute-done.4.theirs_ref.cot_mine
  37.4 0.4 collective-permute-start.5
  37.9 1.3 %expert_backward.1 = (bf16[64,2048]{1,0:T(8,128)(2,1)S(1)}, bf16[64,2048]{1,0:T(8,128)(2,1)S(1)}, bf16[128,512]{1,0:T(8,128)(2,1)S(1)}, bf16[128,512]{1,0:T(8,128)(2,1)S(1)}) custom-call(bf16[64,3584]{1,0:T(8,128)(2,1)S(1)} %get-tuple-element.35.mine_ref.cot_theirs, bf16[64,3584]{1,0:T(8,128)(2,1)S(1)} %collective-permute-done.4.theirs_ref.cot_mine, ...), custom_call_target="tpu_custom_call" | custom-call | tf_op jit(solution)/shard_map/expert_backward/pallas_call | solution.py:267
  39.2 0.2 collective-permute-start.7
  39.4 0.6 late_rows.1
  40.0 0.4 collective-permute-start.6
  40.4 0.4 collective-permute-done.7.refs_3_
  40.8 0.0 collective-permute-done.5.refs_1_
  40.8 0.9 %add_early.1.refs_4_ = bf16[128,3584]{1,0:T(8,128)(2,1)} custom-call(bf16[64,3584]{1,0:T(8,128)(2,1)S(1)} %get-tuple-element.33.refs_0_, bf16[64,3584]{1,0:T(8,128)(2,1)S(1)} %collective-permute-done.5.refs_1_, bf16[64,2048]{1,0:T(8,128)(2,1)S(1)} %get-tuple-element.47.refs_2_, bf16[64,2048]{1,0:T(8,128)(2,1)S(1)} %collective-permute-done.7.refs_3_), custom_call_target="tpu_custom_call" | custom-call | tf_op jit(solution)/shard_map/add_early/pallas_call | solution.py:317
  41.7 0.0 collective-permute-done.6.refs_3_
  41.7 0.9 %add_late.1 = bf16[128,3584]{1,0:T(8,128)(2,1)} custom-call(bf16[64,3584]{1,0:T(8,128)(2,1)S(1)} %get-tuple-element.33.refs_0_, bf16[64,3584]{1,0:T(8,128)(2,1)S(1)} %collective-permute-done.5.refs_1_, bf16[64,1536]{1,0:T(8,128)(2,1)S(1)} %get-tuple-element.45.refs_2_, ...), custom_call_target="tpu_custom_call", output_to_operand_aliasing={{}: (4, {})} | custom-call | tf_op jit(solution)/shard_map/add_late/pallas_call | solution.py:317
  42.6 5.4 %all-to-all-start.1 = ((bf16[16,8,3584]{2,1,0:T(8,128)(2,1)}), bf16[16,8,3584]{2,1,0:T(8,128)(2,1)S(1)}, u32[]{:S(2)}, u32[]{:S(2)}) async-start(bf16[16,8,3584]{2,1,0:T(8,128)(2,1)} %bitcast.15), calls=%async_computation.1 | async-start | bytes 1835008 | tf_op jit(solution)/shard_map/all_to_all | solution.py:414
  48.0 0.5 collective-permute-start.8
  48.5 0.1 collective-permute-start.10
  48.6 0.4 collective-permute-start.9
  49.0 1.1 %selectors.1.select_ref = bf16[384,128]{1,0:T(8,128)(2,1)S(1)} custom-call(s32[8,128]{1,0:T(8,128)} %bitcast.17, f32[8,128]{1,0:T(8,128)} %bitcast.19), custom_call_target="tpu_custom_call" | custom-call | tf_op jit(solution)/shard_map/selectors/pallas_call | solution.py:137
  50.2 0.0 collective-permute-done.8.hid_ref
  50.2 0.0 collective-permute-done.10.up_cot_ref
  50.2 0.0 collective-permute-done.9.gate_cot_ref
  50.2 6.4 %weight_grads.1 = (bf16[3584,512]{1,0:T(8,128)(2,1)}, bf16[3584,512]{1,0:T(8,128)(2,1)}, bf16[512,3584]{1,0:T(8,128)(2,1)}) custom-call(bf16[64,3584]{1,0:T(8,128)(2,1)S(1)} %collective-permute-done.theirs_ref.tok_mine, bf16[64,3584]{1,0:T(8,128)(2,1)S(1)} %get-tuple-element.30.after_ref.mine_ref.tok_theirs, ...), custom_call_target="tpu_custom_call" | custom-call | tf_op jit(solution)/shard_map/weight_grads/pallas_call | solution.py:346
  56.5 11.5 %all-to-all-done.1 = bf16[16,8,3584]{2,1,0:T(8,128)(2,1)S(1)} async-done(((bf16[16,8,3584]{2,1,0:T(8,128)(2,1)}), bf16[16,8,3584]{2,1,0:T(8,128)(2,1)S(1)}, u32[]{:S(2)}, u32[]{:S(2)}) %all-to-all-start.1) | async-done | bytes 917536 | tf_op jit(solution)/shard_map/all_to_all | solution.py:414
  68.1 1.7 %combine.1 = (bf16[128,3584]{1,0:T(8,128)(2,1)}, bf16[128,3584]{1,0:T(8,128)(2,1)}) custom-call(bf16[128,3584]{1,0:T(8,128)(2,1)S(1)} %bitcast.13, bf16[384,128]{1,0:T(8,128)(2,1)S(1)} %selectors.1.select_ref), custom_call_target="tpu_custom_call" | custom-call | tf_op jit(solution)/shard_map/combine/pallas_call | solution.py:386
Async XLA Ops:
  0.6 32.8 %collective-permute-start.1 = (bf16[512,3584]{1,0:T(8,128)(2,1)}, bf16[512,3584]{1,0:T(8,128)(2,1)S(1)}, u32[]{:S(2)}, u32[]{:S(2)}) collective-permute-start(bf16[512,3584]{1,0:T(8,128)(2,1)} %bitcast.20), channel_id=1, source_target_pairs={{0,16},{16,0},{1,17},{17,1},{2,18},{18,2},{3,19},{19,3},{4,20},{20... | collective-permute-start | bytes 11010056 | tf_op jit(solution)/shard_map/ppermute | solution.py:424
  1.2 34.2 %collective-permute-start.2 = (bf16[3584,512]{1,0:T(8,128)(2,1)}, bf16[3584,512]{1,0:T(8,128)(2,1)S(1)}, u32[]{:S(2)}, u32[]{:S(2)}) collective-permute-start(bf16[3584,512]{1,0:T(8,128)(2,1)} %bitcast.21), channel_id=1, source_target_pairs={{0,16},{16,0},{1,17},{17,1},{2,18},{18,2},{3,19},{19,3},{4,20},{20... | collective-permute-start | bytes 11010056 | tf_op jit(solution)/shard_map/ppermute | solution.py:424
  1.2 34.1 %collective-permute-start.3 = (bf16[3584,512]{1,0:T(8,128)(2,1)}, bf16[3584,512]{1,0:T(8,128)(2,1)S(1)}, u32[]{:S(2)}, u32[]{:S(2)}) collective-permute-start(bf16[3584,512]{1,0:T(8,128)(2,1)} %bitcast.22), channel_id=1, source_target_pairs={{0,16},{16,0},{1,17},{17,1},{2,18},{18,2},{3,19},{19,3},{4,20},{20... | collective-permute-start | bytes 11010056 | tf_op jit(solution)/shard_map/ppermute | solution.py:424
  33.3 1.9 %collective-permute-start = (bf16[64,3584]{1,0:T(8,128)(2,1)S(1)}, bf16[64,3584]{1,0:T(8,128)(2,1)S(1)}, u32[]{:S(2)}, u32[]{:S(2)}) collective-permute-start(bf16[64,3584]{1,0:T(8,128)(2,1)S(1)} %get-tuple-element.30.after_ref.mine_ref.tok_theirs), channel_id=1, source_target_pairs={{0,16},{16,0},{1,17},{17,1},{2,18},{18,2},{3,19},{19,3},{4,20},{20... | collective-permute-start | bytes 1376264 | tf_op jit(solution)/shard_map/ppermute | solution.py:421
  35.2 2.2 %collective-permute-start.4 = (bf16[64,3584]{1,0:T(8,128)(2,1)S(1)}, bf16[64,3584]{1,0:T(8,128)(2,1)S(1)}, u32[]{:S(2)}, u32[]{:S(2)}) collective-permute-start(bf16[64,3584]{1,0:T(8,128)(2,1)S(1)} %get-tuple-element.35.mine_ref.cot_theirs), channel_id=1, source_target_pairs={{0,16},{16,0},{1,17},{17,1},{2,18},{18,2},{3,19},{19,3},{4,20},{20... | collective-permute-start | bytes 1376264 | tf_op jit(solution)/shard_map/ppermute | solution.py:421
  37.4 3.4 %collective-permute-start.5 = (bf16[64,3584]{1,0:T(8,128)(2,1)S(1)}, bf16[64,3584]{1,0:T(8,128)(2,1)S(1)}, u32[]{:S(2)}, u32[]{:S(2)}) collective-permute-start(bf16[64,3584]{1,0:T(8,128)(2,1)S(1)} %get-tuple-element.36), channel_id=1, source_target_pairs={{0,16},{16,0},{1,17},{17,1},{2,18},{18,2},{3,19},{19,3},{4,20},{20... | collective-permute-start | bytes 1376264 | tf_op jit(solution)/shard_map/ppermute | solution.py:421
  39.2 1.6 %collective-permute-start.7 = (bf16[64,2048]{1,0:T(8,128)(2,1)S(1)}, bf16[64,2048]{1,0:T(8,128)(2,1)S(1)}, u32[]{:S(2)}, u32[]{:S(2)}) collective-permute-start(bf16[64,2048]{1,0:T(8,128)(2,1)S(1)} %get-tuple-element.48), channel_id=1, source_target_pairs={{0,16},{16,0},{1,17},{17,1},{2,18},{18,2},{3,19},{19,3},{4,20},{20... | collective-permute-start | bytes 786440 | tf_op jit(solution)/shard_map/ppermute | solution.py:421
  40.0 1.7 %collective-permute-start.6 = (bf16[64,1536]{1,0:T(8,128)(2,1)S(1)}, bf16[64,1536]{1,0:T(8,128)(2,1)S(1)}, u32[]{:S(2)}, u32[]{:S(2)}) collective-permute-start(bf16[64,1536]{1,0:T(8,128)(2,1)S(1)} %get-tuple-element.46), channel_id=1, source_target_pairs={{0,16},{16,0},{1,17},{17,1},{2,18},{18,2},{3,19},{19,3},{4,20},{20... | collective-permute-start | bytes 589832 | tf_op jit(solution)/shard_map/ppermute | solution.py:421
  42.6 25.5 %all-to-all-start.1 = ((bf16[16,8,3584]{2,1,0:T(8,128)(2,1)}), bf16[16,8,3584]{2,1,0:T(8,128)(2,1)S(1)}, u32[]{:S(2)}, u32[]{:S(2)}) async-start(bf16[16,8,3584]{2,1,0:T(8,128)(2,1)} %bitcast.15), calls=%async_computation.1 | async-start | bytes 1835008 | tf_op jit(solution)/shard_map/all_to_all | solution.py:414
  48.0 2.2 %collective-permute-start.8 = (bf16[128,512]{1,0:T(8,128)(2,1)S(1)}, bf16[128,512]{1,0:T(8,128)(2,1)S(1)}, u32[]{:S(2)}, u32[]{:S(2)}) collective-permute-start(bf16[128,512]{1,0:T(8,128)(2,1)S(1)} %get-tuple-element.51), channel_id=1, source_target_pairs={{0,16},{16,0},{1,17},{17,1},{2,18},{18,2},{3,19},{19,3},{4,20},{20... | collective-permute-start | bytes 393224 | tf_op jit(solution)/shard_map/ppermute | solution.py:443
  48.5 1.6 %collective-permute-start.10 = (bf16[128,512]{1,0:T(8,128)(2,1)S(1)}, bf16[128,512]{1,0:T(8,128)(2,1)S(1)}, u32[]{:S(2)}, u32[]{:S(2)}) collective-permute-start(bf16[128,512]{1,0:T(8,128)(2,1)S(1)} %get-tuple-element.44.up_cot_ref), channel_id=1, source_target_pairs={{0,16},{16,0},{1,17},{17,1},{2,18},{18,2},{3,19},{19,3},{4,20},{20... | collective-permute-start | bytes 393224 | tf_op jit(solution)/shard_map/ppermute | solution.py:443
  48.6 1.6 %collective-permute-start.9 = (bf16[128,512]{1,0:T(8,128)(2,1)S(1)}, bf16[128,512]{1,0:T(8,128)(2,1)S(1)}, u32[]{:S(2)}, u32[]{:S(2)}) collective-permute-start(bf16[128,512]{1,0:T(8,128)(2,1)S(1)} %get-tuple-element.43.gate_cot_ref), channel_id=1, source_target_pairs={{0,16},{16,0},{1,17},{17,1},{2,18},{18,2},{3,19},{19,3},{4,20},{20... | collective-permute-start | bytes 393224 | tf_op jit(solution)/shard_map/ppermute | solution.py:443

commit v6 on v5

--- a/solution.py
+++ b/solution.py
@@ -293,37 +293,53 @@
     )(*in_vmem(gate_cot, up_cot, gate, up))
 
 
-def add_kernel(cap, first, own_out, arrived_out, own_ref, arrived_ref, *refs):
-    out_hbm, out_ref, sems = refs[-3:]
+def add_columns(cap, first, own_out, arrived_out, own_ref, arrived_ref, out_ref):
     rows = out_ref.shape[0]
     groups = rows // (2 * cap)
-    copies = []
-    for j, here in enumerate(spread(out_ref.shape[1])):
-        cols = pl.ds((first + j) * COLS, COLS)
+    for here in spread(out_ref.shape[1]):
+        cols = pl.ds(first + here.start, COLS)
         out = own_out[:, cols].astype(F32) + arrived_out[:, cols].astype(F32)
         grad = own_ref[:, here].astype(F32) + arrived_ref[:, here].astype(F32)
         both = jnp.concatenate([out.reshape(groups, cap, COLS), grad.reshape(groups, cap, COLS)], axis=1)
         out_ref[:, here] = both.reshape(rows, COLS).astype(BF16)
-        copies.append(pltpu.make_async_copy(out_ref.at[:, here], out_hbm.at[:, cols], sems.at[j]))
-        copies[j].start()
-    for copy in copies:
-        copy.wait()
-
-
-def add_rows(cap, first, own_out, arrived_out, own, arrived, filled=None):
-    half, depth = own_out.shape
-    cols = own.shape[1]
-    more = [] if filled is None else in_hbm(filled)
-    return pl.pallas_call(
-        lambda *refs: add_kernel(cap, first, *refs),
-        in_specs=[WHOLE] * 4 + [REMOTE] * len(more),
+
+
+def add_early(cap, own_out, arrived_out, own, arrived):
+    half, cols = own.shape
+    return pl.pallas_call(
+        lambda *refs: add_columns(cap, 0, *refs),
+        in_specs=[WHOLE] * 4,
+        out_specs=WHOLE,
+        out_shape=pltpu.VMEM((2 * half, cols), BF16),
+        compiler_params=pltpu.CompilerParams(vmem_limit_bytes=16 * MIB),
+        name="add_early",
+    )(*in_vmem(own_out, arrived_out, own, arrived))
+
+
+def add_late_kernel(cap, early_ref, own_out, arrived_out, own_ref, arrived_ref, out_hbm, late_ref, sems):
+    early = early_ref.shape[1]
+    late = late_ref.shape[1]
+    copy_early = pltpu.make_async_copy(early_ref, out_hbm.at[:, pl.ds(0, early)], sems.at[0])
+    copy_early.start()
+    add_columns(cap, early, own_out, arrived_out, own_ref, arrived_ref, late_ref)
+    copy_late = pltpu.make_async_copy(late_ref, out_hbm.at[:, pl.ds(early, late)], sems.at[1])
+    copy_late.start()
+    copy_early.wait()
+    copy_late.wait()
+
+
+def add_late(cap, early, own_out, arrived_out, own, arrived):
+    half, cols = own.shape
+    depth = own_out.shape[1]
+    return pl.pallas_call(
+        lambda *refs: add_late_kernel(cap, *refs),
+        in_specs=[WHOLE] * 5,
         out_specs=REMOTE,
         out_shape=pltpu.HBM((2 * half, depth), BF16),
-        scratch_shapes=[pltpu.VMEM((2 * half, cols), BF16), pltpu.SemaphoreType.DMA((cols // COLS,))],
-        input_output_aliases={4: 0} if more else {},
+        scratch_shapes=[pltpu.VMEM((2 * half, cols), BF16), pltpu.SemaphoreType.DMA((2,))],
         compiler_params=pltpu.CompilerParams(vmem_limit_bytes=16 * MIB),
-        name="add_late" if more else "add_early",
-    )(*in_vmem(own_out, arrived_out, own, arrived), *more)
+        name="add_late",
+    )(*in_vmem(early, own_out, arrived_out, own, arrived))
 
 
 def grads_kernel(
@@ -426,19 +442,20 @@
     tok_mine, cot_mine = compact(exchange(send), cap)
     tok_theirs, _ = swapped(tok_mine)
     down_flip = flip(tok_mine, down)
-    cot_theirs, (tok_theirs, down_flip) = swapped(cot_mine, (tok_theirs, down_flip))
+    cot_theirs, _ = swapped(cot_mine)
+    tok_theirs, down_flip = lax.optimization_barrier((tok_theirs, down_flip))
     own_out, other_out, hidden, gate_act, up_act, gate_flip, up_flip = forward(
         tok_mine, tok_theirs, gate, up, down
     )
-    arrived_out, cot_theirs = swapped(other_out, cot_theirs)
+    arrived_out, _ = swapped(other_out)
     own_early, other_early, gate_cot, up_cot = backward(
         cot_mine, cot_theirs, gate_flip, up_flip, down_flip, gate_act, up_act
     )
     arrived_early, _ = swapped(other_early)
     own_late, other_late = late_rows(gate_cot, up_cot, gate_flip, up_flip)
     arrived_late, _ = swapped(other_late)
-    sums = add_rows(cap, 0, own_out, arrived_out, own_early, arrived_early)
-    sums = add_rows(cap, own_early.shape[1] // COLS, own_out, arrived_out, own_late, arrived_late, sums)
+    sums = add_early(cap, own_out, arrived_out, own_early, arrived_early)
+    sums = add_late(cap, sums, own_out, arrived_out, own_late, arrived_late)
     back = exchange(sums)
     hidden, gate_cot, up_cot = [lax.ppermute(a, "edp", swap) for a in (hidden, gate_cot, up_cot)]
     grad_gate, grad_up, grad_down = grads(

time: 70.1 us -> 69.8 us (level)
  transfers between devices with their start and end apart: 12 -> 12, of which waited for: 3 -> 4; matrix products, arithmetic and copies ran while one was open for 0% -> 0% of each run, Pallas kernels for 22% -> 21%
where the time goes in v6:
time: 69.8 us; the launch traced here: 69.5 us
  blocking collectives  29.5 us (42%)
  Pallas kernels  17.4 us (25%)
  waiting for transfers between devices  12.9 us (18%)
  starting transfers between devices  8.88 us (13%)
  between operations  0.75 us (1%)
    all_to_all x1, blocking collectives, exchange(): lax.all_to_all(blocks, ('edp', 'ep'), split_axis=0, concat_axis=0, tiled=...  29.5 us
    all_to_all x1, waiting for transfers between devices, exchange(): lax.all_to_all(blocks, ('edp', 'ep'), split_axis=0, concat_axis=0, tiled=...  11.5 us
    pallas_call x1, Pallas kernels, grads(): pl.pallas_call(grads_kernel, grid=(depth // COLS,), in_specs=[WHOLE] * 7,...  6.36 us
    all_to_all x1, starting transfers between devices, exchange(): lax.all_to_all(blocks, ('edp', 'ep'), split_axis=0, concat_axis=0, tiled=...  5.41 us
    pallas_call x1, Pallas kernels, forward(): pl.pallas_call(forward_kernel, in_specs=[WHOLE] * 5, out_specs=[WHOLE] *...  2.06 us
    pallas_call x1, Pallas kernels, route(): pl.pallas_call(lambda *refs: route_kernel(cap, *refs), in_specs=[REMOTE]...  1.94 us
    pallas_call x1, Pallas kernels, combine(): pl.pallas_call(combine_kernel, in_specs=[WHOLE, WHOLE], out_specs=[REMOTE...  1.68 us
    ppermute x5, starting transfers between devices, swapped(): return (lax.ppermute(rows, 'edp', swap), after)  1.4 us
  transfers between devices with their start and end apart: 12, of which 4 were waited for; matrix products, arithmetic and copies ran while one was open for 0% of the time, Pallas kernels for 21%

profile of v6, /device:TPU:0, one launch (start us, length us, event | category | flops | bytes accessed | tf_op | source)
XLA Modules:
  0.0 69.5 jit_solution(16804752638839122049)
XLA Ops:
  0.6 0.5 collective-permute-start.1
  1.2 0.1 collective-permute-start.2
  1.2 0.4 collective-permute-start.3
  1.7 1.9 %route.1 = bf16[128,3584]{1,0:T(8,128)(2,1)S(1)} custom-call(s32[8,128]{1,0:T(8,128)} %bitcast.16, f32[8,128]{1,0:T(8,128)} %bitcast.18, bf16[128,3584]{1,0:T(8,128)(2,1)} %refs_2_.1, bf16[128,3584]{1,0:T(8,128)(2,1)} %refs_3_.1), custom_call_target="tpu_custom_call" | custom-call | tf_op jit(solution)/shard_map/route/pallas_call | solution.py:98
  3.6 29.5 %all_to_all.10 = bf16[16,8,3584]{2,1,0:T(8,128)(2,1)S(1)} all-to-all(bf16[16,8,3584]{2,1,0:T(8,128)(2,1)S(1)} %bitcast.14), channel_id=1, replica_groups={{0,1,2,3,4,5,6,7,8,9,10,11,12,13,14,15},{26,27,24,25,30,31,28,29,18,19,..., dimensions={0} | all-to-all | bytes 1835008 | tf_op jit(solution)/shard_map/all_to_all | solution.py:430
  33.1 0.2 compact.1
  33.3 0.1 collective-permute-start
  33.4 0.5 collective-permute-start.5
  33.9 0.0 collective-permute-done.1.down_ref
  33.9 1.0 %flip_down.1.down_ref = bf16[3584,512]{1,0:T(8,128)(2,1)S(1)} custom-call(bf16[64,3584]{1,0:T(8,128)(2,1)S(1)} %get-tuple-element.27.after_ref.mine_ref.tok_theirs, bf16[512,3584]{1,0:T(8,128)(2,1)S(1)} %collective-permute-done.1.down_ref), custom_call_target="tpu_custom_call" | custom-call | tf_op jit(solution)/shard_map/flip_down/pallas_call | solution.py:180
  34.9 0.3 collective-permute-done.theirs_ref.tok_mine
  35.2 0.0 collective-permute-done.2.gate_ref
  35.2 0.0 collective-permute-done.3.up_ref
  35.2 2.1 %expert_forward.1 = (bf16[64,3584]{1,0:T(8,128)(2,1)S(1)}, bf16[64,3584]{1,0:T(8,128)(2,1)S(1)}, bf16[128,512]{1,0:T(8,128)(2,1)S(1)}, f32[128,512]{1,0:T(8,128)...) custom-call(bf16[64,3584]{1,0:T(8,128)(2,1)S(1)} %get-tuple-element.27.after_ref.mine_ref, ...), custom_call_target="tpu_custom_call" | custom-call | tf_op jit(solution)/shard_map/expert_forward/pallas_call | solution.py:219
  37.3 0.2 collective-permute-start.4
  37.5 0.0 collective-permute-done.5.theirs_ref.cot_mine
  37.5 1.3 %expert_backward.1 = (bf16[64,2048]{1,0:T(8,128)(2,1)S(1)}, bf16[64,2048]{1,0:T(8,128)(2,1)S(1)}, bf16[128,512]{1,0:T(8,128)(2,1)S(1)}, bf16[128,512]{1,0:T(8,128)(2,1)S(1)}) custom-call(bf16[64,3584]{1,0:T(8,128)(2,1)S(1)} %get-tuple-element.31.mine_ref.cot_theirs, bf16[64,3584]{1,0:T(8,128)(2,1)S(1)} %collective-permute-done.5.theirs_ref.cot_mine, ...), custom_call_target="tpu_custom_call" | custom-call | tf_op jit(solution)/shard_map/expert_backward/pallas_call | solution.py:267
  38.8 0.4 collective-permute-start.6
  39.2 0.6 late_rows.1
  39.8 0.2 collective-permute-start.7
  40.0 0.4 collective-permute-done.6.refs_3_
  40.4 0.0 collective-permute-done.4.refs_1_.refs_2_
  40.4 0.2 add_early.1.refs_0_
  40.6 0.7 %collective-permute-done.7.refs_4_ = bf16[64,1536]{1,0:T(8,128)(2,1)S(1)} collective-permute-done((bf16[64,1536]{1,0:T(8,128)(2,1)S(1)}, bf16[64,1536]{1,0:T(8,128)(2,1)S(1)}, u32[]{:S(2)}, u32[]{:S(2)}) %collective-permute-start.7) | collective-permute-done | bytes 196640 | tf_op jit(solution)/shard_map/ppermute | solution.py:437
  41.3 0.9 %add_late.1 = bf16[128,3584]{1,0:T(8,128)(2,1)} custom-call(bf16[128,2048]{1,0:T(8,128)(2,1)S(1)} %add_early.1.refs_0_, bf16[64,3584]{1,0:T(8,128)(2,1)S(1)} %get-tuple-element.29.refs_0_.refs_1_, bf16[64,3584]{1,0:T(8,128)(2,1)S(1)} %collective-permute-done.4.refs_1_.refs_2_, bf16[64,1536]{1,0:T(8,128)(2,1)S(1)} %get-tuple-element.41.refs_3_, ...), custom_call_target="tpu_custom_call" | custom-call | tf_op jit(solution)/shard_map/add_late/pallas_call | solution.py:334
  42.3 5.4 %all-to-all-start.1 = ((bf16[16,8,3584]{2,1,0:T(8,128)(2,1)}), bf16[16,8,3584]{2,1,0:T(8,128)(2,1)S(1)}, u32[]{:S(2)}, u32[]{:S(2)}) async-start(bf16[16,8,3584]{2,1,0:T(8,128)(2,1)} %bitcast.15), calls=%async_computation.1 | async-start | bytes 1835008 | tf_op jit(solution)/shard_map/all_to_all | solution.py:430
  47.7 0.5 collective-permute-start.10
  48.2 0.1 collective-permute-start.9
  48.3 0.4 collective-permute-start.8
  48.7 1.1 %selectors.1.select_ref = bf16[384,128]{1,0:T(8,128)(2,1)S(1)} custom-call(s32[8,128]{1,0:T(8,128)} %bitcast.17, f32[8,128]{1,0:T(8,128)} %bitcast.19), custom_call_target="tpu_custom_call" | custom-call | tf_op jit(solution)/shard_map/selectors/pallas_call | solution.py:137
  49.9 0.0 collective-permute-done.10.up_cot_ref
  49.9 0.0 collective-permute-done.9.gate_cot_ref
  49.9 0.0 collective-permute-done.8.hid_ref
  49.9 6.4 %weight_grads.1 = (bf16[3584,512]{1,0:T(8,128)(2,1)}, bf16[3584,512]{1,0:T(8,128)(2,1)}, bf16[512,3584]{1,0:T(8,128)(2,1)}) custom-call(bf16[64,3584]{1,0:T(8,128)(2,1)S(1)} %collective-permute-done.theirs_ref.tok_mine, bf16[64,3584]{1,0:T(8,128)(2,1)S(1)} %get-tuple-element.27.after_ref.mine_ref.tok_theirs, ...), custom_call_target="tpu_custom_call" | custom-call | tf_op jit(solution)/shard_map/weight_grads/pallas_call | solution.py:362
  56.2 11.5 %all-to-all-done.1 = bf16[16,8,3584]{2,1,0:T(8,128)(2,1)S(1)} async-done(((bf16[16,8,3584]{2,1,0:T(8,128)(2,1)}), bf16[16,8,3584]{2,1,0:T(8,128)(2,1)S(1)}, u32[]{:S(2)}, u32[]{:S(2)}) %all-to-all-start.1) | async-done | bytes 917536 | tf_op jit(solution)/shard_map/all_to_all | solution.py:430
  67.8 1.7 %combine.1 = (bf16[128,3584]{1,0:T(8,128)(2,1)}, bf16[128,3584]{1,0:T(8,128)(2,1)}) custom-call(bf16[128,3584]{1,0:T(8,128)(2,1)S(1)} %bitcast.13, bf16[384,128]{1,0:T(8,128)(2,1)S(1)} %selectors.1.select_ref), custom_call_target="tpu_custom_call" | custom-call | tf_op jit(solution)/shard_map/combine/pallas_call | solution.py:402
Async XLA Ops:
  0.6 33.3 %collective-permute-start.1 = (bf16[512,3584]{1,0:T(8,128)(2,1)}, bf16[512,3584]{1,0:T(8,128)(2,1)S(1)}, u32[]{:S(2)}, u32[]{:S(2)}) collective-permute-start(bf16[512,3584]{1,0:T(8,128)(2,1)} %bitcast.20), channel_id=1, source_target_pairs={{0,16},{16,0},{1,17},{17,1},{2,18},{18,2},{3,19},{19,3},{4,20},{20... | collective-permute-start | bytes 11010056 | tf_op jit(solution)/shard_map/ppermute | solution.py:440
  1.2 34.0 %collective-permute-start.2 = (bf16[3584,512]{1,0:T(8,128)(2,1)}, bf16[3584,512]{1,0:T(8,128)(2,1)S(1)}, u32[]{:S(2)}, u32[]{:S(2)}) collective-permute-start(bf16[3584,512]{1,0:T(8,128)(2,1)} %bitcast.21), channel_id=1, source_target_pairs={{0,16},{16,0},{1,17},{17,1},{2,18},{18,2},{3,19},{19,3},{4,20},{20... | collective-permute-start | bytes 11010056 | tf_op jit(solution)/shard_map/ppermute | solution.py:440
  1.2 34.0 %collective-permute-start.3 = (bf16[3584,512]{1,0:T(8,128)(2,1)}, bf16[3584,512]{1,0:T(8,128)(2,1)S(1)}, u32[]{:S(2)}, u32[]{:S(2)}) collective-permute-start(bf16[3584,512]{1,0:T(8,128)(2,1)} %bitcast.22), channel_id=1, source_target_pairs={{0,16},{16,0},{1,17},{17,1},{2,18},{18,2},{3,19},{19,3},{4,20},{20... | collective-permute-start | bytes 11010056 | tf_op jit(solution)/shard_map/ppermute | solution.py:440
  33.3 1.9 %collective-permute-start = (bf16[64,3584]{1,0:T(8,128)(2,1)S(1)}, bf16[64,3584]{1,0:T(8,128)(2,1)S(1)}, u32[]{:S(2)}, u32[]{:S(2)}) collective-permute-start(bf16[64,3584]{1,0:T(8,128)(2,1)S(1)} %get-tuple-element.27.after_ref.mine_ref.tok_theirs), channel_id=1, source_target_pairs={{0,16},{16,0},{1,17},{17,1},{2,18},{18,2},{3,19},{19,3},{4,20},{20... | collective-permute-start | bytes 1376264 | tf_op jit(solution)/shard_map/ppermute | solution.py:437
  33.4 4.1 %collective-permute-start.5 = (bf16[64,3584]{1,0:T(8,128)(2,1)S(1)}, bf16[64,3584]{1,0:T(8,128)(2,1)S(1)}, u32[]{:S(2)}, u32[]{:S(2)}) collective-permute-start(bf16[64,3584]{1,0:T(8,128)(2,1)S(1)} %get-tuple-element.31.mine_ref.cot_theirs), channel_id=1, source_target_pairs={{0,16},{16,0},{1,17},{17,1},{2,18},{18,2},{3,19},{19,3},{4,20},{20... | collective-permute-start | bytes 1376264 | tf_op jit(solution)/shard_map/ppermute | solution.py:437
  37.3 3.1 %collective-permute-start.4 = (bf16[64,3584]{1,0:T(8,128)(2,1)S(1)}, bf16[64,3584]{1,0:T(8,128)(2,1)S(1)}, u32[]{:S(2)}, u32[]{:S(2)}) collective-permute-start(bf16[64,3584]{1,0:T(8,128)(2,1)S(1)} %get-tuple-element.30), channel_id=1, source_target_pairs={{0,16},{16,0},{1,17},{17,1},{2,18},{18,2},{3,19},{19,3},{4,20},{20... | collective-permute-start | bytes 1376264 | tf_op jit(solution)/shard_map/ppermute | solution.py:437
  38.8 1.6 %collective-permute-start.6 = (bf16[64,2048]{1,0:T(8,128)(2,1)S(1)}, bf16[64,2048]{1,0:T(8,128)(2,1)S(1)}, u32[]{:S(2)}, u32[]{:S(2)}) collective-permute-start(bf16[64,2048]{1,0:T(8,128)(2,1)S(1)} %get-tuple-element.38), channel_id=1, source_target_pairs={{0,16},{16,0},{1,17},{17,1},{2,18},{18,2},{3,19},{19,3},{4,20},{20... | collective-permute-start | bytes 786440 | tf_op jit(solution)/shard_map/ppermute | solution.py:437
  39.8 1.5 %collective-permute-start.7 = (bf16[64,1536]{1,0:T(8,128)(2,1)S(1)}, bf16[64,1536]{1,0:T(8,128)(2,1)S(1)}, u32[]{:S(2)}, u32[]{:S(2)}) collective-permute-start(bf16[64,1536]{1,0:T(8,128)(2,1)S(1)} %get-tuple-element.42), channel_id=1, source_target_pairs={{0,16},{16,0},{1,17},{17,1},{2,18},{18,2},{3,19},{19,3},{4,20},{20... | collective-permute-start | bytes 589832 | tf_op jit(solution)/shard_map/ppermute | solution.py:437
  42.3 25.5 %all-to-all-start.1 = ((bf16[16,8,3584]{2,1,0:T(8,128)(2,1)}), bf16[16,8,3584]{2,1,0:T(8,128)(2,1)S(1)}, u32[]{:S(2)}, u32[]{:S(2)}) async-start(bf16[16,8,3584]{2,1,0:T(8,128)(2,1)} %bitcast.15), calls=%async_computation.1 | async-start | bytes 1835008 | tf_op jit(solution)/shard_map/all_to_all | solution.py:430
  47.7 2.2 %collective-permute-start.10 = (bf16[128,512]{1,0:T(8,128)(2,1)S(1)}, bf16[128,512]{1,0:T(8,128)(2,1)S(1)}, u32[]{:S(2)}, u32[]{:S(2)}) collective-permute-start(bf16[128,512]{1,0:T(8,128)(2,1)S(1)} %get-tuple-element.40.up_cot_ref), channel_id=1, source_target_pairs={{0,16},{16,0},{1,17},{17,1},{2,18},{18,2},{3,19},{19,3},{4,20},{20... | collective-permute-start | bytes 393224 | tf_op jit(solution)/shard_map/ppermute | solution.py:460
  48.2 1.6 %collective-permute-start.9 = (bf16[128,512]{1,0:T(8,128)(2,1)S(1)}, bf16[128,512]{1,0:T(8,128)(2,1)S(1)}, u32[]{:S(2)}, u32[]{:S(2)}) collective-permute-start(bf16[128,512]{1,0:T(8,128)(2,1)S(1)} %get-tuple-element.39.gate_cot_ref), channel_id=1, source_target_pairs={{0,16},{16,0},{1,17},{17,1},{2,18},{18,2},{3,19},{19,3},{4,20},{20... | collective-permute-start | bytes 393224 | tf_op jit(solution)/shard_map/ppermute | solution.py:460
  48.3 1.6 %collective-permute-start.8 = (bf16[128,512]{1,0:T(8,128)(2,1)S(1)}, bf16[128,512]{1,0:T(8,128)(2,1)S(1)}, u32[]{:S(2)}, u32[]{:S(2)}) collective-permute-start(bf16[128,512]{1,0:T(8,128)(2,1)S(1)} %get-tuple-element.45), channel_id=1, source_target_pairs={{0,16},{16,0},{1,17},{17,1},{2,18},{18,2},{3,19},{19,3},{4,20},{20... | collective-permute-start | bytes 393224 | tf_op jit(solution)/shard_map/ppermute | solution.py:460

commit v7 on v6

--- a/solution.py
+++ b/solution.py
@@ -150,22 +150,27 @@
     )(*in_hbm(ids, weight))
 
 
-def compact_kernel(cap, rows_ref, tok_ref, cot_ref):
+def compact_kernel(cap, rows_ref, early_ref, late_ref, cot_ref):
     groups = rows_ref.shape[0] // (2 * cap)
-    half = tok_ref.shape[0]
-    for cols in spread(rows_ref.shape[1]):
+    half, early = early_ref.shape
+    for j, cols in enumerate(spread(rows_ref.shape[1])):
         both = rows_ref[:, cols].astype(F32).reshape(groups, 2, cap, COLS)
-        tok_ref[:, cols] = both[:, 0].reshape(half, COLS).astype(BF16)
+        tok = both[:, 0].reshape(half, COLS).astype(BF16)
+        if j * COLS < early:
+            early_ref[:, cols] = tok
+        else:
+            late_ref[:, pl.ds(j * COLS - early, COLS)] = tok
         cot_ref[:, cols] = both[:, 1].reshape(half, COLS).astype(BF16)
 
 
 def compact(rows, cap):
     half, depth = rows.shape[0] // 2, rows.shape[1]
+    early = early_cols(depth)
     return pl.pallas_call(
         lambda *refs: compact_kernel(cap, *refs),
         in_specs=[WHOLE],
-        out_specs=[WHOLE] * 2,
-        out_shape=[pltpu.VMEM((half, depth), BF16)] * 2,
+        out_specs=[WHOLE] * 3,
+        out_shape=[pltpu.VMEM((half, w), BF16) for w in (early, depth - early, depth)],
         compiler_params=pltpu.CompilerParams(vmem_limit_bytes=8 * MIB),
         name="compact",
     )(*in_vmem(rows))
@@ -193,32 +198,60 @@
     other_ref[:, cols] = value[half:].astype(BF16)
 
 
+def projections(mine_ref, theirs_ref, gate_ref, up_ref, first, gate_act, up_act, flips):
+    for cols in spread(mine_ref.shape[1]):
+        there = pl.ds(first + cols.start, COLS)
+        rows = jnp.concatenate([mine_ref[:, cols], theirs_ref[:, cols]], axis=0)
+        gate_act = gate_act + matmul(rows, gate_ref[there, :])
+        up_act = up_act + matmul(rows, up_ref[there, :])
+        flips[:, cols] = jnp.transpose(gate_ref[there, :])
+    return gate_act, up_act
+
+
+def begin_kernel(mine_ref, theirs_ref, gate_ref, up_ref, gate_act_ref, up_act_ref, gate_early_ref):
+    zero = jnp.zeros(gate_act_ref.shape, F32)
+    gate_act_ref[...], up_act_ref[...] = projections(
+        mine_ref, theirs_ref, gate_ref, up_ref, 0, zero, zero, gate_early_ref
+    )
+
+
+def begin(mine, theirs, gate, up):
+    half, early = mine.shape
+    width = gate.shape[1]
+    return pl.pallas_call(
+        begin_kernel,
+        in_specs=[WHOLE] * 4,
+        out_specs=[WHOLE] * 3,
+        out_shape=[pltpu.VMEM((2 * half, width), F32)] * 2 + [pltpu.VMEM((width, early), BF16)],
+        compiler_params=pltpu.CompilerParams(vmem_limit_bytes=SCOPED),
+        name="expert_begin",
+    )(*in_vmem(mine, theirs, gate, up))
+
+
 def forward_kernel(
-    mine_ref, theirs_ref, gate_ref, up_ref, down_ref,
-    own_ref, other_ref, hid_ref, gate_act_ref, up_act_ref, gate_flip_ref, up_flip_ref,
+    mine_ref, theirs_ref, gate_ref, up_ref, down_ref, gate_begun, up_begun,
+    own_ref, other_ref, hid_ref, gate_act_ref, up_act_ref, gate_late_ref, up_early_ref,
 ):
-    gate_act = jnp.zeros(gate_act_ref.shape, F32)
-    up_act = jnp.zeros(up_act_ref.shape, F32)
-    for cols in spread(mine_ref.shape[1]):
-        rows = jnp.concatenate([mine_ref[:, cols], theirs_ref[:, cols]], axis=0)
-        gate_act = gate_act + matmul(rows, gate_ref[cols, :])
-        up_act = up_act + matmul(rows, up_ref[cols, :])
-        gate_flip_ref[:, cols] = jnp.transpose(gate_ref[cols, :])
+    early = up_early_ref.shape[1]
+    gate_act, up_act = projections(
+        mine_ref, theirs_ref, gate_ref, up_ref, early, gate_begun[...], up_begun[...], gate_late_ref
+    )
     gate_act_ref[...] = gate_act
     up_act_ref[...] = up_act
     hidden = (gate_act * jax.nn.sigmoid(gate_act) * up_act).astype(BF16)
     hid_ref[...] = hidden
-    for cols in spread(mine_ref.shape[1]):
+    for j, cols in enumerate(spread(down_ref.shape[1])):
         split_store(matmul(hidden, down_ref[:, cols]), own_ref, other_ref, cols)
-        up_flip_ref[:, cols] = jnp.transpose(up_ref[cols, :])
-
-
-def forward(mine, theirs, gate, up, down):
-    half, depth = mine.shape
-    width = gate.shape[1]
+        if j * COLS < early:
+            up_early_ref[:, cols] = jnp.transpose(up_ref[cols, :])
+
+
+def forward(mine, theirs, gate, up, down, gate_begun, up_begun):
+    half, late = mine.shape
+    depth, width = gate.shape
     return pl.pallas_call(
         forward_kernel,
-        in_specs=[WHOLE] * 5,
+        in_specs=[WHOLE] * 7,
         out_specs=[WHOLE] * 7,
         out_shape=[
             pltpu.VMEM((half, depth), BF16),
@@ -226,24 +259,23 @@
             pltpu.VMEM((2 * half, width), BF16),
             pltpu.VMEM((2 * half, width), F32),
             pltpu.VMEM((2 * half, width), F32),
-            pltpu.VMEM((width, depth), BF16),
-            pltpu.VMEM((width, depth), BF16),
+            pltpu.VMEM((width, late), BF16),
+            pltpu.VMEM((width, depth - late), BF16),
         ],
         compiler_params=pltpu.CompilerParams(vmem_limit_bytes=SCOPED),
         name="expert_forward",
-    )(*in_vmem(mine, theirs, gate, up, down))
-
-
-def row_grads(gate_cot, up_cot, gate_ref, up_ref, own_ref, other_ref, first):
-    for j in range(own_ref.shape[1] // COLS):
-        cols = pl.ds((first + j) * COLS, COLS)
+    )(*in_vmem(mine, theirs, gate, up, down, gate_begun, up_begun))
+
+
+def row_grads(gate_cot, up_cot, gate_ref, up_ref, own_ref, other_ref):
+    for cols in spread(own_ref.shape[1]):
         back = matmul(gate_cot, gate_ref[:, cols]) + matmul(up_cot, up_ref[:, cols])
-        split_store(back, own_ref, other_ref, pl.ds(j * COLS, COLS))
+        split_store(back, own_ref, other_ref, cols)
 
 
 def backward_kernel(
-    mine_ref, theirs_ref, gate_ref, up_ref, down_ref, gate_act_ref, up_act_ref,
-    own_ref, other_ref, gate_cot_ref, up_cot_ref,
+    mine_ref, theirs_ref, gate_early_ref, up_early_ref, up_ref, down_ref, gate_act_ref, up_act_ref,
+    own_ref, other_ref, gate_cot_ref, up_cot_ref, up_late_ref,
 ):
     rows = jnp.concatenate([mine_ref[...], theirs_ref[...]], axis=0)
     hidden_cot = matmul(rows, down_ref[...])
@@ -253,36 +285,38 @@
     up_cot = (hidden_cot * (gate_act * sigma)).astype(BF16)
     gate_cot_ref[...] = gate_cot
     up_cot_ref[...] = up_cot
-    row_grads(gate_cot, up_cot, gate_ref, up_ref, own_ref, other_ref, 0)
+    early = own_ref.shape[1]
+    for cols in spread(up_late_ref.shape[1]):
+        up_late_ref[:, cols] = jnp.transpose(up_ref[pl.ds(early + cols.start, COLS), :])
+    row_grads(gate_cot, up_cot, gate_early_ref, up_early_ref, own_ref, other_ref)
 
 
 def early_cols(depth):
     return depth // COLS * 4 // 7 * COLS
 
 
-def backward(mine, theirs, gate, up, down, gate_act, up_act):
+def backward(mine, theirs, gate_early, up_early, up, down, gate_act, up_act):
     half, depth = mine.shape
-    width = gate.shape[0]
-    early = early_cols(depth)
+    width, early = gate_early.shape
     return pl.pallas_call(
         backward_kernel,
-        in_specs=[WHOLE] * 7,
-        out_specs=[WHOLE] * 4,
-        out_shape=[pltpu.VMEM((half, early), BF16)] * 2 + [pltpu.VMEM((2 * half, width), BF16)] * 2,
+        in_specs=[WHOLE] * 8,
+        out_specs=[WHOLE] * 5,
+        out_shape=[pltpu.VMEM((half, early), BF16)] * 2
+        + [pltpu.VMEM((2 * half, width), BF16)] * 2
+        + [pltpu.VMEM((width, depth - early), BF16)],
         compiler_params=pltpu.CompilerParams(vmem_limit_bytes=SCOPED),
         name="expert_backward",
-    )(*in_vmem(mine, theirs, gate, up, down, gate_act, up_act))
+    )(*in_vmem(mine, theirs, gate_early, up_early, up, down, gate_act, up_act))
 
 
 def late_kernel(gate_cot_ref, up_cot_ref, gate_ref, up_ref, own_ref, other_ref):
-    first = (gate_ref.shape[1] - own_ref.shape[1]) // COLS
-    row_grads(gate_cot_ref[...], up_cot_ref[...], gate_ref, up_ref, own_ref, other_ref, first)
-
-
-def late_rows(gate_cot, up_cot, gate, up):
+    row_grads(gate_cot_ref[...], up_cot_ref[...], gate_ref, up_ref, own_ref, other_ref)
+
+
+def late_rows(gate_cot, up_cot, gate_late, up_late):
     half = gate_cot.shape[0] // 2
-    depth = gate.shape[1]
-    late = depth - early_cols(depth)
+    late = gate_late.shape[1]
     return pl.pallas_call(
         late_kernel,
         in_specs=[WHOLE] * 4,
@@ -290,7 +324,7 @@
         out_shape=[pltpu.VMEM((half, late), BF16)] * 2,
         compiler_params=pltpu.CompilerParams(vmem_limit_bytes=8 * MIB),
         name="late_rows",
-    )(*in_vmem(gate_cot, up_cot, gate, up))
+    )(*in_vmem(gate_cot, up_cot, gate_late, up_late))
 
 
 def add_columns(cap, first, own_out, arrived_out, own_ref, arrived_ref, out_ref):
@@ -439,25 +473,29 @@
     gate, up, down = [
         lax.ppermute(w[0], "edp", swap) for w in (gate_weight, up_weight, down_weight)
     ]
-    tok_mine, cot_mine = compact(exchange(send), cap)
-    tok_theirs, _ = swapped(tok_mine)
-    down_flip = flip(tok_mine, down)
+    early_mine, late_mine, cot_mine = compact(exchange(send), cap)
+    early_theirs, _ = swapped(early_mine)
+    late_theirs, _ = swapped(late_mine)
+    down_flip = flip(early_mine, down)
     cot_theirs, _ = swapped(cot_mine)
-    tok_theirs, down_flip = lax.optimization_barrier((tok_theirs, down_flip))
-    own_out, other_out, hidden, gate_act, up_act, gate_flip, up_flip = forward(
-        tok_mine, tok_theirs, gate, up, down
+    early_theirs, down_flip = lax.optimization_barrier((early_theirs, down_flip))
+    gate_begun, up_begun, gate_early = begin(early_mine, early_theirs, gate, up)
+    own_out, other_out, hidden, gate_act, up_act, gate_late, up_early = forward(
+        late_mine, late_theirs, gate, up, down, gate_begun, up_begun
     )
     arrived_out, _ = swapped(other_out)
-    own_early, other_early, gate_cot, up_cot = backward(
-        cot_mine, cot_theirs, gate_flip, up_flip, down_flip, gate_act, up_act
+    own_early, other_early, gate_cot, up_cot, up_late = backward(
+        cot_mine, cot_theirs, gate_early, up_early, up, down_flip, gate_act, up_act
     )
     arrived_early, _ = swapped(other_early)
-    own_late, other_late = late_rows(gate_cot, up_cot, gate_flip, up_flip)
+    own_late, other_late = late_rows(gate_cot, up_cot, gate_late, up_late)
     arrived_late, _ = swapped(other_late)
     sums = add_early(cap, own_out, arrived_out, own_early, arrived_early)
     sums = add_late(cap, sums, own_out, arrived_out, own_late, arrived_late)
     back = exchange(sums)
     hidden, gate_cot, up_cot = [lax.ppermute(a, "edp", swap) for a in (hidden, gate_cot, up_cot)]
+    tok_mine = jnp.concatenate([early_mine, late_mine], axis=1)
+    tok_theirs = jnp.concatenate([early_theirs, late_theirs], axis=1)
     grad_gate, grad_up, grad_down = grads(
         tok_theirs, tok_mine, cot_theirs, cot_mine, hidden, gate_cot, up_cot
     )

time: 69.8 us -> 69.9 us (level)
    all_to_all x1, waiting for transfers between devices: 11.5 us -> 10.5 us  [exchange(): lax.all_to_all(blocks, ('edp', 'ep'), split_axis=0, concat_axis=0, tiled=...]
    ppermute x3, waiting for transfers between devices: 0.01 us -> 0.99 us  [per_device(): lax.ppermute(a, 'edp', swap)]
    ppermute x5 -> x6, starting transfers between devices: 1.4 us -> 1.72 us  [swapped(): return (lax.ppermute(rows, 'edp', swap), after)]
    pallas_call x2 -> x3, Pallas kernels: 3.39 us -> 3.41 us  [the longest x1 1.37 us: backward(): pl.pallas_call(backward_kernel, in_specs=[WHOLE] * 8, out_specs=[WHOLE] *...]
  transfers between devices with their start and end apart: 12 -> 13, of which waited for: 4 -> 7; matrix products, arithmetic and copies ran while one was open for 0% -> 0% of each run, Pallas kernels for 21% -> 21%
where the time goes in v7:
time: 69.9 us; the launch traced here: 69.6 us
  blocking collectives  29.5 us (42%)
  Pallas kernels  17.4 us (25%)
  waiting for transfers between devices  12.4 us (18%)
  starting transfers between devices  9.47 us (14%)
  between operations  0.76 us (1%)
    all_to_all x1, blocking collectives, exchange(): lax.all_to_all(blocks, ('edp', 'ep'), split_axis=0, concat_axis=0, tiled=...  29.5 us
    all_to_all x1, waiting for transfers between devices, exchange(): lax.all_to_all(blocks, ('edp', 'ep'), split_axis=0, concat_axis=0, tiled=...  10.5 us
    pallas_call x1, Pallas kernels, grads(): pl.pallas_call(grads_kernel, grid=(depth // COLS,), in_specs=[WHOLE] * 7,...  6.33 us
    all_to_all x1, starting transfers between devices, exchange(): lax.all_to_all(blocks, ('edp', 'ep'), split_axis=0, concat_axis=0, tiled=...  5.4 us
    pallas_call x1, Pallas kernels, route(): pl.pallas_call(lambda *refs: route_kernel(cap, *refs), in_specs=[REMOTE]...  1.94 us
    ppermute x6, starting transfers between devices, swapped(): return (lax.ppermute(rows, 'edp', swap), after)  1.72 us
    pallas_call x1, Pallas kernels, combine(): pl.pallas_call(combine_kernel, in_specs=[WHOLE, WHOLE], out_specs=[REMOTE...  1.68 us
  transfers between devices with their start and end apart: 13, of which 7 were waited for; matrix products, arithmetic and copies ran while one was open for 0% of the time, Pallas kernels for 21%

profile of v7, /device:TPU:0, one launch (start us, length us, event | category | flops | bytes accessed | tf_op | source)
XLA Modules:
  0.0 69.6 jit_solution(18149636918245854657)
XLA Ops:
  0.6 0.5 collective-permute-start.3
  1.2 0.1 collective-permute-start.2
  1.2 0.4 collective-permute-start.1
  1.7 1.9 %route.1 = bf16[128,3584]{1,0:T(8,128)(2,1)S(1)} custom-call(s32[8,128]{1,0:T(8,128)} %bitcast.16, f32[8,128]{1,0:T(8,128)} %bitcast.18, bf16[128,3584]{1,0:T(8,128)(2,1)} %refs_2_.1, bf16[128,3584]{1,0:T(8,128)(2,1)} %refs_3_.1), custom_call_target="tpu_custom_call" | custom-call | tf_op jit(solution)/shard_map/route/pallas_call | solution.py:98
  3.6 29.5 %all_to_all.10 = bf16[16,8,3584]{2,1,0:T(8,128)(2,1)S(1)} all-to-all(bf16[16,8,3584]{2,1,0:T(8,128)(2,1)S(1)} %bitcast.14), channel_id=1, replica_groups={{0,1,2,3,4,5,6,7,8,9,10,11,12,13,14,15},{26,27,24,25,30,31,28,29,18,19,..., dimensions={0} | all-to-all | bytes 1835008 | tf_op jit(solution)/shard_map/all_to_all | solution.py:464
  33.1 0.2 compact.1
  33.3 0.1 collective-permute-start.4
  33.4 0.5 collective-permute-start.6
  33.9 0.0 collective-permute-done.3.down_ref
  33.9 0.1 collective-permute-start
  34.0 1.0 %flip_down.1.down_ref = bf16[3584,512]{1,0:T(8,128)(2,1)S(1)} custom-call(bf16[64,2048]{1,0:T(8,128)(2,1)S(1)} %get-tuple-element.33.after_ref.mine_ref, bf16[512,3584]{1,0:T(8,128)(2,1)S(1)} %collective-permute-done.3.down_ref), custom_call_target="tpu_custom_call" | custom-call | tf_op jit(solution)/shard_map/flip_down/pallas_call | solution.py:185
  35.0 0.0 collective-permute-done.4.theirs_ref
  35.0 0.0 collective-permute-done.2.up_ref
  35.0 0.0 collective-permute-done.1.gate_ref
  35.0 0.8 %expert_begin.1 = (f32[128,512]{1,0:T(8,128)S(1)}, f32[128,512]{1,0:T(8,128)S(1)}, bf16[512,2048]{1,0:T(8,128)(2,1)S(1)}) custom-call(bf16[64,2048]{1,0:T(8,128)(2,1)S(1)} %get-tuple-element.33.after_ref.mine_ref, bf16[64,2048]{1,0:T(8,128)(2,1)S(1)} %collective-permute-done.4.theirs_ref, bf16[3584,512]{1,0:T(8,128)(2,1)S(1)} %collective-permute-done.1.gate_ref, ...), custom_call_target="tpu_custom_call" | custom-call | tf_op jit(solution)/shard_map/expert_begin/pallas_call | solution.py:221
  35.8 0.1 collective-permute-done.theirs_ref
  35.8 1.3 %expert_forward.1 = (bf16[64,3584]{1,0:T(8,128)(2,1)S(1)}, bf16[64,3584]{1,0:T(8,128)(2,1)S(1)}, bf16[128,512]{1,0:T(8,128)(2,1)S(1)}, f32[128,512]{1,0:T(8,128)...) custom-call(bf16[64,1536]{1,0:T(8,128)(2,1)S(1)} %get-tuple-element.32.mine_ref, ...), custom_call_target="tpu_custom_call" | custom-call | tf_op jit(solution)/shard_map/expert_forward/pallas_call | solution.py:252
  37.1 0.4 collective-permute-start.5
  37.6 0.0 collective-permute-done.6.theirs_ref.cot_mine
  37.6 1.4 %expert_backward.1 = (bf16[64,2048]{1,0:T(8,128)(2,1)S(1)}, bf16[64,2048]{1,0:T(8,128)(2,1)S(1)}, bf16[128,512]{1,0:T(8,128)(2,1)S(1)}, bf16[128,512]{1,0:T(8,128)(2,1)S(1)}, bf16[512,1536]{1,0:T(8,128)(2,1)S(1)}) custom-call(bf16[64,3584]{1,0:T(8,128)(2,1)S(1)} %get-tuple-element.39.mine_ref.cot_theirs, ...), custom_call_target="tpu_custom_call" | custom-call | tf_op jit(solution)/shard_map/expert_backward/pallas_call | solution.py:301
  38.9 0.2 collective-permute-start.7
  39.1 0.6 late_rows.1
  39.7 0.4 collective-permute-start.8
  40.2 0.4 collective-permute-done.7.refs_3_
  40.5 0.0 collective-permute-done.5.refs_1_.refs_2_
  40.5 0.2 add_early.1.refs_0_
  40.8 0.5 collective-permute-done.8.refs_4_
  41.2 0.9 %add_late.1 = bf16[128,3584]{1,0:T(8,128)(2,1)} custom-call(bf16[128,2048]{1,0:T(8,128)(2,1)S(1)} %add_early.1.refs_0_, bf16[64,3584]{1,0:T(8,128)(2,1)S(1)} %get-tuple-element.37.refs_0_.refs_1_, bf16[64,3584]{1,0:T(8,128)(2,1)S(1)} %collective-permute-done.5.refs_1_.refs_2_, bf16[64,1536]{1,0:T(8,128)(2,1)S(1)} %get-tuple-element.51.refs_3_, ...), custom_call_target="tpu_custom_call" | custom-call | tf_op jit(solution)/shard_map/add_late/pallas_call | solution.py:368
  42.2 5.4 %all-to-all-start.1 = ((bf16[16,8,3584]{2,1,0:T(8,128)(2,1)}), bf16[16,8,3584]{2,1,0:T(8,128)(2,1)S(1)}, u32[]{:S(2)}, u32[]{:S(2)}) async-start(bf16[16,8,3584]{2,1,0:T(8,128)(2,1)} %bitcast.15), calls=%async_computation.1 | async-start | bytes 1835008 | tf_op jit(solution)/shard_map/all_to_all | solution.py:464
  47.6 1.1 %selectors.1.select_ref = bf16[384,128]{1,0:T(8,128)(2,1)S(1)} custom-call(s32[8,128]{1,0:T(8,128)} %bitcast.17, f32[8,128]{1,0:T(8,128)} %bitcast.19), custom_call_target="tpu_custom_call" | custom-call | tf_op jit(solution)/shard_map/selectors/pallas_call | solution.py:137
  48.8 0.8 %collective-permute-start.10 = (bf16[128,512]{1,0:T(8,128)(2,1)S(1)}, bf16[128,512]{1,0:T(8,128)(2,1)S(1)}, u32[]{:S(2)}, u32[]{:S(2)}) collective-permute-start(bf16[128,512]{1,0:T(8,128)(2,1)S(1)} %get-tuple-element.47.gate_cot_ref), channel_id=1, source_target_pairs={{0,16},{16,0},{1,17},{17,1},{2,18},{18,2},{3,19},{19,3},{4,20},{20... | collective-permute-start | bytes 393224 | tf_op jit(solution)/shard_map/ppermute | solution.py:496
  49.6 0.1 collective-permute-start.11
  49.7 0.4 collective-permute-start.9
  50.1 0.4 collective-permute-done.10.gate_cot_ref
  50.6 0.4 collective-permute-done.11.up_cot_ref
  50.9 0.2 collective-permute-done.9.hid_ref
  51.1 6.3 %weight_grads.1 = (bf16[3584,512]{1,0:T(8,128)(2,1)}, bf16[3584,512]{1,0:T(8,128)(2,1)}, bf16[512,3584]{1,0:T(8,128)(2,1)}) custom-call(bf16[64,3584]{1,0:T(8,128)(2,1)S(1)} %pad_maximum_fusion.tok_mine, bf16[64,3584]{1,0:T(8,128)(2,1)S(1)} %pad_maximum_fusion.1.tok_theirs, bf16[64,3584]{1,0:T(8,128)(2,1)S(1)} %collective-permute-done.6.theirs_ref.cot_mine, ...), custom_call_target="tpu_custom_call" | custom-call | tf_op jit(solution)/shard_map/weight_grads/pallas_call | solution.py:396
  57.4 10.5 %all-to-all-done.1 = bf16[16,8,3584]{2,1,0:T(8,128)(2,1)S(1)} async-done(((bf16[16,8,3584]{2,1,0:T(8,128)(2,1)}), bf16[16,8,3584]{2,1,0:T(8,128)(2,1)S(1)}, u32[]{:S(2)}, u32[]{:S(2)}) %all-to-all-start.1) | async-done | bytes 917536 | tf_op jit(solution)/shard_map/all_to_all | solution.py:464
  67.9 1.7 %combine.1 = (bf16[128,3584]{1,0:T(8,128)(2,1)}, bf16[128,3584]{1,0:T(8,128)(2,1)}) custom-call(bf16[128,3584]{1,0:T(8,128)(2,1)S(1)} %bitcast.13, bf16[384,128]{1,0:T(8,128)(2,1)S(1)} %selectors.1.select_ref), custom_call_target="tpu_custom_call" | custom-call | tf_op jit(solution)/shard_map/combine/pallas_call | solution.py:436
  (2 shorter events, 0.1 us)
Async XLA Ops:
  0.6 33.3 %collective-permute-start.3 = (bf16[512,3584]{1,0:T(8,128)(2,1)}, bf16[512,3584]{1,0:T(8,128)(2,1)S(1)}, u32[]{:S(2)}, u32[]{:S(2)}) collective-permute-start(bf16[512,3584]{1,0:T(8,128)(2,1)} %bitcast.20), channel_id=1, source_target_pairs={{0,16},{16,0},{1,17},{17,1},{2,18},{18,2},{3,19},{19,3},{4,20},{20... | collective-permute-start | bytes 11010056 | tf_op jit(solution)/shard_map/ppermute | solution.py:474
  1.2 33.8 %collective-permute-start.2 = (bf16[3584,512]{1,0:T(8,128)(2,1)}, bf16[3584,512]{1,0:T(8,128)(2,1)S(1)}, u32[]{:S(2)}, u32[]{:S(2)}) collective-permute-start(bf16[3584,512]{1,0:T(8,128)(2,1)} %bitcast.21), channel_id=1, source_target_pairs={{0,16},{16,0},{1,17},{17,1},{2,18},{18,2},{3,19},{19,3},{4,20},{20... | collective-permute-start | bytes 11010056 | tf_op jit(solution)/shard_map/ppermute | solution.py:474
  1.2 33.8 %collective-permute-start.1 = (bf16[3584,512]{1,0:T(8,128)(2,1)}, bf16[3584,512]{1,0:T(8,128)(2,1)S(1)}, u32[]{:S(2)}, u32[]{:S(2)}) collective-permute-start(bf16[3584,512]{1,0:T(8,128)(2,1)} %bitcast.22), channel_id=1, source_target_pairs={{0,16},{16,0},{1,17},{17,1},{2,18},{18,2},{3,19},{19,3},{4,20},{20... | collective-permute-start | bytes 11010056 | tf_op jit(solution)/shard_map/ppermute | solution.py:474
  33.3 1.7 %collective-permute-start.4 = (bf16[64,2048]{1,0:T(8,128)(2,1)S(1)}, bf16[64,2048]{1,0:T(8,128)(2,1)S(1)}, u32[]{:S(2)}, u32[]{:S(2)}) collective-permute-start(bf16[64,2048]{1,0:T(8,128)(2,1)S(1)} %get-tuple-element.33.after_ref.mine_ref), channel_id=1, source_target_pairs={{0,16},{16,0},{1,17},{17,1},{2,18},{18,2},{3,19},{19,3},{4,20},{20... | collective-permute-start | bytes 786440 | tf_op jit(solution)/shard_map/ppermute | solution.py:471
  33.4 4.2 %collective-permute-start.6 = (bf16[64,3584]{1,0:T(8,128)(2,1)S(1)}, bf16[64,3584]{1,0:T(8,128)(2,1)S(1)}, u32[]{:S(2)}, u32[]{:S(2)}) collective-permute-start(bf16[64,3584]{1,0:T(8,128)(2,1)S(1)} %get-tuple-element.39.mine_ref.cot_theirs), channel_id=1, source_target_pairs={{0,16},{16,0},{1,17},{17,1},{2,18},{18,2},{3,19},{19,3},{4,20},{20... | collective-permute-start | bytes 1376264 | tf_op jit(solution)/shard_map/ppermute | solution.py:471
  33.9 2.0 %collective-permute-start = (bf16[64,1536]{1,0:T(8,128)(2,1)S(1)}, bf16[64,1536]{1,0:T(8,128)(2,1)S(1)}, u32[]{:S(2)}, u32[]{:S(2)}) collective-permute-start(bf16[64,1536]{1,0:T(8,128)(2,1)S(1)} %get-tuple-element.32.mine_ref), channel_id=1, source_target_pairs={{0,16},{16,0},{1,17},{17,1},{2,18},{18,2},{3,19},{19,3},{4,20},{20... | collective-permute-start | bytes 589832 | tf_op jit(solution)/shard_map/ppermute | solution.py:471
  37.1 3.4 %collective-permute-start.5 = (bf16[64,3584]{1,0:T(8,128)(2,1)S(1)}, bf16[64,3584]{1,0:T(8,128)(2,1)S(1)}, u32[]{:S(2)}, u32[]{:S(2)}) collective-permute-start(bf16[64,3584]{1,0:T(8,128)(2,1)S(1)} %get-tuple-element.38), channel_id=1, source_target_pairs={{0,16},{16,0},{1,17},{17,1},{2,18},{18,2},{3,19},{19,3},{4,20},{20... | collective-permute-start | bytes 1376264 | tf_op jit(solution)/shard_map/ppermute | solution.py:471
  38.9 1.6 %collective-permute-start.7 = (bf16[64,2048]{1,0:T(8,128)(2,1)S(1)}, bf16[64,2048]{1,0:T(8,128)(2,1)S(1)}, u32[]{:S(2)}, u32[]{:S(2)}) collective-permute-start(bf16[64,2048]{1,0:T(8,128)(2,1)S(1)} %get-tuple-element.46), channel_id=1, source_target_pairs={{0,16},{16,0},{1,17},{17,1},{2,18},{18,2},{3,19},{19,3},{4,20},{20... | collective-permute-start | bytes 786440 | tf_op jit(solution)/shard_map/ppermute | solution.py:471
  39.7 1.5 %collective-permute-start.8 = (bf16[64,1536]{1,0:T(8,128)(2,1)S(1)}, bf16[64,1536]{1,0:T(8,128)(2,1)S(1)}, u32[]{:S(2)}, u32[]{:S(2)}) collective-permute-start(bf16[64,1536]{1,0:T(8,128)(2,1)S(1)} %get-tuple-element.52), channel_id=1, source_target_pairs={{0,16},{16,0},{1,17},{17,1},{2,18},{18,2},{3,19},{19,3},{4,20},{20... | collective-permute-start | bytes 589832 | tf_op jit(solution)/shard_map/ppermute | solution.py:471
  42.2 25.7 %all-to-all-start.1 = ((bf16[16,8,3584]{2,1,0:T(8,128)(2,1)}), bf16[16,8,3584]{2,1,0:T(8,128)(2,1)S(1)}, u32[]{:S(2)}, u32[]{:S(2)}) async-start(bf16[16,8,3584]{2,1,0:T(8,128)(2,1)} %bitcast.15), calls=%async_computation.1 | async-start | bytes 1835008 | tf_op jit(solution)/shard_map/all_to_all | solution.py:464
  48.8 1.8 %collective-permute-start.10 = (bf16[128,512]{1,0:T(8,128)(2,1)S(1)}, bf16[128,512]{1,0:T(8,128)(2,1)S(1)}, u32[]{:S(2)}, u32[]{:S(2)}) collective-permute-start(bf16[128,512]{1,0:T(8,128)(2,1)S(1)} %get-tuple-element.47.gate_cot_ref), channel_id=1, source_target_pairs={{0,16},{16,0},{1,17},{17,1},{2,18},{18,2},{3,19},{19,3},{4,20},{20... | collective-permute-start | bytes 393224 | tf_op jit(solution)/shard_map/ppermute | solution.py:496
  49.6 1.3 %collective-permute-start.11 = (bf16[128,512]{1,0:T(8,128)(2,1)S(1)}, bf16[128,512]{1,0:T(8,128)(2,1)S(1)}, u32[]{:S(2)}, u32[]{:S(2)}) collective-permute-start(bf16[128,512]{1,0:T(8,128)(2,1)S(1)} %get-tuple-element.48.up_cot_ref), channel_id=1, source_target_pairs={{0,16},{16,0},{1,17},{17,1},{2,18},{18,2},{3,19},{19,3},{4,20},{20... | collective-permute-start | bytes 393224 | tf_op jit(solution)/shard_map/ppermute | solution.py:496
  49.7 1.5 %collective-permute-start.9 = (bf16[128,512]{1,0:T(8,128)(2,1)S(1)}, bf16[128,512]{1,0:T(8,128)(2,1)S(1)}, u32[]{:S(2)}, u32[]{:S(2)}) collective-permute-start(bf16[128,512]{1,0:T(8,128)(2,1)S(1)} %get-tuple-element.55), channel_id=1, source_target_pairs={{0,16},{16,0},{1,17},{17,1},{2,18},{18,2},{3,19},{19,3},{4,20},{20... | collective-permute-start | bytes 393224 | tf_op jit(solution)/shard_map/ppermute | solution.py:496
